TPU v7x, 32 devices: a whole 2x2x4 slice. The times are simulated.
32 devices in a mesh: groups: 2 (over x), batch: 8 (over z, y), tensor: 2 (over core).
Axes of the slice: x: 2, y: 2, z: 4, core: 2. Of those that a mesh axis runs over, the one named last changes fastest.
Arguments:
- tokens: bfloat16 [256, 5120], P(('groups', 'batch'), 'tensor'), parts along dimension 0, may hold values from -6 to 6
- gate_weight: bfloat16 [5120, 13824], P(None, ('batch', 'tensor')), may hold values from -0.078125 to 0.078125
- up_weight: bfloat16 [5120, 13824], P(None, ('batch', 'tensor')), may hold values from -0.078125 to 0.078125
- down_weight: bfloat16 [13824, 5120], P(('batch', 'tensor')), may hold values from -0.0546875 to 0.0546875
- adapter_in: bfloat16 [32, 64, 13824], P('groups', None, ('batch', 'tensor')), parts along dimension 0, may hold values from -0.0546875 to 0.0546875
- adapter_out: bfloat16 [32, 64, 5120], P('groups', None, ('batch', 'tensor')), parts along dimension 0, may hold values from -0.75 to 0.75
- cotangent: bfloat16 [256, 5120], P('groups', ('batch', 'tensor')), parts along dimension 0, may hold values from -6 to 6
- block_owner: int32 [4], P('groups'), parts along dimension 0, may hold values from 0 to 15
- block_length: int32 [4], P('groups'), parts along dimension 0, may hold values from 1 to 64
- placement: int32 [32], P('groups'), parts along dimension 0, may hold values from 0 to 15, each once
Outputs:
- mixed: bfloat16 [256, 5120], P('groups', ('batch', 'tensor')), parts along dimension 0
- grad_in: bfloat16 [32, 64, 13824], P(('groups', 'batch', 'tensor')), parts along dimension 0
- grad_out: bfloat16 [32, 64, 5120], P(('groups', 'batch', 'tensor')), parts along dimension 0
There are 2 independent parts, one for each index of `groups`. A program takes and returns all parts, laid end to end along the dimension named above; an argument that names none is the same for every part. Nothing has to cross between parts.
Inputs may be any that keep to these rules, and one draw needn't show every extreme that they name: `block_owner`: owner of each block of 64 tokens; some owners have no block. `block_length`: padded tokens lie at the end of each block. `placement`: a permutation; slot j belongs to the j-th device of batch+tensor.
All inputs are finite; a program needn't handle non-finite values.
Results may differ from a plain program's by a relative error of at most 0.0085.
Values may be sent and summed in bfloat16 or wider, within the bound.
No kernel may reach another device: no remote copies, remote signals or barrier semaphores. Data moves between devices by JAX's collectives and lax.ppermute only.
A program may use at most 128 MiB of HBM per device.

v0:
```python
import jax
import jax.numpy as jnp
from jax import lax
from jax.sharding import PartitionSpec as P

lowrank_adapter_scale = 2.0


def on_device(
    tokens,
    gate_weight,
    up_weight,
    down_weight,
    adapter_in,
    adapter_out,
    cotangent,
    block_owner,
    block_length,
    placement,
):
    highest = lax.Precision.HIGHEST
    hidden_width = gate_weight.shape[1]
    whole_rows = lax.all_gather(tokens, "tensor", axis=1, tiled=True)
    rows_piece = lax.all_gather(whole_rows, "batch", axis=0, tiled=True)
    both_values = jnp.concatenate(
        [
            jnp.dot(rows_piece, gate_weight, preferred_element_type=jnp.float32),
            jnp.dot(rows_piece, up_weight, preferred_element_type=jnp.float32),
        ],
        axis=1,
    )
    gate_value = both_values[:, :hidden_width]
    up_value = both_values[:, hidden_width:]
    hidden = (jax.nn.silu(gate_value) * up_value).astype(jnp.bfloat16)
    base_term = jnp.dot(hidden, down_weight, preferred_element_type=jnp.float32)
    token_total_count = hidden.shape[0]
    batch_count = lax.axis_size("batch")
    tensor_count = lax.axis_size("tensor")
    feature_count = base_term.shape[1]
    column_width = feature_count // (batch_count * tensor_count)
    chip_sum = lax.psum(base_term.astype(jnp.bfloat16), "tensor")
    batch_part = lax.psum_scatter(chip_sum, "batch", scatter_dimension=1, tiled=True).astype(
        jnp.float32
    )
    frozen_base_total = lax.dynamic_slice_in_dim(
        batch_part, lax.axis_index("tensor") * column_width, column_width, 1
    )
    block_count = block_owner.shape[0]
    block_size = token_total_count // block_count
    owner_count = adapter_in.shape[0]
    in_blocks = adapter_in[block_owner]
    out_blocks = adapter_out[block_owner]
    hidden_blocks = hidden.reshape(block_count, block_size, hidden_width)
    position = lax.broadcasted_iota(jnp.int32, (block_count, block_size), 1)
    live_mask = (position < block_length[:, None]).astype(jnp.bfloat16)
    masked = cotangent.reshape(block_count, block_size, cotangent.shape[1]) * live_mask[:, :, None]
    low_part = jnp.einsum(
        "bsf,brf->bsr", hidden_blocks, in_blocks, preferred_element_type=jnp.float32
    )
    back_part = jnp.einsum("bsd,brd->bsr", masked, out_blocks, preferred_element_type=jnp.float32)
    low_sum, back_sum = lax.psum((low_part, back_part), ("batch", "tensor"))
    low = low_sum.astype(jnp.bfloat16)
    back = back_sum.astype(jnp.bfloat16)
    adapter_contribution = jnp.einsum(
        "bsr,brd->bsd", low, out_blocks, preferred_element_type=jnp.float32
    )
    mixed = (
        frozen_base_total
        + lowrank_adapter_scale * adapter_contribution.reshape(token_total_count, -1)
    ).astype(jnp.bfloat16)
    owner_indicator = (
        lax.broadcasted_iota(jnp.int32, (owner_count, block_count), 0) == block_owner[None, :]
    ).astype(jnp.float32)
    owner_token_counts = jnp.dot(
        owner_indicator, block_length.astype(jnp.float32), precision=highest
    )
    coefficient = (
        owner_indicator * (lowrank_adapter_scale / jnp.maximum(owner_token_counts, 1.0))[:, None]
    )
    out_terms = jnp.einsum("bsr,bsd->brd", low, masked, preferred_element_type=jnp.float32)
    in_terms = jnp.einsum("bsr,bsf->brf", back, hidden_blocks, preferred_element_type=jnp.float32)
    owner_out = jnp.einsum("ob,brd->ord", coefficient, out_terms, precision=highest)
    owner_in = jnp.einsum("ob,brf->orf", coefficient, in_terms, precision=highest)
    slot_in = owner_in[placement].astype(jnp.bfloat16)
    slot_out = owner_out[placement].astype(jnp.bfloat16)
    grad_in, grad_out = (
        lax.all_to_all(slot_in, ("batch", "tensor"), split_axis=0, concat_axis=2, tiled=True),
        lax.all_to_all(slot_out, ("batch", "tensor"), split_axis=0, concat_axis=2, tiled=True),
    )
    return (mixed, grad_in, grad_out)


def solution(mesh):
    placed = (
        P(("groups", "batch"), "tensor"),
        P(None, ("batch", "tensor")),
        P(None, ("batch", "tensor")),
        P(("batch", "tensor"), None),
        P("groups", None, ("batch", "tensor")),
        P("groups", None, ("batch", "tensor")),
        P("groups", ("batch", "tensor")),
        P("groups"),
        P("groups"),
        P("groups"),
    )
    return jax.shard_map(
        on_device,
        mesh=mesh,
        in_specs=placed,
        out_specs=(
            P("groups", ("batch", "tensor")),
            P(("groups", "batch", "tensor"), None, None),
            P(("groups", "batch", "tensor"), None, None),
        ),
        check_vma=False,
    )
```

profile of v0, /device:TPU:2, one launch (start us, length us, event | category | flops | bytes accessed | tf_op | source)
XLA Modules:
  0.0 280.1 jit_solution(4538097202153336883)
XLA Ops:
  7.2 0.0 copy-start
  7.2 0.0 all-gather.2.cloned.1.call-start
  7.2 3.7 %all_gather.6 = bf16[16,5120]{1,0:T(8,128)(2,1)} all-gather(bf16[16,2560]{1,0:T(8,128)(2,1)} %param.10), channel_id=1, replica_groups=mesh['groups'=2,'batch'=8,'tensor'=2] {'tensor'}, dimensions={1}, use_global_device_ids=true | all-gather | bytes 245760 | tf_op jit(solution)/shard_map/all_gather | solution.py:23
  10.9 0.0 all-gather.2.cloned.1.call-update
  11.0 0.7 compare_select_fusion.1
  11.6 0.0 copy-done
  11.6 0.6 gather_fusion
  12.2 1.7 gather_fusion.1
  13.9 1.0 copy.32
  14.9 0.7 compare_select_fusion
  15.6 0.7 compare_convert_fusion
  16.3 0.9 fusion.2
  17.2 0.2 fusion.10
  17.4 36.7 %all-gather.2.cloned.1.call-done = bf16[128,5120]{1,0:T(8,128)(2,1)} async-done(((bf16[16,5120]{1,0:T(8,128)(2,1)}), bf16[128,5120]{1,0:T(8,128)(2,1)}) %all-gather.2.cloned.1.call-update) | async-done | bytes 1310736 | tf_op jit(solution)/shard_map/all_gather | solution.py:24
  54.1 0.0 copy-start.1
  54.1 6.5 %fusion.31 = f32[128,864]{0,1:T(8,128)S(1)} fusion(bf16[128,5120]{1,0:T(8,128)(2,1)} %all-gather.2.cloned.1.call-done, bf16[5120,864]{0,1:T(8,128)(2,1)} %param.11), kind=kOutput, calls=%fused_computation.47 | convolution fusion | flops 1132462080 | bytes 10600448 | tf_op jit(solution)/shard_map/dot_general | solution.py:27
  60.6 0.0 copy-done.1
  60.6 0.0 copy-start.4
  60.6 6.0 %fusion = bf16[128,864]{0,1:T(8,128)(2,1)S(1)} fusion(bf16[128,5120]{1,0:T(8,128)(2,1)S(1)} %copy-done.1, bf16[5120,864]{0,1:T(8,128)(2,1)} %param.12, f32[128,864]{0,1:T(8,128)S(1)} %fusion.31), kind=kOutput, calls=%fused_computation.6 | convolution fusion | flops 1133125632 | bytes 10821632 | tf_op jit(solution)/shard_map/dot_general | solution.py:28
  66.6 0.2 copy.31
  66.8 0.2 fusion.32
  67.0 59.0 %all-reduce = (bf16[2,64,64]{2,1,0:T(8,128)(2,1)S(1)}, bf16[2,64,64]{2,1,0:T(8,128)(2,1)S(1)}) all-reduce(f32[2,64,64]{2,1,0:T(8,128)S(1)} %fusion.32, f32[2,64,64]{2,1,0:T(8,128)S(1)} %fusion.10), channel_id=1, replica_groups=mesh['groups'=2,'batch'=8,'tensor'=2] {'batch','tensor'}, use_global_device_ids=true, to_apply=%region_2.3 | all-reduce | flops 16384 | bytes 98304 | tf_op jit(solution)/shard_map/psum | solution.py:61
  126.0 0.2 fusion.8
  126.2 0.0 copy-done.4
  126.2 1.6 fusion.6
  127.8 0.2 copy.39
  128.0 1.5 gather_fusion.3
  129.5 3.6 %all-to-all-start.1 = ((bf16[16,64,320]{2,1,0:T(8,128)(2,1)}), bf16[16,64,320]{2,1,0:T(8,128)(2,1)S(1)}, u32[]{:S(2)}, u32[]{:S(2)}) async-start(bf16[16,64,320]{2,1,0:T(8,128)(2,1)} %gather_fusion.3), calls=%async_computation.1 | async-start | bytes 1572864 | tf_op jit(solution)/shard_map/all_to_all | solution.py:88
  133.2 0.3 fusion.33
  133.4 3.4 %fusion.3 = bf16[16,64,864]{2,0,1:T(8,128)(2,1)S(1)} fusion(f32[2,64,864]{2,1,0:T(8,128)S(1)} %fusion.33, f32[16]{0:T(128)S(1)} %fusion.2, s32[2]{0:T(128)S(1)} %copy-done.4), kind=kOutput, calls=%fused_computation.11 | convolution fusion | flops 21233728 | bytes 2211912 | tf_op jit(solution)/shard_map/ob,brf->orf/dot_general | solution.py:83
  136.8 1.7 copy.35
  138.5 3.5 %gather_fusion.2 = bf16[16,64,864]{2,1,0:T(8,128)(2,1)} fusion(bf16[16,64,864]{2,1,0:T(8,128)(2,1)} %copy.35, s32[1024]{0:T(1024)S(1)} %pad_clamp_fusion), kind=kCustom, calls=%fused_computation.2 | custom fusion | bytes 3539008 | tf_op jit(solution)/shard_map/gather | solution.py:84
  142.0 9.8 %all-to-all-done.1 = bf16[16,64,320]{2,1,0:T(8,128)(2,1)S(1)} async-done(((bf16[16,64,320]{2,1,0:T(8,128)(2,1)}), bf16[16,64,320]{2,1,0:T(8,128)(2,1)S(1)}, u32[]{:S(2)}, u32[]{:S(2)}) %all-to-all-start.1) | async-done | bytes 655392 | tf_op jit(solution)/shard_map/all_to_all | solution.py:88
  151.8 0.0 copy-start.2
  151.8 0.9 copy-done.2
  152.7 5.5 %all-to-all-start = ((bf16[16,64,864]{2,1,0:T(8,128)(2,1)}), bf16[16,64,864]{2,1,0:T(8,128)(2,1)}, u32[]{:S(2)}, u32[]{:S(2)}) async-start(bf16[16,64,864]{2,1,0:T(8,128)(2,1)} %gather_fusion.2), calls=%async_computation | async-start | bytes 3670016 | tf_op jit(solution)/shard_map/all_to_all | solution.py:87
  158.2 0.2 reduce-scatter.4.cloned.1.call-start
  158.4 5.1 %convolution_convert_fusion = bf16[128,5120]{1,0:T(8,128)(2,1)S(1)} fusion(bf16[128,864]{0,1:T(8,128)(2,1)S(1)} %fusion, bf16[864,5120]{1,0:T(8,128)(2,1)} %param.13), kind=kOutput, calls=%fused_computation.4 | convolution fusion | flops 1133117440 | bytes 10379264 | tf_op jit(solution)/shard_map/dot_general | solution.py:35
  163.5 1.4 copy.44
  164.9 0.0 copy-start.3
  164.9 0.0 reduce-scatter.4.cloned.1.call-update
  164.9 0.0 all-reduce.3.cloned.1.call-start
  165.0 78.8 %reduce-scatter.4.cloned.1.call-done = bf16[640,128]{1,0:T(8,128)(2,1)} async-done(((bf16[5120,128]{1,0:T(8,128)(2,1)}), bf16[640,128]{1,0:T(8,128)(2,1)}) %reduce-scatter.4.cloned.1.call-update) | async-done | bytes 163856
  243.8 1.7 copy.45
  245.5 0.0 all-reduce.3.cloned.1.call-update
  245.5 0.8 convolution_multiply_fusion.1
  246.4 0.0 copy-done.3
  246.4 0.5 copy.40
  246.8 1.5 all_to_all.33
  248.3 15.1 %all-reduce.3.cloned.1.call-done = bf16[128,640]{1,0:T(8,128)(2,1)} async-done(((bf16[128,640]{1,0:T(8,128)(2,1)}), bf16[128,640]{1,0:T(8,128)(2,1)}) %all-reduce.3.cloned.1.call-update) | async-done | bytes 163856 | tf_op jit(solution)/shard_map/psum | solution.py:41
  263.4 1.1 fusion.5
  264.5 0.7 copy.41
  265.3 0.0 all-to-all-done
  265.3 3.8 %copy.36 = bf16[1,64,16,864]{3,2,1,0:T(8,128)(2,1)} copy(bf16[1,64,16,864]{3,1,2,0:T(8,128)(2,1)} %bitcast.7) | data formatting | bytes 3538944 | tf_op jit(solution)/shard_map/all_to_all | solution.py:87
  269.0 4.5 %all_to_all.29 = bf16[1,64,13824]{2,1,0:T(8,128)(2,1)} reshape(bf16[1,64,16,864]{3,2,1,0:T(8,128)(2,1)} %copy.36) | data formatting | bytes 3538944 | tf_op jit(solution)/shard_map/all_to_all | solution.py:87
  (2 shorter events, 0.0 us)
Async XLA Ops:
  7.2 4.5 %copy-start = (bf16[16,64,864]{2,1,0:T(8,128)(2,1)S(1)}, bf16[16,64,864]{2,1,0:T(8,128)(2,1)}, u32[]{:S(2)}) copy-start(bf16[16,64,864]{2,1,0:T(8,128)(2,1)} %param.14) | copy-start | bytes 5308420
  7.2 47.0 %all-gather.2.cloned.1.call-start = ((), (), s32[]{:S(2)}) async-start(), calls=%async_computation.3 | async-start | bytes 1474560 | tf_op jit(solution)/shard_map/all_gather | solution.py:24
  54.1 6.5 %copy-start.1 = (bf16[128,5120]{1,0:T(8,128)(2,1)S(1)}, bf16[128,5120]{1,0:T(8,128)(2,1)}, u32[]{:S(2)}) copy-start(bf16[128,5120]{1,0:T(8,128)(2,1)} %all-gather.2.cloned.1.call-done) | copy-start | bytes 3932164
  60.6 65.6 %copy-start.4 = (s32[2]{0:T(128)S(1)}, s32[2]{0:T(128)}, u32[]{:S(2)}) copy-start(s32[2]{0:T(128)} %param.17) | copy-start | bytes 28
  129.5 22.3 %all-to-all-start.1 = ((bf16[16,64,320]{2,1,0:T(8,128)(2,1)}), bf16[16,64,320]{2,1,0:T(8,128)(2,1)S(1)}, u32[]{:S(2)}, u32[]{:S(2)}) async-start(bf16[16,64,320]{2,1,0:T(8,128)(2,1)} %gather_fusion.3), calls=%async_computation.1 | async-start | bytes 1572864 | tf_op jit(solution)/shard_map/all_to_all | solution.py:88
  151.8 0.9 copy-start.2
  152.7 112.6 %all-to-all-start = ((bf16[16,64,864]{2,1,0:T(8,128)(2,1)}), bf16[16,64,864]{2,1,0:T(8,128)(2,1)}, u32[]{:S(2)}, u32[]{:S(2)}) async-start(bf16[16,64,864]{2,1,0:T(8,128)(2,1)} %gather_fusion.2), calls=%async_computation | async-start | bytes 3670016 | tf_op jit(solution)/shard_map/all_to_all | solution.py:87
  158.2 85.6 %reduce-scatter.4.cloned.1.call-start = ((), (), s32[]{:S(2)}) async-start(), calls=%async_computation.5 | async-start | bytes 1474560
  164.9 81.5 %copy-start.3 = (bf16[16,64,320]{2,1,0:T(8,128)(2,1)S(1)}, bf16[16,64,320]{2,1,0:T(8,128)(2,1)}, u32[]{:S(2)}) copy-start(bf16[16,64,320]{2,1,0:T(8,128)(2,1)} %copy-done.2) | copy-start | bytes 1966084
  164.9 98.5 %all-reduce.3.cloned.1.call-start = ((), (), s32[]{:S(2)}) async-start(), calls=%async_computation.4 | async-start | bytes 327680 | tf_op jit(solution)/shard_map/psum | solution.py:41
Sparse Core Ops, SparseCore 0:
  11.1 43.0 all-gather.1
  165.1 78.6 reduce-scatter.3
  246.1 17.2 all-reduce.2
where the time goes:
time: 282 us; the launch traced here: 280 us
  waiting for transfers between devices  140 us (50%)
  blocking collectives  62.7 us (22%)
  local copies, waits for them, and re-layouts  25.4 us (9%)
  matrix products  25.1 us (9%)
  between operations  13.9 us (5%)
  starting transfers between devices  9.39 us (3%)
  other arithmetic  3.16 us (1%)
    unnamed x4, waiting for transfers between devices  78.8 us
    psum x1, blocking collectives, on_device(): low_sum, back_sum = lax.psum((low_part, back_part), ('batch', 'tensor'))  59 us
    all_gather x1, waiting for transfers between devices, on_device(): rows_piece = lax.all_gather(whole_rows, 'batch', axis=0, tiled=True)  36.7 us
    psum x1, waiting for transfers between devices, on_device(): chip_sum = lax.psum(base_term.astype(jnp.bfloat16), 'tensor')  15.1 us
    all_to_all x1, waiting for transfers between devices, on_device(): lax.all_to_all(slot_out, ('batch', 'tensor'), split_axis=0, concat_axis=2...  9.83 us
    all_to_all x2, local copies, waits for them, and re-layouts, on_device(): lax.all_to_all(slot_in, ('batch', 'tensor'), split_axis=0, concat_axis=2,...  8.27 us
    dot_general x1, matrix products, on_device(): jnp.dot(rows_piece, gate_weight, preferred_element_type=jnp.float32)  6.45 us
    dot_general x1, matrix products, on_device(): jnp.dot(rows_piece, up_weight, preferred_element_type=jnp.float32)  5.97 us
  transfers between devices with their start and end apart: 5, of which 4 were waited for; matrix products, arithmetic and copies ran while one was open for 10% of the time, Pallas kernels for 0%

commit v1 on v0

v1 whole, which is shorter than its diff:
```python
import jax
import jax.numpy as jnp
from jax import lax
from jax.sharding import PartitionSpec as P

lowrank_adapter_scale = 2.0


def partner_shifts(count):
    return [[(i, i ^ k) for i in range(count)] for k in range(1, count)]


def gather_pieces(piece, axis):
    count = lax.axis_size(axis)
    if count & (count - 1) or count > 8:
        return lax.all_gather(piece, axis)
    me = lax.axis_index(axis)
    whole = jnp.zeros((count,) + piece.shape, piece.dtype)
    whole = lax.dynamic_update_index_in_dim(whole, piece, me, 0)
    for k, pairs in enumerate(partner_shifts(count), 1):
        arrived = lax.ppermute(piece, axis, pairs)
        whole = lax.dynamic_update_index_in_dim(whole, arrived, me ^ k, 0)
    return whole


def exchange_sum(pieces, axis):
    count = lax.axis_size(axis)
    if count & (count - 1) or count > 8:
        arrived = lax.all_to_all(pieces, axis, split_axis=0, concat_axis=0, tiled=True)
        return arrived.astype(jnp.float32).sum(0)
    me = lax.axis_index(axis)
    total = lax.dynamic_index_in_dim(pieces, me, 0, keepdims=False).astype(jnp.float32)
    for k, pairs in enumerate(partner_shifts(count), 1):
        leaving = lax.dynamic_index_in_dim(pieces, me ^ k, 0, keepdims=False)
        total = total + lax.ppermute(leaving, axis, pairs).astype(jnp.float32)
    return total


def pair_gather(piece):
    count = lax.axis_size("tensor")
    if count != 2:
        return lax.all_gather(piece, "tensor")
    other = lax.ppermute(piece, "tensor", [(0, 1), (1, 0)])
    mine_first = lax.axis_index("tensor") == 0
    return jnp.stack([jnp.where(mine_first, piece, other), jnp.where(mine_first, other, piece)])


def on_device(
    tokens,
    gate_weight,
    up_weight,
    down_weight,
    adapter_in,
    adapter_out,
    cotangent,
    block_owner,
    block_length,
    placement,
):
    f32, bf16 = jnp.float32, jnp.bfloat16
    batch_count, tensor_count = lax.axis_size("batch"), lax.axis_size("tensor")
    core = lax.axis_index("tensor")
    width = gate_weight.shape[1]
    model_width = gate_weight.shape[0]
    columns = cotangent.shape[1]
    token_count = cotangent.shape[0]
    block_count = block_owner.shape[0]
    block_size = token_count // block_count
    rank = adapter_in.shape[1]

    token_block = lax.broadcasted_iota(jnp.int32, (block_count, block_size), 0).reshape(-1)
    position = lax.broadcasted_iota(jnp.int32, (block_count, block_size), 1).reshape(-1)
    token_owner = jnp.repeat(block_owner, block_size)
    live = position < jnp.repeat(block_length, block_size)
    own_block = lax.broadcasted_iota(jnp.int32, (block_count, 1, 1), 0) == token_block

    def in_rank_space(matrices, features):
        every = jnp.dot(
            matrices.reshape(block_count * rank, -1), features, preferred_element_type=f32
        )
        return jnp.where(own_block, every.reshape(block_count, rank, token_count), 0.0).sum(0)

    in_blocks = adapter_in[block_owner]
    out_blocks = adapter_out[block_owner]
    cot_t = cotangent.T
    half = gather_pieces(tokens, "batch").reshape(token_count, -1)
    halves = pair_gather(half)
    rows = jnp.concatenate([halves[c] for c in range(tensor_count)], axis=1)

    back_part = jnp.where(live, in_rank_space(out_blocks, cot_t), 0.0).astype(bf16)
    cot_all = gather_pieces(cot_t, "batch")

    def weights_first(weight, values):
        return lax.dot_general(
            weight, values, (((0,), (1,)), ((), ())), preferred_element_type=f32
        )

    gate_value = weights_first(gate_weight, rows)
    up_value = weights_first(up_weight, rows)
    hidden = (jax.nn.silu(gate_value) * up_value).astype(bf16)
    hidden_all = gather_pieces(hidden, "batch")

    low_part = in_rank_space(in_blocks, hidden)
    base_part = lax.dot_general(
        down_weight, hidden, (((0,), (0,)), ((), ())), preferred_element_type=f32
    ).astype(bf16)
    base_part = base_part.reshape(batch_count, tensor_count, columns, token_count)
    ranked = jnp.concatenate([low_part.astype(bf16), back_part], axis=0)
    if tensor_count == 2:
        leaving = lax.dynamic_index_in_dim(base_part, 1 - core, 1, keepdims=False)
        kept = lax.dynamic_index_in_dim(base_part, core, 1, keepdims=False)
        arrived, ranked_other = lax.ppermute((leaving, ranked), "tensor", [(0, 1), (1, 0)])
        chip_base = (kept.astype(f32) + arrived.astype(f32)).astype(bf16)
        chip_ranked = (ranked.astype(f32) + ranked_other.astype(f32)).astype(bf16)
    else:
        chip_base = lax.psum_scatter(base_part, "tensor", scatter_dimension=1)
        chip_ranked = lax.psum(ranked, "tensor")
    leaving = jnp.concatenate(
        [chip_base, jnp.broadcast_to(chip_ranked, (batch_count,) + chip_ranked.shape)], axis=1
    )
    total = exchange_sum(leaving, "batch")
    base_sum = total[:columns]
    low = total[columns : columns + rank].astype(bf16)
    back = total[columns + rank :].astype(bf16)

    spread = jnp.where(own_block, low[None], jnp.zeros((), bf16)).reshape(-1, token_count)
    contribution = lax.dot_general(
        out_blocks.reshape(block_count * rank, columns),
        spread,
        (((0,), (0,)), ((), ())),
        preferred_element_type=f32,
    )
    mixed = (base_sum + lowrank_adapter_scale * contribution).astype(bf16).T

    slot = lax.axis_index(("batch", "tensor"))
    owner = placement[slot]
    count = jnp.where(block_owner == owner, block_length, 0).sum().astype(f32)
    coefficient = lowrank_adapter_scale / jnp.maximum(count, 1.0)
    chosen = token_owner == owner
    low_chosen = jnp.where(chosen & live, low, jnp.zeros((), bf16))
    back_chosen = jnp.where(chosen, back, jnp.zeros((), bf16))

    def slot_grad(ranked_values, pieces):
        both = pair_gather(pieces)
        features = jnp.swapaxes(both, 0, 1).reshape(-1, token_count)
        grad = lax.dot_general(
            ranked_values, features, (((1,), (1,)), ((), ())), preferred_element_type=f32
        )
        return (coefficient * grad).astype(bf16)[None]

    return mixed, slot_grad(back_chosen, hidden_all), slot_grad(low_chosen, cot_all)


def solution(mesh):
    placed = (
        P(("groups", "batch"), "tensor"),
        P(None, ("batch", "tensor")),
        P(None, ("batch", "tensor")),
        P(("batch", "tensor"), None),
        P("groups", None, ("batch", "tensor")),
        P("groups", None, ("batch", "tensor")),
        P("groups", ("batch", "tensor")),
        P("groups"),
        P("groups"),
        P("groups"),
    )
    return jax.shard_map(
        on_device,
        mesh=mesh,
        in_specs=placed,
        out_specs=(
            P("groups", ("batch", "tensor")),
            P(("groups", "batch", "tensor"), None, None),
            P(("groups", "batch", "tensor"), None, None),
        ),
        check_vma=False,
    )
```

time: 282 us -> 136 us (0.48)
  waiting for transfers between devices: 140 us -> 30.8 us
  blocking collectives: 62.7 us -> 0 us
  starting transfers between devices: 9.39 us -> 56.1 us
  between operations: 13.9 us -> 1.8 us
  matrix products: 25.1 us -> 16 us
  other arithmetic: 3.16 us -> 6.76 us
    unnamed x4 -> x0, waiting for transfers between devices: 78.8 us -> none
    psum x1 -> x0, blocking collectives: 59 us -> none  [on_device(): low_sum, back_sum = lax.psum((low_part, back_part), ('batch', 'tensor'))]
    ppermute x0 -> x33, starting transfers between devices: none -> 56.1 us  [the longest x21 33.2 us: gather_pieces(): arrived = lax.ppermute(piece, axis, pairs)]
    all_gather x1 -> x0, waiting for transfers between devices: 36.7 us -> none  [on_device(): rows_piece = lax.all_gather(whole_rows, 'batch', axis=0, tiled=True)]
    ppermute x0 -> x33, waiting for transfers between devices: none -> 30.8 us  [the longest x21 21.7 us: gather_pieces(): arrived = lax.ppermute(piece, axis, pairs)]
    psum x1 -> x0, waiting for transfers between devices: 15.1 us -> none  [on_device(): chip_sum = lax.psum(base_term.astype(jnp.bfloat16), 'tensor')]
    dynamic_update_slice x0 -> x23, local copies, waits for them, and re-layouts: none -> 14.7 us  [the longest x21 13.2 us: gather_pieces(): whole = lax.dynamic_update_index_in_dim(whole, arrived, me ^ k, 0)]
    all_to_all x4 -> x0, local copies, waits for them, and re-layouts: 10.2 us -> none  [the longest x2 8.27 us: on_device(): lax.all_to_all(slot_in, ('batch', 'tensor'), split_axis=0, concat_axis=2,...]
  transfers between devices with their start and end apart: 5 -> 33, of which waited for: 4 -> 9; matrix products, arithmetic and copies ran while one was open for 10% -> 31% of each run, Pallas kernels for 0% -> 0%
where the time goes in v1:
time: 136 us; the launch traced here: 135 us
  starting transfers between devices  56.1 us (41%)
  waiting for transfers between devices  30.8 us (23%)
  local copies, waits for them, and re-layouts  23.9 us (18%)
  matrix products  16 us (12%)
  other arithmetic  6.76 us (5%)
  between operations  1.8 us (1%)
    ppermute x21, starting transfers between devices, gather_pieces(): arrived = lax.ppermute(piece, axis, pairs)  33.2 us
    ppermute x7, starting transfers between devices, exchange_sum(): total = total + lax.ppermute(leaving, axis, pairs).astype(jnp.float32)  22.3 us
    ppermute x21, waiting for transfers between devices, gather_pieces(): arrived = lax.ppermute(piece, axis, pairs)  21.7 us
    dynamic_update_slice x21, local copies, waits for them, and re-layouts, gather_pieces(): whole = lax.dynamic_update_index_in_dim(whole, arrived, me ^ k, 0)  13.2 us
    dot_general x2, matrix products, weights_first(): lax.dot_general(weight, values, (((0,), (1,)), ((), ())), preferred_eleme...  9.23 us
    ppermute x7, waiting for transfers between devices, exchange_sum(): total = total + lax.ppermute(leaving, axis, pairs).astype(jnp.float32)  9.09 us
    dot_general x2, matrix products, slot_grad(): lax.dot_general(ranked_values, features, (((1,), (1,)), ((), ())), prefer...  3.99 us
    another operation x4, other arithmetic, pair_gather(): jnp.stack([jnp.where(mine_first, piece, other), jnp.where(mine_first, oth...  3.53 us
  transfers between devices with their start and end apart: 33, of which 9 were waited for; matrix products, arithmetic and copies ran while one was open for 31% of the time, Pallas kernels for 0%

profile of v1, /device:TPU:2, one launch (start us, length us, event | category | flops | bytes accessed | tf_op | source)
XLA Modules:
  0.0 135.3 jit_solution(574935026099911024)
XLA Ops:
  0.7 1.6 %collective-permute-start = (bf16[16,2560]{1,0:T(8,128)(2,1)}, bf16[16,2560]{1,0:T(8,128)(2,1)S(1)}, u32[]{:S(2)}, u32[]{:S(2)}) collective-permute-start(bf16[16,2560]{1,0:T(8,128)(2,1)} %param.10), channel_id=1, source_target_pairs={{0,2},{2,0},{4,6},{6,4},{8,10},{10,8},{12,14},{14,12},{1,3},{3,1},... | collective-permute-start | bytes 245768 | tf_op jit(solution)/shard_map/ppermute | solution.py:21
  2.3 1.6 %collective-permute-start.1 = (bf16[16,2560]{1,0:T(8,128)(2,1)}, bf16[16,2560]{1,0:T(8,128)(2,1)S(1)}, u32[]{:S(2)}, u32[]{:S(2)}) collective-permute-start(bf16[16,2560]{1,0:T(8,128)(2,1)} %param.10), channel_id=1, source_target_pairs={{0,4},{2,6},{4,0},{6,2},{8,12},{10,14},{12,8},{14,10},{1,5},{3,7},... | collective-permute-start | bytes 245768 | tf_op jit(solution)/shard_map/ppermute | solution.py:21
  4.2 2.6 %collective-permute-start.3 = (bf16[16,2560]{1,0:T(8,128)(2,1)}, bf16[16,2560]{1,0:T(8,128)(2,1)S(1)}, u32[]{:S(2)}, u32[]{:S(2)}) collective-permute-start(bf16[16,2560]{1,0:T(8,128)(2,1)} %param.10), channel_id=1, source_target_pairs={{0,8},{2,10},{4,12},{6,14},{8,0},{10,2},{12,4},{14,6},{1,9},{3,11}... | collective-permute-start | bytes 245768 | tf_op jit(solution)/shard_map/ppermute | solution.py:21
  6.8 1.3 collective-permute-start.4
  8.1 0.7 iota_compare_fusion
  8.8 1.2 dynamic_slice.45
  10.1 2.0 %select_reduce_fusion = (s32[]{:T(128)}, pred[2]{0:T(512)(128)(4,1)S(1)}, s32[2]{0:T(128)S(1)}) fusion(s32[2]{0:T(128)} %param.18, s32[2]{0:T(128)} %param.17, s32[]{:T(128)} %bitcast.27), kind=kLoop, calls=%fused_computation.115 | loop fusion | flops 11 | bytes 34 | tf_op jit(solution)/shard_map/reduce_sum | solution.py:137
  12.2 1.7 %gather_fusion.1 = bf16[2,64,320]{2,1,0:T(8,128)(2,1)S(1)} fusion(bf16[16,64,320]{2,1,0:T(8,128)(2,1)} %param.15, s32[1024]{0:T(1024)S(1)} %pad_clamp_fusion), kind=kCustom, calls=%fused_computation.1 | custom fusion | bytes 163848 | tf_op jit(solution)/shard_map/gather | solution.py:84
  14.0 0.9 bitcast_dynamic-update-slice_fusion.23
  14.9 0.9 broadcast_in_dim.196
  15.8 0.6 bitcast_dynamic-update-slice_fusion.8
  16.7 0.6 gather_fusion
  18.1 3.7 %collective-permute-start.5 = (bf16[16,2560]{1,0:T(8,128)(2,1)S(1)}, bf16[16,2560]{1,0:T(8,128)(2,1)S(1)}, u32[]{:S(2)}, u32[]{:S(2)}) collective-permute-start(bf16[16,2560]{1,0:T(8,128)(2,1)S(1)} %copy-done.3), channel_id=1, source_target_pairs={{0,12},{2,14},{4,8},{6,10},{8,4},{10,6},{12,0},{14,2},{1,13},{3,15... | collective-permute-start | bytes 245768 | tf_op jit(solution)/shard_map/ppermute | solution.py:21
  22.1 1.6 %collective-permute-start.25 = (bf16[320,128]{1,0:T(8,128)(2,1)S(1)}, bf16[320,128]{1,0:T(8,128)(2,1)S(1)}, u32[]{:S(2)}, u32[]{:S(2)}) collective-permute-start(bf16[320,128]{1,0:T(8,128)(2,1)S(1)} %bitcast.140), channel_id=1, source_target_pairs={{0,2},{2,0},{4,6},{6,4},{8,10},{10,8},{12,14},{14,12},{1,3},{3,1},... | collective-permute-start | bytes 245768 | tf_op jit(solution)/shard_map/ppermute | solution.py:21
  23.8 2.0 %collective-permute-start.27 = (bf16[320,128]{1,0:T(8,128)(2,1)S(1)}, bf16[320,128]{1,0:T(8,128)(2,1)S(1)}, u32[]{:S(2)}, u32[]{:S(2)}) collective-permute-start(bf16[320,128]{1,0:T(8,128)(2,1)S(1)} %bitcast.142), channel_id=1, source_target_pairs={{0,6},{2,4},{4,2},{6,0},{8,14},{10,12},{12,10},{14,8},{1,7},{3,5},... | collective-permute-start | bytes 245768 | tf_op jit(solution)/shard_map/ppermute | solution.py:21
  25.8 2.3 %collective-permute-start.28 = (bf16[320,128]{1,0:T(8,128)(2,1)S(1)}, bf16[320,128]{1,0:T(8,128)(2,1)S(1)}, u32[]{:S(2)}, u32[]{:S(2)}) collective-permute-start(bf16[320,128]{1,0:T(8,128)(2,1)S(1)} %bitcast.143), channel_id=1, source_target_pairs={{0,8},{2,10},{4,12},{6,14},{8,0},{10,2},{12,4},{14,6},{1,9},{3,11}... | collective-permute-start | bytes 245768 | tf_op jit(solution)/shard_map/ppermute | solution.py:21
  28.1 1.7 %collective-permute-done.6 = bf16[16,2560]{1,0:T(8,128)(2,1)S(1)} collective-permute-done((bf16[16,2560]{1,0:T(8,128)(2,1)S(1)}, bf16[16,2560]{1,0:T(8,128)(2,1)S(1)}, u32[]{:S(2)}, u32[]{:S(2)}) %collective-permute-start.6) | collective-permute-done | bytes 81952 | tf_op jit(solution)/shard_map/ppermute | solution.py:21
  29.9 3.7 %collective-permute-start.30 = (bf16[320,128]{1,0:T(8,128)(2,1)S(1)}, bf16[320,128]{1,0:T(8,128)(2,1)S(1)}, u32[]{:S(2)}, u32[]{:S(2)}) collective-permute-start(bf16[320,128]{1,0:T(8,128)(2,1)S(1)} %bitcast.145), channel_id=1, source_target_pairs={{0,12},{2,14},{4,8},{6,10},{8,4},{10,6},{12,0},{14,2},{1,13},{3,15... | collective-permute-start | bytes 245768 | tf_op jit(solution)/shard_map/ppermute | solution.py:21
  33.6 0.6 bitcast_dynamic-update-slice_fusion.15
  34.6 0.6 bitcast_dynamic-update-slice_fusion.14
  35.3 0.6 bitcast_dynamic-update-slice_fusion.13
  35.9 1.7 %collective-permute-done.28 = bf16[320,128]{1,0:T(8,128)(2,1)S(1)} collective-permute-done((bf16[320,128]{1,0:T(8,128)(2,1)S(1)}, bf16[320,128]{1,0:T(8,128)(2,1)S(1)}, u32[]{:S(2)}, u32[]{:S(2)}) %collective-permute-start.28) | collective-permute-done | bytes 81952 | tf_op jit(solution)/shard_map/ppermute | solution.py:21
  37.6 0.6 bitcast_dynamic-update-slice_fusion.12
  38.2 2.1 %collective-permute-done.29 = bf16[320,128]{1,0:T(8,128)(2,1)S(1)} collective-permute-done((bf16[320,128]{1,0:T(8,128)(2,1)S(1)}, bf16[320,128]{1,0:T(8,128)(2,1)S(1)}, u32[]{:S(2)}, u32[]{:S(2)}) %collective-permute-start.29) | collective-permute-done | bytes 81952 | tf_op jit(solution)/shard_map/ppermute | solution.py:21
  40.3 0.6 bitcast_dynamic-update-slice_fusion.11
  40.9 0.6 bitcast_dynamic-update-slice_fusion.10
  41.6 0.6 bitcast_dynamic-update-slice_fusion.9
  42.4 6.1 %convolution_bitcast_fusion.1 = f32[864,128]{1,0:T(8,128)S(1)} fusion(bf16[5120,864]{0,1:T(8,128)(2,1)} %param.11, bf16[128,2560]{1,0:T(8,128)(2,1)S(1)} %get-tuple-element.12, bf16[128,2560]{1,0:T(8,128)(2,1)S(1)} %get-tuple-element.11), kind=kOutput, calls=%fused_computation.26 | convolution fusion | flops 1135083520 | bytes 10600448 | tf_op jit(solution)/shard_map/dot_general | solution.py:94
  48.5 1.4 %broadcast_in_dim.185 = bf16[8,864,128]{2,1,0:T(8,128)(2,1)} broadcast(bf16[]{:T(256)} %constant.108.clone.1), dimensions={} | broadcast | bytes 1769474 | tf_op jit(solution)/shard_map/broadcast_in_dim | solution.py:18
  50.0 3.1 %bitcast_dynamic-update-slice_fusion.7 = (bf16[8,864,128]{2,1,0:T(8,128)(2,1)}, bf16[864,128]{1,0:T(8,128)(2,1)S(1)}) fusion(bf16[8,864,128]{2,1,0:T(8,128)(2,1)} %broadcast_in_dim.185, s32[]{:T(128)S(6)} %select_n.129, bf16[5120,864]{0,1:T(8,128)(2,1)S(1)} %bitcast.148, bf16[128,2560]{1,0:T(8,128)(2,1)S(1)} %get-tuple-element.12, ...), kind=kOutput, calls=%fused_computation.61 | convolution fusion | flops 1135747072 | bytes 11042820 | tf_op jit(solution)/shard_map/dot_general | solution.py:94
  53.1 0.5 collective-permute-start.17
  53.6 2.5 %collective-permute-start.18 = (bf16[864,128]{1,0:T(8,128)(2,1)S(1)}, bf16[864,128]{1,0:T(8,128)(2,1)}, u32[]{:S(2)}, u32[]{:S(2)}) collective-permute-start(bf16[864,128]{1,0:T(8,128)(2,1)S(1)} %get-tuple-element.21), channel_id=1, source_target_pairs={{0,4},{2,6},{4,0},{6,2},{8,12},{10,14},{12,8},{14,10},{1,5},{3,7},... | collective-permute-start | bytes 663560 | tf_op jit(solution)/shard_map/ppermute | solution.py:21
  56.1 1.0 collective-permute-start.19
  57.1 2.0 %collective-permute-start.20 = (bf16[864,128]{1,0:T(8,128)(2,1)S(1)}, bf16[864,128]{1,0:T(8,128)(2,1)}, u32[]{:S(2)}, u32[]{:S(2)}) collective-permute-start(bf16[864,128]{1,0:T(8,128)(2,1)S(1)} %get-tuple-element.21), channel_id=1, source_target_pairs={{0,8},{2,10},{4,12},{6,14},{8,0},{10,2},{12,4},{14,6},{1,9},{3,11}... | collective-permute-start | bytes 663560 | tf_op jit(solution)/shard_map/ppermute | solution.py:21
  59.3 1.6 %fusion.2 = bf16[5120,128]{0,1:T(8,128)(2,1)S(1)} fusion(bf16[864,128]{1,0:T(8,128)(2,1)S(1)} %get-tuple-element.21, bf16[864,5120]{1,0:T(8,128)(2,1)S(1)} %bitcast.134), kind=kOutput, calls=%fused_computation.6 | convolution fusion | flops 1133117440 | bytes 10379264 | tf_op jit(solution)/shard_map/dot_general | solution.py:104
  60.9 1.7 %copy.15 = bf16[5120,128]{1,0:T(8,128)(2,1)} copy(bf16[5120,128]{0,1:T(8,128)(2,1)S(1)} %fusion.2) | data formatting | bytes 2621440 | tf_op jit(solution)/shard_map/convert_element_type | solution.py:106
  62.6 1.1 dynamic-slice_bitcast_fusion
  63.7 1.0 collective-permute-start.21
  64.7 1.6 %bitcast_dynamic-update-slice_fusion.6 = bf16[8,864,128]{2,1,0:T(8,128)(2,1)} fusion(bf16[8,864,128]{2,1,0:T(8,128)(2,1)} %get-tuple-element.20, s32[]{:T(128)S(6)} %select_n.130, bf16[864,128]{1,0:T(8,128)(2,1)} %collective-permute-done.17), kind=kLoop, calls=%fused_computation.60 | loop fusion | bytes 442372 | tf_op jit(solution)/shard_map/jit(dynamic_update_index_in_dim)/dynamic_update_slice | solution.py:22
  66.3 1.7 %collective-permute-done.18 = bf16[864,128]{1,0:T(8,128)(2,1)} collective-permute-done((bf16[864,128]{1,0:T(8,128)(2,1)S(1)}, bf16[864,128]{1,0:T(8,128)(2,1)}, u32[]{:S(2)}, u32[]{:S(2)}) %collective-permute-start.18) | collective-permute-done | bytes 221216 | tf_op jit(solution)/shard_map/ppermute | solution.py:21
  68.0 2.8 %collective-permute-start.22 = (bf16[864,128]{1,0:T(8,128)(2,1)S(1)}, bf16[864,128]{1,0:T(8,128)(2,1)S(1)}, u32[]{:S(2)}, u32[]{:S(2)}) collective-permute-start(bf16[864,128]{1,0:T(8,128)(2,1)S(1)} %get-tuple-element.21), channel_id=1, source_target_pairs={{0,12},{2,14},{4,8},{6,10},{8,4},{10,6},{12,0},{14,2},{1,13},{3,15... | collective-permute-start | bytes 663560 | tf_op jit(solution)/shard_map/ppermute | solution.py:21
  70.8 1.6 %bitcast_dynamic-update-slice_fusion.5 = bf16[8,864,128]{2,1,0:T(8,128)(2,1)} fusion(bf16[8,864,128]{2,1,0:T(8,128)(2,1)} %bitcast_dynamic-update-slice_fusion.6, s32[]{:T(128)S(6)} %select_n.131, bf16[864,128]{1,0:T(8,128)(2,1)} %collective-permute-done.18), kind=kLoop, calls=%fused_computation.59 | loop fusion | bytes 442372 | tf_op jit(solution)/shard_map/jit(dynamic_update_index_in_dim)/dynamic_update_slice | solution.py:22
  72.4 1.3 collective-permute-done.19
  73.8 2.2 %collective-permute-start.23 = (bf16[864,128]{1,0:T(8,128)(2,1)S(1)}, bf16[864,128]{1,0:T(8,128)(2,1)S(1)}, u32[]{:S(2)}, u32[]{:S(2)}) collective-permute-start(bf16[864,128]{1,0:T(8,128)(2,1)S(1)} %get-tuple-element.21), channel_id=1, source_target_pairs={{0,14},{2,12},{4,10},{6,8},{8,6},{10,4},{12,2},{14,0},{1,15},{3,13... | collective-permute-start | bytes 663560 | tf_op jit(solution)/shard_map/ppermute | solution.py:21
  75.9 1.6 %bitcast_dynamic-update-slice_fusion.4 = bf16[8,864,128]{2,1,0:T(8,128)(2,1)} fusion(bf16[8,864,128]{2,1,0:T(8,128)(2,1)} %bitcast_dynamic-update-slice_fusion.5, s32[]{:T(128)S(6)} %select_n.132, bf16[864,128]{1,0:T(8,128)(2,1)} %collective-permute-done.19), kind=kLoop, calls=%fused_computation.58 | loop fusion | bytes 442372 | tf_op jit(solution)/shard_map/jit(dynamic_update_index_in_dim)/dynamic_update_slice | solution.py:22
  77.6 1.6 %bitcast_dynamic-update-slice_fusion.3 = bf16[8,864,128]{2,1,0:T(8,128)(2,1)} fusion(bf16[8,864,128]{2,1,0:T(8,128)(2,1)} %bitcast_dynamic-update-slice_fusion.4, s32[]{:T(128)S(6)} %select_n.133, bf16[864,128]{1,0:T(8,128)(2,1)} %collective-permute-done.20), kind=kLoop, calls=%fused_computation.57 | loop fusion | bytes 442372 | tf_op jit(solution)/shard_map/jit(dynamic_update_index_in_dim)/dynamic_update_slice | solution.py:22
  79.2 13.2 %collective-permute-done.21 = bf16[864,128]{1,0:T(8,128)(2,1)S(1)} collective-permute-done((bf16[864,128]{1,0:T(8,128)(2,1)S(1)}, bf16[864,128]{1,0:T(8,128)(2,1)S(1)}, u32[]{:S(2)}, u32[]{:S(2)}) %collective-permute-start.21) | collective-permute-done | bytes 221216 | tf_op jit(solution)/shard_map/ppermute | solution.py:21
  92.4 0.7 bitcast_dynamic-update-slice_fusion.2
  93.1 0.7 bitcast_dynamic-update-slice_fusion.1
  93.8 0.7 bitcast_dynamic-update-slice_fusion
  94.5 0.5 collective-permute-start.24
  95.3 2.4 %collective-permute-start.16 = (bf16[448,128]{1,0:T(8,128)(2,1)S(1)}, bf16[448,128]{1,0:T(8,128)(2,1)S(1)}, u32[]{:S(2)}, u32[]{:S(2)}) collective-permute-start(bf16[448,128]{1,0:T(8,128)(2,1)S(1)} %fusion.31), channel_id=1, source_target_pairs={{0,14},{2,12},{4,10},{6,8},{8,6},{10,4},{12,2},{14,0},{1,15},{3,13... | collective-permute-start | bytes 344072 | tf_op jit(solution)/shard_map/ppermute | solution.py:35
  97.7 1.6 %collective-permute-start.15 = (bf16[448,128]{1,0:T(8,128)(2,1)S(1)}, bf16[448,128]{1,0:T(8,128)(2,1)S(1)}, u32[]{:S(2)}, u32[]{:S(2)}) collective-permute-start(bf16[448,128]{1,0:T(8,128)(2,1)S(1)} %get-tuple-element.18), channel_id=1, source_target_pairs={{0,12},{2,14},{4,8},{6,10},{8,4},{10,6},{12,0},{14,2},{1,13},{3,15... | collective-permute-start | bytes 344072 | tf_op jit(solution)/shard_map/ppermute | solution.py:35
  99.3 10.6 %collective-permute-start.14 = (bf16[448,128]{1,0:T(8,128)(2,1)S(1)}, bf16[448,128]{1,0:T(8,128)(2,1)S(1)}, u32[]{:S(2)}, u32[]{:S(2)}) collective-permute-start(bf16[448,128]{1,0:T(8,128)(2,1)S(1)} %get-tuple-element.17), channel_id=1, source_target_pairs={{0,10},{2,8},{4,14},{6,12},{8,2},{10,0},{12,6},{14,4},{1,11},{3,9}... | collective-permute-start | bytes 344072 | tf_op jit(solution)/shard_map/ppermute | solution.py:35
  109.9 1.4 %select_bitcast_fusion.3 = (bf16[1,8,320,128]{3,2,0,1:T(8,128)(2,1)S(1)}, bf16[1,8,320,128]{3,2,0,1:T(8,128)(2,1)S(1)}) fusion(bf16[8,320,128]{2,1,0:T(8,128)(2,1)} %bitcast_dynamic-update-slice_fusion.9, bf16[8,320,128]{2,1,0:T(8,128)(2,1)} %collective-permute-done.32, pred[]{:T(512)S(6)} %eq.53), kind=kLoop, calls=%fused_computation.42 | loop fusion | flops 655360 | bytes 2621441 | tf_op jit(solution)/shard_map/stack | solution.py:45
  111.3 1.5 %collective-permute-start.12 = (bf16[448,128]{1,0:T(8,128)(2,1)S(1)}, bf16[448,128]{1,0:T(8,128)(2,1)S(1)}, u32[]{:S(2)}, u32[]{:S(2)}) collective-permute-start(bf16[448,128]{1,0:T(8,128)(2,1)S(1)} %get-tuple-element.15), channel_id=1, source_target_pairs={{0,6},{2,4},{4,2},{6,0},{8,14},{10,12},{12,10},{14,8},{1,7},{3,5},... | collective-permute-start | bytes 344072 | tf_op jit(solution)/shard_map/ppermute | solution.py:35
  112.8 6.3 %collective-permute-start.11 = (bf16[448,128]{1,0:T(8,128)(2,1)S(1)}, bf16[448,128]{1,0:T(8,128)(2,1)S(1)}, u32[]{:S(2)}, u32[]{:S(2)}) collective-permute-start(bf16[448,128]{1,0:T(8,128)(2,1)S(1)} %get-tuple-element.14), channel_id=1, source_target_pairs={{0,4},{2,6},{4,0},{6,2},{8,12},{10,14},{12,8},{14,10},{1,5},{3,7},... | collective-permute-start | bytes 344072 | tf_op jit(solution)/shard_map/ppermute | solution.py:35
  119.1 4.4 %collective-permute-done.14 = bf16[448,128]{1,0:T(8,128)(2,1)S(1)} collective-permute-done((bf16[448,128]{1,0:T(8,128)(2,1)S(1)}, bf16[448,128]{1,0:T(8,128)(2,1)S(1)}, u32[]{:S(2)}, u32[]{:S(2)}) %collective-permute-start.14) | collective-permute-done | bytes 114720 | tf_op jit(solution)/shard_map/ppermute | solution.py:35
  123.7 3.5 %collective-permute-done.11 = bf16[448,128]{1,0:T(8,128)(2,1)S(1)} collective-permute-done((bf16[448,128]{1,0:T(8,128)(2,1)S(1)}, bf16[448,128]{1,0:T(8,128)(2,1)S(1)}, u32[]{:S(2)}, u32[]{:S(2)}) %collective-permute-start.11) | collective-permute-done | bytes 114720 | tf_op jit(solution)/shard_map/ppermute | solution.py:35
  127.2 1.1 collective-permute-done.10
  128.4 1.4 %fusion.4 = bf16[1,64,5120]{2,1,0:T(8,128)(2,1)} fusion(bf16[5120,128]{1,0:T(8,128)(2,1)S(1)} %bitcast.138, f32[]{:T(128)S(6)} %div.8, pred[128]{0:T(512)(128)(4,1)S(1)} %and.5, bf16[448,128]{1,0:T(8,128)(2,1)S(1)} %get-tuple-element.5), kind=kOutput, calls=%fused_computation.9 | convolution fusion | flops 84549632 | bytes 1982980 | tf_op jit(solution)/shard_map/dot_general | solution.py:146
  129.9 0.8 fusion.32
  130.7 1.7 %select_bitcast_fusion.1 = (bf16[1,8,864,128]{3,2,0,1:T(8,128)(2,1)S(1)}, bf16[1,8,864,128]{3,2,0,1:T(8,128)(2,1)S(1)}) fusion(bf16[8,864,128]{2,1,0:T(8,128)(2,1)} %bitcast_dynamic-update-slice_fusion, bf16[8,864,128]{2,1,0:T(8,128)(2,1)S(1)} %collective-permute-done.24, pred[]{:T(512)S(6)} %eq.53), kind=kLoop, calls=%fused_computation.20 | loop fusion | flops 1769472 | bytes 7077889 | tf_op jit(solution)/shard_map/stack | solution.py:45
  132.8 2.6 %fusion.1 = bf16[1,64,13824]{2,1,0:T(8,128)(2,1)} fusion(bf16[13824,128]{1,0:T(8,128)(2,1)S(1)} %bitcast.135, f32[]{:T(128)S(6)} %div.8, bf16[448,128]{1,0:T(8,128)(2,1)S(1)} %get-tuple-element.5, pred[128]{0:T(512)(128)(4,1)S(1)} %eq.60), kind=kOutput, calls=%fused_computation.4 | convolution fusion | flops 228270080 | bytes 5325316 | tf_op jit(solution)/shard_map/dot_general | solution.py:146
  (87 shorter events, 3.2 us)
Async XLA Ops:
  0.6 16.0 %copy-start = (bf16[16,64,864]{2,1,0:T(8,128)(2,1)S(1)}, bf16[16,64,864]{2,1,0:T(8,128)(2,1)}, u32[]{:S(2)}) copy-start(bf16[16,64,864]{2,1,0:T(8,128)(2,1)} %param.14) | copy-start | bytes 5308420
  0.6 17.5 %copy-start.3 = (bf16[16,2560]{1,0:T(8,128)(2,1)S(1)}, bf16[16,2560]{1,0:T(8,128)(2,1)}, u32[]{:S(2)}) copy-start(bf16[16,2560]{1,0:T(8,128)(2,1)} %param.10) | copy-start | bytes 245764
  0.7 15.1 %copy-start.2 = (bf16[128,320]{0,1:T(8,128)(2,1)S(1)}, bf16[128,320]{0,1:T(8,128)(2,1)}, u32[]{:S(2)}) copy-start(bf16[128,320]{0,1:T(8,128)(2,1)} %param.16) | copy-start | bytes 245764
  0.7 17.5 %collective-permute-start = (bf16[16,2560]{1,0:T(8,128)(2,1)}, bf16[16,2560]{1,0:T(8,128)(2,1)S(1)}, u32[]{:S(2)}, u32[]{:S(2)}) collective-permute-start(bf16[16,2560]{1,0:T(8,128)(2,1)} %param.10), channel_id=1, source_target_pairs={{0,2},{2,0},{4,6},{6,4},{8,10},{10,8},{12,14},{14,12},{1,3},{3,1},... | collective-permute-start | bytes 245768 | tf_op jit(solution)/shard_map/ppermute | solution.py:21
  2.3 19.6 %collective-permute-start.1 = (bf16[16,2560]{1,0:T(8,128)(2,1)}, bf16[16,2560]{1,0:T(8,128)(2,1)S(1)}, u32[]{:S(2)}, u32[]{:S(2)}) collective-permute-start(bf16[16,2560]{1,0:T(8,128)(2,1)} %param.10), channel_id=1, source_target_pairs={{0,4},{2,6},{4,0},{6,2},{8,12},{10,14},{12,8},{14,10},{1,5},{3,7},... | collective-permute-start | bytes 245768 | tf_op jit(solution)/shard_map/ppermute | solution.py:21
  3.8 18.3 %collective-permute-start.2 = (bf16[16,2560]{1,0:T(8,128)(2,1)}, bf16[16,2560]{1,0:T(8,128)(2,1)S(1)}, u32[]{:S(2)}, u32[]{:S(2)}) collective-permute-start(bf16[16,2560]{1,0:T(8,128)(2,1)} %param.10), channel_id=1, source_target_pairs={{0,6},{2,4},{4,2},{6,0},{8,14},{10,12},{12,10},{14,8},{1,7},{3,5},... | collective-permute-start | bytes 245768 | tf_op jit(solution)/shard_map/ppermute | solution.py:21
  4.2 19.5 %collective-permute-start.3 = (bf16[16,2560]{1,0:T(8,128)(2,1)}, bf16[16,2560]{1,0:T(8,128)(2,1)S(1)}, u32[]{:S(2)}, u32[]{:S(2)}) collective-permute-start(bf16[16,2560]{1,0:T(8,128)(2,1)} %param.10), channel_id=1, source_target_pairs={{0,8},{2,10},{4,12},{6,14},{8,0},{10,2},{12,4},{14,6},{1,9},{3,11}... | collective-permute-start | bytes 245768 | tf_op jit(solution)/shard_map/ppermute | solution.py:21
  6.8 17.0 %collective-permute-start.4 = (bf16[16,2560]{1,0:T(8,128)(2,1)}, bf16[16,2560]{1,0:T(8,128)(2,1)S(1)}, u32[]{:S(2)}, u32[]{:S(2)}) collective-permute-start(bf16[16,2560]{1,0:T(8,128)(2,1)} %param.10), channel_id=1, source_target_pairs={{0,10},{2,8},{4,14},{6,12},{8,2},{10,0},{12,6},{14,4},{1,11},{3,9}... | collective-permute-start | bytes 245768 | tf_op jit(solution)/shard_map/ppermute | solution.py:21
  18.1 7.7 %collective-permute-start.5 = (bf16[16,2560]{1,0:T(8,128)(2,1)S(1)}, bf16[16,2560]{1,0:T(8,128)(2,1)S(1)}, u32[]{:S(2)}, u32[]{:S(2)}) collective-permute-start(bf16[16,2560]{1,0:T(8,128)(2,1)S(1)} %copy-done.3), channel_id=1, source_target_pairs={{0,12},{2,14},{4,8},{6,10},{8,4},{10,6},{12,0},{14,2},{1,13},{3,15... | collective-permute-start | bytes 245768 | tf_op jit(solution)/shard_map/ppermute | solution.py:21
  21.8 8.0 %collective-permute-start.6 = (bf16[16,2560]{1,0:T(8,128)(2,1)S(1)}, bf16[16,2560]{1,0:T(8,128)(2,1)S(1)}, u32[]{:S(2)}, u32[]{:S(2)}) collective-permute-start(bf16[16,2560]{1,0:T(8,128)(2,1)S(1)} %copy-done.3), channel_id=1, source_target_pairs={{0,14},{2,12},{4,10},{6,8},{8,6},{10,4},{12,2},{14,0},{1,15},{3,13... | collective-permute-start | bytes 245768 | tf_op jit(solution)/shard_map/ppermute | solution.py:21
  22.1 7.8 %collective-permute-start.25 = (bf16[320,128]{1,0:T(8,128)(2,1)S(1)}, bf16[320,128]{1,0:T(8,128)(2,1)S(1)}, u32[]{:S(2)}, u32[]{:S(2)}) collective-permute-start(bf16[320,128]{1,0:T(8,128)(2,1)S(1)} %bitcast.140), channel_id=1, source_target_pairs={{0,2},{2,0},{4,6},{6,4},{8,10},{10,8},{12,14},{14,12},{1,3},{3,1},... | collective-permute-start | bytes 245768 | tf_op jit(solution)/shard_map/ppermute | solution.py:21
  23.7 10.5 %collective-permute-start.26 = (bf16[320,128]{1,0:T(8,128)(2,1)S(1)}, bf16[320,128]{1,0:T(8,128)(2,1)S(1)}, u32[]{:S(2)}, u32[]{:S(2)}) collective-permute-start(bf16[320,128]{1,0:T(8,128)(2,1)S(1)} %bitcast.141), channel_id=1, source_target_pairs={{0,4},{2,6},{4,0},{6,2},{8,12},{10,14},{12,8},{14,10},{1,5},{3,7},... | collective-permute-start | bytes 245768 | tf_op jit(solution)/shard_map/ppermute | solution.py:21
  23.8 11.4 %collective-permute-start.27 = (bf16[320,128]{1,0:T(8,128)(2,1)S(1)}, bf16[320,128]{1,0:T(8,128)(2,1)S(1)}, u32[]{:S(2)}, u32[]{:S(2)}) collective-permute-start(bf16[320,128]{1,0:T(8,128)(2,1)S(1)} %bitcast.142), channel_id=1, source_target_pairs={{0,6},{2,4},{4,2},{6,0},{8,14},{10,12},{12,10},{14,8},{1,7},{3,5},... | collective-permute-start | bytes 245768 | tf_op jit(solution)/shard_map/ppermute | solution.py:21
  25.8 11.7 %collective-permute-start.28 = (bf16[320,128]{1,0:T(8,128)(2,1)S(1)}, bf16[320,128]{1,0:T(8,128)(2,1)S(1)}, u32[]{:S(2)}, u32[]{:S(2)}) collective-permute-start(bf16[320,128]{1,0:T(8,128)(2,1)S(1)} %bitcast.143), channel_id=1, source_target_pairs={{0,8},{2,10},{4,12},{6,14},{8,0},{10,2},{12,4},{14,6},{1,9},{3,11}... | collective-permute-start | bytes 245768 | tf_op jit(solution)/shard_map/ppermute | solution.py:21
  29.8 10.5 %collective-permute-start.29 = (bf16[320,128]{1,0:T(8,128)(2,1)S(1)}, bf16[320,128]{1,0:T(8,128)(2,1)S(1)}, u32[]{:S(2)}, u32[]{:S(2)}) collective-permute-start(bf16[320,128]{1,0:T(8,128)(2,1)S(1)} %bitcast.144), channel_id=1, source_target_pairs={{0,10},{2,8},{4,14},{6,12},{8,2},{10,0},{12,6},{14,4},{1,11},{3,9}... | collective-permute-start | bytes 245768 | tf_op jit(solution)/shard_map/ppermute | solution.py:21
  29.9 11.0 %collective-permute-start.30 = (bf16[320,128]{1,0:T(8,128)(2,1)S(1)}, bf16[320,128]{1,0:T(8,128)(2,1)S(1)}, u32[]{:S(2)}, u32[]{:S(2)}) collective-permute-start(bf16[320,128]{1,0:T(8,128)(2,1)S(1)} %bitcast.145), channel_id=1, source_target_pairs={{0,12},{2,14},{4,8},{6,10},{8,4},{10,6},{12,0},{14,2},{1,13},{3,15... | collective-permute-start | bytes 245768 | tf_op jit(solution)/shard_map/ppermute | solution.py:21
  34.2 7.4 %collective-permute-start.31 = (bf16[320,128]{1,0:T(8,128)(2,1)S(1)}, bf16[320,128]{1,0:T(8,128)(2,1)S(1)}, u32[]{:S(2)}, u32[]{:S(2)}) collective-permute-start(bf16[320,128]{1,0:T(8,128)(2,1)S(1)} %bitcast.146), channel_id=1, source_target_pairs={{0,14},{2,12},{4,10},{6,8},{8,6},{10,4},{12,2},{14,0},{1,15},{3,13... | collective-permute-start | bytes 245768 | tf_op jit(solution)/shard_map/ppermute | solution.py:21
  35.3 7.0 %collective-permute-start.7 = (bf16[128,2560]{1,0:T(8,128)(2,1)S(1)}, bf16[128,2560]{1,0:T(8,128)(2,1)S(1)}, u32[]{:S(2)}, u32[]{:S(2)}) collective-permute-start(bf16[128,2560]{1,0:T(8,128)(2,1)S(1)} %bitcast.139), channel_id=1, source_target_pairs={{0,1},{1,0},{2,3},{3,2},{4,5},{5,4},{6,7},{7,6},{8,9},{9,8},{10,11... | collective-permute-start | bytes 1966088 | tf_op jit(solution)/shard_map/ppermute | solution.py:43
  42.2 67.6 %collective-permute-start.32 = (bf16[8,320,128]{2,1,0:T(8,128)(2,1)}, bf16[8,320,128]{2,1,0:T(8,128)(2,1)}, u32[]{:S(2)}, u32[]{:S(2)}) collective-permute-start(bf16[8,320,128]{2,1,0:T(8,128)(2,1)} %bitcast_dynamic-update-slice_fusion.9), channel_id=1, source_target_pairs={{0,1},{1,0},{2,3},{3,2},{4,5},{5,4},{6,7},{7,6},{8,9},{9,8},{10,11... | collective-permute-start | bytes 1966088 | tf_op jit(solution)/shard_map/ppermute | solution.py:43
  42.2 7.7 %slice-start.3 = ((s8[8847360]{0:T(1024)(128)(4,1)}), s8[4194304]{0:T(1024)(128)(4,1)S(1)}, s32[]{:S(2)}) async-start(s8[8847360]{0:T(1024)(128)(4,1)} %bitcast.147), calls=%async_computation.3 | async-start | bytes 8388608
  42.4 7.6 %slice-start.4 = ((s8[8847360]{0:T(1024)(128)(4,1)}), s8[4194304]{0:T(1024)(128)(4,1)S(1)}, s32[]{:S(2)}) async-start(s8[8847360]{0:T(1024)(128)(4,1)} %bitcast.147), calls=%async_computation.4 | async-start | bytes 8388608
  42.4 7.6 %slice-start.5 = ((s8[8847360]{0:T(1024)(128)(4,1)}), s8[458752]{0:T(1024)(128)(4,1)S(1)}, s32[]{:S(2)}) async-start(s8[8847360]{0:T(1024)(128)(4,1)} %bitcast.147), calls=%async_computation.5 | async-start | bytes 917504
  48.5 10.8 %slice-start = ((s8[8847360]{0:T(1024)(128)(4,1)}), s8[4194304]{0:T(1024)(128)(4,1)S(1)}, s32[]{:S(2)}) async-start(s8[8847360]{0:T(1024)(128)(4,1)} %bitcast.133), calls=%async_computation | async-start | bytes 8388608
  50.0 9.3 %slice-start.1 = ((s8[8847360]{0:T(1024)(128)(4,1)}), s8[4194304]{0:T(1024)(128)(4,1)S(1)}, s32[]{:S(2)}) async-start(s8[8847360]{0:T(1024)(128)(4,1)} %bitcast.133), calls=%async_computation.1 | async-start | bytes 8388608
  50.0 9.3 %slice-start.2 = ((s8[8847360]{0:T(1024)(128)(4,1)}), s8[458752]{0:T(1024)(128)(4,1)S(1)}, s32[]{:S(2)}) async-start(s8[8847360]{0:T(1024)(128)(4,1)} %bitcast.133), calls=%async_computation.2 | async-start | bytes 917504
  53.1 10.6 %collective-permute-start.17 = (bf16[864,128]{1,0:T(8,128)(2,1)S(1)}, bf16[864,128]{1,0:T(8,128)(2,1)}, u32[]{:S(2)}, u32[]{:S(2)}) collective-permute-start(bf16[864,128]{1,0:T(8,128)(2,1)S(1)} %get-tuple-element.21), channel_id=1, source_target_pairs={{0,2},{2,0},{4,6},{6,4},{8,10},{10,8},{12,14},{14,12},{1,3},{3,1},... | collective-permute-start | bytes 663560 | tf_op jit(solution)/shard_map/ppermute | solution.py:21
  53.6 14.4 %collective-permute-start.18 = (bf16[864,128]{1,0:T(8,128)(2,1)S(1)}, bf16[864,128]{1,0:T(8,128)(2,1)}, u32[]{:S(2)}, u32[]{:S(2)}) collective-permute-start(bf16[864,128]{1,0:T(8,128)(2,1)S(1)} %get-tuple-element.21), channel_id=1, source_target_pairs={{0,4},{2,6},{4,0},{6,2},{8,12},{10,14},{12,8},{14,10},{1,5},{3,7},... | collective-permute-start | bytes 663560 | tf_op jit(solution)/shard_map/ppermute | solution.py:21
  56.1 17.7 %collective-permute-start.19 = (bf16[864,128]{1,0:T(8,128)(2,1)S(1)}, bf16[864,128]{1,0:T(8,128)(2,1)}, u32[]{:S(2)}, u32[]{:S(2)}) collective-permute-start(bf16[864,128]{1,0:T(8,128)(2,1)S(1)} %get-tuple-element.21), channel_id=1, source_target_pairs={{0,6},{2,4},{4,2},{6,0},{8,14},{10,12},{12,10},{14,8},{1,7},{3,5},... | collective-permute-start | bytes 663560 | tf_op jit(solution)/shard_map/ppermute | solution.py:21
  57.1 20.5 %collective-permute-start.20 = (bf16[864,128]{1,0:T(8,128)(2,1)S(1)}, bf16[864,128]{1,0:T(8,128)(2,1)}, u32[]{:S(2)}, u32[]{:S(2)}) collective-permute-start(bf16[864,128]{1,0:T(8,128)(2,1)S(1)} %get-tuple-element.21), channel_id=1, source_target_pairs={{0,8},{2,10},{4,12},{6,14},{8,0},{10,2},{12,4},{14,6},{1,9},{3,11}... | collective-permute-start | bytes 663560 | tf_op jit(solution)/shard_map/ppermute | solution.py:21
  63.7 31.3 %copy-start.1 = (bf16[5120,128]{1,0:T(8,128)(2,1)S(1)}, bf16[5120,128]{1,0:T(8,128)(2,1)}, u32[]{:S(2)}) copy-start(bf16[5120,128]{1,0:T(8,128)(2,1)} %copy.15) | copy-start | bytes 3932164
  63.7 28.6 %collective-permute-start.21 = (bf16[864,128]{1,0:T(8,128)(2,1)S(1)}, bf16[864,128]{1,0:T(8,128)(2,1)S(1)}, u32[]{:S(2)}, u32[]{:S(2)}) collective-permute-start(bf16[864,128]{1,0:T(8,128)(2,1)S(1)} %get-tuple-element.21), channel_id=1, source_target_pairs={{0,10},{2,8},{4,14},{6,12},{8,2},{10,0},{12,6},{14,4},{1,11},{3,9}... | collective-permute-start | bytes 663560 | tf_op jit(solution)/shard_map/ppermute | solution.py:21
  68.0 25.1 %collective-permute-start.22 = (bf16[864,128]{1,0:T(8,128)(2,1)S(1)}, bf16[864,128]{1,0:T(8,128)(2,1)S(1)}, u32[]{:S(2)}, u32[]{:S(2)}) collective-permute-start(bf16[864,128]{1,0:T(8,128)(2,1)S(1)} %get-tuple-element.21), channel_id=1, source_target_pairs={{0,12},{2,14},{4,8},{6,10},{8,4},{10,6},{12,0},{14,2},{1,13},{3,15... | collective-permute-start | bytes 663560 | tf_op jit(solution)/shard_map/ppermute | solution.py:21
  73.8 20.0 %collective-permute-start.23 = (bf16[864,128]{1,0:T(8,128)(2,1)S(1)}, bf16[864,128]{1,0:T(8,128)(2,1)S(1)}, u32[]{:S(2)}, u32[]{:S(2)}) collective-permute-start(bf16[864,128]{1,0:T(8,128)(2,1)S(1)} %get-tuple-element.21), channel_id=1, source_target_pairs={{0,14},{2,12},{4,10},{6,8},{8,6},{10,4},{12,2},{14,0},{1,15},{3,13... | collective-permute-start | bytes 663560 | tf_op jit(solution)/shard_map/ppermute | solution.py:21
  77.5 17.4 %collective-permute-start.9 = (bf16[128,128]{1,0:T(8,128)(2,1)S(1)}, bf16[128,128]{1,0:T(8,128)(2,1)S(1)}, u32[]{:S(2)}, u32[]{:S(2)}) collective-permute-start(bf16[128,128]{1,0:T(8,128)(2,1)S(1)} %pad_maximum_fusion.5), channel_id=1, source_target_pairs={{0,1},{1,0},{2,3},{3,2},{4,5},{5,4},{6,7},{7,6},{8,9},{9,8},{10,11... | collective-permute-start | bytes 98312 | tf_op jit(solution)/shard_map/ppermute | solution.py:112
  92.4 2.6 %collective-permute-start.8 = (bf16[8,320,128]{2,1,0:T(8,128)(2,1)S(1)}, bf16[8,320,128]{2,1,0:T(8,128)(2,1)S(1)}, u32[]{:S(2)}, u32[]{:S(2)}) collective-permute-start(bf16[8,320,128]{2,1,0:T(8,128)(2,1)S(1)} %dynamic-slice_bitcast_fusion), channel_id=1, source_target_pairs={{0,1},{1,0},{2,3},{3,2},{4,5},{5,4},{6,7},{7,6},{8,9},{9,8},{10,11... | collective-permute-start | bytes 1966088 | tf_op jit(solution)/shard_map/ppermute | solution.py:112
  94.5 36.2 %collective-permute-start.24 = (bf16[8,864,128]{2,1,0:T(8,128)(2,1)}, bf16[8,864,128]{2,1,0:T(8,128)(2,1)S(1)}, u32[]{:S(2)}, u32[]{:S(2)}) collective-permute-start(bf16[8,864,128]{2,1,0:T(8,128)(2,1)} %bitcast_dynamic-update-slice_fusion), channel_id=1, source_target_pairs={{0,1},{1,0},{2,3},{3,2},{4,5},{5,4},{6,7},{7,6},{8,9},{9,8},{10,11... | collective-permute-start | bytes 5308424 | tf_op jit(solution)/shard_map/ppermute | solution.py:43
  95.3 16.0 %collective-permute-start.16 = (bf16[448,128]{1,0:T(8,128)(2,1)S(1)}, bf16[448,128]{1,0:T(8,128)(2,1)S(1)}, u32[]{:S(2)}, u32[]{:S(2)}) collective-permute-start(bf16[448,128]{1,0:T(8,128)(2,1)S(1)} %fusion.31), channel_id=1, source_target_pairs={{0,14},{2,12},{4,10},{6,8},{8,6},{10,4},{12,2},{14,0},{1,15},{3,13... | collective-permute-start | bytes 344072 | tf_op jit(solution)/shard_map/ppermute | solution.py:35
  97.7 15.1 %collective-permute-start.15 = (bf16[448,128]{1,0:T(8,128)(2,1)S(1)}, bf16[448,128]{1,0:T(8,128)(2,1)S(1)}, u32[]{:S(2)}, u32[]{:S(2)}) collective-permute-start(bf16[448,128]{1,0:T(8,128)(2,1)S(1)} %get-tuple-element.18), channel_id=1, source_target_pairs={{0,12},{2,14},{4,8},{6,10},{8,4},{10,6},{12,0},{14,2},{1,13},{3,15... | collective-permute-start | bytes 344072 | tf_op jit(solution)/shard_map/ppermute | solution.py:35
  99.3 24.2 %collective-permute-start.14 = (bf16[448,128]{1,0:T(8,128)(2,1)S(1)}, bf16[448,128]{1,0:T(8,128)(2,1)S(1)}, u32[]{:S(2)}, u32[]{:S(2)}) collective-permute-start(bf16[448,128]{1,0:T(8,128)(2,1)S(1)} %get-tuple-element.17), channel_id=1, source_target_pairs={{0,10},{2,8},{4,14},{6,12},{8,2},{10,0},{12,6},{14,4},{1,11},{3,9}... | collective-permute-start | bytes 344072 | tf_op jit(solution)/shard_map/ppermute | solution.py:35
  111.2 12.4 %collective-permute-start.13 = (bf16[448,128]{1,0:T(8,128)(2,1)S(1)}, bf16[448,128]{1,0:T(8,128)(2,1)S(1)}, u32[]{:S(2)}, u32[]{:S(2)}) collective-permute-start(bf16[448,128]{1,0:T(8,128)(2,1)S(1)} %get-tuple-element.16), channel_id=1, source_target_pairs={{0,8},{2,10},{4,12},{6,14},{8,0},{10,2},{12,4},{14,6},{1,9},{3,11}... | collective-permute-start | bytes 344072 | tf_op jit(solution)/shard_map/ppermute | solution.py:35
  111.3 12.3 %collective-permute-start.12 = (bf16[448,128]{1,0:T(8,128)(2,1)S(1)}, bf16[448,128]{1,0:T(8,128)(2,1)S(1)}, u32[]{:S(2)}, u32[]{:S(2)}) collective-permute-start(bf16[448,128]{1,0:T(8,128)(2,1)S(1)} %get-tuple-element.15), channel_id=1, source_target_pairs={{0,6},{2,4},{4,2},{6,0},{8,14},{10,12},{12,10},{14,8},{1,7},{3,5},... | collective-permute-start | bytes 344072 | tf_op jit(solution)/shard_map/ppermute | solution.py:35
  112.8 14.4 %collective-permute-start.11 = (bf16[448,128]{1,0:T(8,128)(2,1)S(1)}, bf16[448,128]{1,0:T(8,128)(2,1)S(1)}, u32[]{:S(2)}, u32[]{:S(2)}) collective-permute-start(bf16[448,128]{1,0:T(8,128)(2,1)S(1)} %get-tuple-element.14), channel_id=1, source_target_pairs={{0,4},{2,6},{4,0},{6,2},{8,12},{10,14},{12,8},{14,10},{1,5},{3,7},... | collective-permute-start | bytes 344072 | tf_op jit(solution)/shard_map/ppermute | solution.py:35
  123.5 4.8 %collective-permute-start.10 = (bf16[448,128]{1,0:T(8,128)(2,1)S(1)}, bf16[448,128]{1,0:T(8,128)(2,1)S(1)}, u32[]{:S(2)}, u32[]{:S(2)}) collective-permute-start(bf16[448,128]{1,0:T(8,128)(2,1)S(1)} %get-tuple-element.13), channel_id=1, source_target_pairs={{0,2},{2,0},{4,6},{6,4},{8,10},{10,8},{12,14},{14,12},{1,3},{3,1},... | collective-permute-start | bytes 344072 | tf_op jit(solution)/shard_map/ppermute | solution.py:35

commit v2 on v1

--- a/solution.py
+++ b/solution.py
@@ -1,9 +1,369 @@
+import functools
+
 import jax
 import jax.numpy as jnp
 from jax import lax
+from jax.experimental import pallas as pl
+from jax.experimental.pallas import tpu as pltpu
 from jax.sharding import PartitionSpec as P
 
 lowrank_adapter_scale = 2.0
+
+ROWS_BY_ROWS = (((1,), (1,)), ((), ()))
+GRAD_FLOPS = 20_000_000_000
+IN_VMEM = pl.BlockSpec(memory_space=pltpu.VMEM)
+IN_HBM = pl.BlockSpec(memory_space=pl.ANY)
+IN_SMEM = pl.BlockSpec(memory_space=pltpu.SMEM)
+
+
+def kernel_call(body, out_shape, in_specs, flops, moved, scratch=(), out_specs=None, limit=16):
+    return pl.pallas_call(
+        body,
+        out_shape=out_shape,
+        in_specs=in_specs,
+        out_specs=jax.tree.map(lambda _: IN_VMEM, out_shape) if out_specs is None else out_specs,
+        scratch_shapes=list(scratch),
+        compiler_params=pltpu.CompilerParams(vmem_limit_bytes=limit << 20),
+        cost_estimate=pl.CostEstimate(flops=flops, bytes_accessed=moved, transcendentals=0),
+    )
+
+
+def assemble_body(me, core, *refs):
+    out = refs[-1]
+    count = (len(refs) - 1) // 2
+    rows, half = refs[0].shape
+    for k in range(count):
+        here = pl.ds(pl.multiple_of((me[0] ^ k) * rows, rows), rows)
+        out[here, pl.ds(pl.multiple_of(core[0] * half, 128), half)] = refs[k][...]
+        out[here, pl.ds(pl.multiple_of((1 - core[0]) * half, 128), half)] = refs[count + k][...]
+
+
+def token_facts(block_count, token_count):
+    lane = lax.broadcasted_iota(jnp.int32, (1, token_count), 1)
+    size = token_count // block_count
+    return [(lane >= b * size) & (lane < (b + 1) * size) for b in range(block_count)], lane, size
+
+
+def live_mask(length, block_count, token_count):
+    blocks, lane, size = token_facts(block_count, token_count)
+    live = jnp.zeros((1, token_count), jnp.bool_)
+    for b in range(block_count):
+        live = live | (blocks[b] & (lane < b * size + length[b]))
+    return live
+
+
+def chosen_mask(owner, mine, block_count, token_count):
+    blocks, lane, _ = token_facts(block_count, token_count)
+    first = lane < 0
+    for b in range(block_count):
+        first = first | (blocks[b] & (lane < jnp.where(owner[b] == mine, token_count, 0)))
+    return first
+
+
+def back_body(owner, length, adapter_out, cot, out):
+    block_count, token_count = owner.shape[0], cot.shape[1]
+    blocks, _, _ = token_facts(block_count, token_count)
+    columns = cot.shape[0]
+    out[:columns] = cot[...]
+    total = jnp.zeros((adapter_out.shape[1], token_count), jnp.float32)
+    for b in range(block_count):
+        every = jnp.dot(adapter_out[owner[b]], cot[...], preferred_element_type=jnp.float32)
+        total = jnp.where(blocks[b], every, total)
+    total = jnp.where(live_mask(length, block_count, token_count), total, 0.0)
+    out[columns:] = total.astype(out.dtype)
+
+
+def split_body(owner, core, base, hidden, adapter_in, kept, leaving):
+    block_count, token_count = owner.shape[0], base.shape[0]
+    rank = adapter_in.shape[1]
+    columns = (kept.shape[0] - rank) // 8
+    for b in range(8):
+        both = base[:, b * 2 * columns : (b + 1) * 2 * columns].astype(jnp.float32).T
+        both = both.astype(kept.dtype)
+        here = pl.ds(b * columns, columns)
+
+        @pl.when(core[0] == 0)
+        def _():
+            kept[here] = both[:columns]
+            leaving[here] = both[columns:]
+
+        @pl.when(core[0] != 0)
+        def _():
+            kept[here] = both[columns:]
+            leaving[here] = both[:columns]
+
+    blocks, _, _ = token_facts(block_count, token_count)
+    low = jnp.zeros((rank, token_count), jnp.float32)
+    for b in range(block_count):
+        every = jnp.dot(adapter_in[owner[b]], hidden[...], preferred_element_type=jnp.float32)
+        low = jnp.where(blocks[b], every, low)
+    tail = pl.ds(8 * columns, rank)
+    kept[tail] = low.astype(kept.dtype)
+    leaving[tail] = low.astype(kept.dtype)
+
+
+def add_body(me, kept, arrived, own, leaving):
+    rank = own.shape[0] - (kept.shape[0] - own.shape[0])
+    columns = (own.shape[0] - rank) // 4
+    side = me[0] % 2
+
+    def added(first, count):
+        here = pl.ds(first, count)
+        total = kept[here].astype(jnp.float32) + arrived[here].astype(jnp.float32)
+        return total.astype(own.dtype)
+
+    for z in range(4):
+        here = pl.ds(z * columns, columns)
+        own[here] = added(pl.multiple_of((2 * z + side) * columns, 16), columns)
+        leaving[here] = added(pl.multiple_of((2 * z + 1 - side) * columns, 16), columns)
+    low = added(8 * columns, rank)
+    own[4 * columns :] = low
+    leaving[4 * columns :] = low
+
+
+def add_pair_body(me, own, arrived, *refs):
+    outs = refs[-4:]
+    columns = (own.shape[0] - outs[0].shape[0]) // 3
+    place = me[0] // 2
+
+    def added(first, count):
+        here = pl.ds(first, count)
+        total = own[here].astype(jnp.float32) + arrived[here].astype(jnp.float32)
+        return total.astype(own.dtype)
+
+    low = added(4 * columns, own.shape[0] - 4 * columns)
+    for flip, out in enumerate(outs):
+        out[:columns] = added(pl.multiple_of((place ^ flip) * columns, 16), columns)
+        out[columns:] = low
+
+
+def final_body(owner, length, mine, adapter_out, *refs):
+    arrived, (mixed, ranked) = refs[:-2], refs[-2:]
+    block_count, token_count = owner.shape[0], mixed.shape[1]
+    columns = mixed.shape[0]
+    total = arrived[0][...].astype(jnp.float32)
+    for share in arrived[1:]:
+        total = total + share[...].astype(jnp.float32)
+    low = total[columns:]
+    blocks, _, _ = token_facts(block_count, token_count)
+    contribution = jnp.zeros(mixed.shape, jnp.float32)
+    for b in range(block_count):
+        every = lax.dot_general(
+            adapter_out[owner[b]],
+            low.astype(jnp.bfloat16),
+            (((0,), (0,)), ((), ())),
+            preferred_element_type=jnp.float32,
+        )
+        contribution = jnp.where(blocks[b], every, contribution)
+    mixed[...] = (total[:columns] + lowrank_adapter_scale * contribution).astype(mixed.dtype)
+    chosen = chosen_mask(owner, mine[0], block_count, token_count)
+    live = live_mask(length, block_count, token_count)
+    ranked[...] = jnp.where(chosen & live, low, 0.0).astype(ranked.dtype)
+
+
+def stack_body(me, *refs):
+    out = refs[-1]
+    for flip, piece in enumerate(refs[:-1]):
+        out[(me[0] // 2) ^ flip] = piece[...]
+
+
+def interleave_body(me, near, far, out):
+    side = me[0] % 2
+    for z in range(near.shape[0]):
+        out[2 * z + side] = near[z]
+        out[2 * z + 1 - side] = far[z]
+
+
+def gathered_body(owner, mine, core, gathered, gathered_other, features, ranked):
+    columns = features.shape[0] // (2 * gathered.shape[0])
+    back = jnp.zeros(ranked.shape, jnp.float32)
+    for half, pieces in ((core[0], gathered), (1 - core[0], gathered_other)):
+        for b in range(pieces.shape[0]):
+            here = pl.ds(pl.multiple_of((2 * b + half) * columns, 16), columns)
+            features[here] = pieces[b, :columns]
+            back = back + pieces[b, columns:].astype(jnp.float32)
+    chosen = chosen_mask(owner, mine[0], owner.shape[0], ranked.shape[1])
+    ranked[...] = jnp.where(chosen, back, 0.0).astype(ranked.dtype)
+
+
+def coefficient_of(owner, length, mine):
+    count = jnp.int32(0)
+    for b in range(owner.shape[0]):
+        count = count + jnp.where(owner[b] == mine[0], length[b], 0)
+    return lowrank_adapter_scale / jnp.maximum(count, 1).astype(jnp.float32)
+
+
+def grad_of_array_body(owner, length, mine, ranked, features, out):
+    total = lax.dot_general(
+        ranked[...], features[...], ROWS_BY_ROWS, preferred_element_type=jnp.float32
+    )
+    out[0] = (coefficient_of(owner, length, mine) * total).astype(out.dtype)
+
+
+def grad_of_pieces_body(owner, length, mine, me, ranked, *refs, flips):
+    near, near_other, far, far_other = refs[:4]
+    out, features, result, sems = refs[-4:]
+    rows = near.shape[0]
+    chip, core = (me[0] ^ flips) // 2, me[1]
+    lower = me[0] % 2
+    copies = []
+    for k, piece in enumerate((near, near_other, far, far_other)):
+        place = jnp.where(k < 2, lower, 1 - lower) * 2 + jnp.where(k % 2 == 0, core, 1 - core)
+        here = pl.ds(pl.multiple_of(place * rows, 16), rows)
+        copies.append(pltpu.make_async_copy(piece, features.at[here], sems.at[k]))
+    for copy in copies:
+        copy.start()
+    for copy in copies:
+        copy.wait()
+    total = lax.dot_general(
+        ranked[...], features[...], ROWS_BY_ROWS, preferred_element_type=jnp.float32
+    )
+    result[...] = (coefficient_of(owner, length, mine) * total).astype(result.dtype)
+    columns = 4 * rows
+    target = out.at[0, :, pl.ds(pl.multiple_of(chip * columns, 128), columns)]
+    copy = pltpu.make_async_copy(result, target, sems.at[4])
+    copy.start()
+    copy.wait()
+
+
+def on_chips(
+    tokens,
+    gate_weight,
+    up_weight,
+    down_weight,
+    adapter_in,
+    adapter_out,
+    cotangent,
+    block_owner,
+    block_length,
+    placement,
+):
+    f32, bf16 = jnp.float32, jnp.bfloat16
+    me, core = lax.axis_index("batch").reshape(1), lax.axis_index("tensor").reshape(1)
+    place = jnp.concatenate([me, core])
+    mine = lax.dynamic_slice_in_dim(placement, lax.axis_index(("batch", "tensor")), 1)
+    width = gate_weight.shape[1]
+    model_width = gate_weight.shape[0]
+    token_count, columns = cotangent.shape
+    rank = adapter_in.shape[1]
+    row_count = tokens.shape[0]
+
+    def flip(piece, k):
+        return lax.ppermute(piece, "batch", [(i, i ^ k) for i in range(8)])
+
+    def to_other_core(piece):
+        return lax.ppermute(piece, "tensor", [(0, 1), (1, 0)])
+
+    def along_z(piece):
+        return {0: piece, **{k: flip(piece, k) for k in (2, 4, 6)}}
+
+    def then_along_y(line):
+        return [line[k] if k in line else flip(line[k ^ 1], 1) for k in range(8)]
+
+    own = then_along_y(along_z(tokens))
+    other = [to_other_core(piece) for piece in own]
+    cot_t = cotangent.T
+    cot_and_back = kernel_call(
+        back_body,
+        jax.ShapeDtypeStruct((columns + rank, token_count), bf16),
+        [IN_SMEM, IN_SMEM, IN_VMEM, IN_VMEM],
+        flops=4 * rank * columns * token_count,
+        moved=2 * adapter_out.size,
+    )(block_owner, block_length, adapter_out, cot_t)
+    rows = kernel_call(
+        assemble_body,
+        jax.ShapeDtypeStruct((token_count, model_width), bf16),
+        [IN_SMEM, IN_SMEM] + [IN_VMEM] * 16,
+        flops=0,
+        moved=4 * token_count * model_width,
+    )(me, core, *own, *other)
+    line = along_z(cot_and_back)
+    stack = jax.ShapeDtypeStruct((4, columns + rank, token_count), bf16)
+    column = kernel_call(
+        stack_body, stack, [IN_SMEM] + [IN_VMEM] * 4, flops=0, moved=0
+    )(me, *[line[k] for k in (0, 2, 4, 6)])
+    both = jax.ShapeDtypeStruct((8, columns + rank, token_count), bf16)
+    gathered = kernel_call(
+        interleave_body, both, [IN_SMEM] + [IN_VMEM] * 2, flops=0, moved=0
+    )(me, column, flip(column, 1))
+    gathered_other = to_other_core(gathered)
+
+    gate_value = lax.dot_general(gate_weight.T, rows, ROWS_BY_ROWS, preferred_element_type=f32)
+    up_value = lax.dot_general(up_weight.T, rows, ROWS_BY_ROWS, preferred_element_type=f32)
+    hidden = (jax.nn.silu(gate_value) * up_value).astype(bf16)
+    line = along_z(hidden)
+    hidden_own = then_along_y(line)
+    base_part = lax.dot_general(
+        hidden, down_weight, (((0,), (0,)), ((), ())), preferred_element_type=f32
+    ).astype(bf16)
+    hidden_other = [to_other_core(piece) for piece in hidden_own]
+    halves = jax.ShapeDtypeStruct((8 * columns + rank, token_count), bf16)
+    kept, leaving = kernel_call(
+        split_body,
+        [halves, halves],
+        [IN_SMEM, IN_SMEM] + [IN_VMEM] * 3,
+        flops=4 * rank * width * token_count,
+        moved=4 * token_count * model_width,
+    )(block_owner, core, base_part, hidden, adapter_in)
+    quarter = jax.ShapeDtypeStruct((4 * columns + rank, token_count), bf16)
+    stays, leaving = kernel_call(
+        add_body, [quarter, quarter], [IN_SMEM] + [IN_VMEM] * 2, flops=0, moved=0
+    )(me, kept, to_other_core(leaving))
+    share = jax.ShapeDtypeStruct((columns + rank, token_count), bf16)
+    shares = kernel_call(
+        add_pair_body, [share] * 4, [IN_SMEM] + [IN_VMEM] * 2 + [IN_HBM] * 3, flops=0, moved=0
+    )(me, stays, flip(leaving, 1), *[line[k] for k in (2, 4, 6)])
+    shares = [shares[0]] + [flip(shares[z], 2 * z) for z in (1, 2, 3)]
+    mixed, low_chosen = kernel_call(
+        final_body,
+        [
+            jax.ShapeDtypeStruct((columns, token_count), bf16),
+            jax.ShapeDtypeStruct((rank, token_count), bf16),
+        ],
+        [IN_SMEM] * 3 + [IN_VMEM] * 5,
+        flops=4 * rank * columns * token_count,
+        moved=2 * halves.size,
+    )(block_owner, block_length, mine, adapter_out, *shares)
+    cot_all, back_chosen = kernel_call(
+        gathered_body,
+        [
+            jax.ShapeDtypeStruct((model_width, token_count), bf16),
+            jax.ShapeDtypeStruct((rank, token_count), bf16),
+        ],
+        [IN_SMEM] * 3 + [IN_VMEM] * 2,
+        flops=0,
+        moved=4 * token_count * model_width,
+    )(block_owner, mine, core, gathered, gathered_other)
+    grad_out = kernel_call(
+        grad_of_array_body,
+        jax.ShapeDtypeStruct((1, rank, model_width), bf16),
+        [IN_SMEM] * 3 + [IN_VMEM] * 2,
+        flops=2 * rank * token_count * model_width,
+        moved=3 * token_count * model_width,
+    )(block_owner, block_length, mine, low_chosen, cot_all)
+    grad_in = None
+    for k in (0, 2, 4, 6):
+        pieces = [hidden_own[k], hidden_other[k], hidden_own[k ^ 1], hidden_other[k ^ 1]]
+        buffers = [] if grad_in is None else [grad_in]
+        grad_in = pl.pallas_call(
+            functools.partial(grad_of_pieces_body, flips=k),
+            out_shape=jax.ShapeDtypeStruct((1, rank, 16 * width), bf16),
+            in_specs=[IN_SMEM] * 4 + [IN_VMEM] + [IN_HBM] * (4 + len(buffers)),
+            out_specs=IN_HBM,
+            scratch_shapes=[
+                pltpu.VMEM((4 * width, token_count), bf16),
+                pltpu.VMEM((rank, 4 * width), bf16),
+                pltpu.SemaphoreType.DMA((5,)),
+            ],
+            input_output_aliases={9: 0} if buffers else {},
+            compiler_params=pltpu.CompilerParams(vmem_limit_bytes=16 << 20),
+            cost_estimate=pl.CostEstimate(
+                flops=GRAD_FLOPS,
+                bytes_accessed=3 * token_count * 4 * width,
+                transcendentals=0,
+            ),
+        )(block_owner, block_length, mine, place, back_chosen, *pieces, *buffers)
+    return mixed.T, grad_in, grad_out
 
 
 def partner_shifts(count):
@@ -45,7 +405,7 @@
     return jnp.stack([jnp.where(mine_first, piece, other), jnp.where(mine_first, other, piece)])
 
 
-def on_device(
+def on_any_mesh(
     tokens,
     gate_weight,
     up_weight,
@@ -164,6 +524,9 @@
         P("groups"),
         P("groups"),
     )
+    on_device = on_any_mesh
+    if mesh.shape["batch"] == 8 and mesh.shape["tensor"] == 2:
+        on_device = on_chips
     return jax.shard_map(
         on_device,
         mesh=mesh,

time: 136 us -> 103 us (0.76)
  Pallas kernels: 0 us -> 24.3 us
  starting transfers between devices: 56.1 us -> 33 us
  local copies, waits for them, and re-layouts: 23.9 us -> 4.93 us
  other arithmetic: 6.76 us -> 0.08 us
  matrix products: 16 us -> 10.2 us
  waiting for transfers between devices: 30.8 us -> 27.8 us
    pallas_call x0 -> x14, Pallas kernels: none -> 24.3 us  [the longest x4 15.1 us: on_chips(): pl.pallas_call(functools.partial(grad_of_pieces_body, flips=k), out_shape...]
    ppermute x33 -> x40, starting transfers between devices: 56.1 us -> 33 us  [the longest x22 30.4 us: flip(): return lax.ppermute(piece, 'batch', [(i, i ^ k) for i in range(8)])]
    dynamic_update_slice x23 -> x0, local copies, waits for them, and re-layouts: 14.7 us -> none  [the longest x21 13.2 us: gather_pieces(): whole = lax.dynamic_update_index_in_dim(whole, arrived, me ^ k, 0)]
    dot_general x8 -> x3, matrix products: 16 us -> 10.2 us  [the longest x1 6.11 us: on_chips(): lax.dot_general(gate_weight.T, rows, ROWS_BY_ROWS, preferred_element_type...]
    unnamed x20 -> x32, local copies, waits for them, and re-layouts: 0.06 us -> 4.28 us
    another operation x5 -> x0, other arithmetic: 3.66 us -> none  [the longest x4 3.53 us: pair_gather(): jnp.stack([jnp.where(mine_first, piece, other), jnp.where(mine_first, oth...]
    ppermute x33 -> x40, waiting for transfers between devices: 30.8 us -> 27.8 us  [the longest x22 27.8 us: flip(): return lax.ppermute(piece, 'batch', [(i, i ^ k) for i in range(8)])]
    broadcast_in_dim x5 -> x0, local copies, waits for them, and re-layouts: 2.51 us -> none  [the longest x3 2.4 us: gather_pieces(): whole = jnp.zeros((count,) + piece.shape, piece.dtype)]
  transfers between devices with their start and end apart: 33 -> 40, of which waited for: 9 -> 11; matrix products, arithmetic and copies ran while one was open for 31% -> 11% of each run, Pallas kernels for 0% -> 19%
where the time goes in v2:
time: 103 us; the launch traced here: 101 us
  starting transfers between devices  33 us (32%)
  waiting for transfers between devices  27.8 us (27%)
  Pallas kernels  24.3 us (24%)
  matrix products  10.2 us (10%)
  local copies, waits for them, and re-layouts  4.93 us (5%)
    ppermute x22, starting transfers between devices, flip(): return lax.ppermute(piece, 'batch', [(i, i ^ k) for i in range(8)])  30.4 us
    ppermute x22, waiting for transfers between devices, flip(): return lax.ppermute(piece, 'batch', [(i, i ^ k) for i in range(8)])  27.8 us
    pallas_call x4, Pallas kernels, on_chips(): pl.pallas_call(functools.partial(grad_of_pieces_body, flips=k), out_shape...  15.1 us
    dot_general x1, matrix products, on_chips(): lax.dot_general(gate_weight.T, rows, ROWS_BY_ROWS, preferred_element_type...  6.11 us
    unnamed x32, local copies, waits for them, and re-layouts  4.28 us
    ppermute x18, starting transfers between devices, to_other_core(): return lax.ppermute(piece, 'tensor', [(0, 1), (1, 0)])  2.62 us
    pallas_call x1, Pallas kernels, on_chips(): kernel_call(grad_of_array_body, jax.ShapeDtypeStruct((1, rank, model_widt...  2.59 us
    dot_general x1, matrix products, on_chips(): lax.dot_general(up_weight.T, rows, ROWS_BY_ROWS, preferred_element_type=f32)  2.48 us
  transfers between devices with their start and end apart: 40, of which 11 were waited for; matrix products, arithmetic and copies ran while one was open for 11% of the time, Pallas kernels for 19%

profile of v2, /device:TPU:2, one launch (start us, length us, event | category | flops | bytes accessed | tf_op | source)
XLA Modules:
  0.0 101.3 jit_solution(14432930539650171732)
XLA Ops:
  0.6 1.6 %collective-permute-start.1 = (bf16[16,2560]{1,0:T(8,128)(2,1)}, bf16[16,2560]{1,0:T(8,128)(2,1)S(1)}, u32[]{:S(2)}, u32[]{:S(2)}) collective-permute-start(bf16[16,2560]{1,0:T(8,128)(2,1)} %refs_0_.1), channel_id=1, source_target_pairs={{0,4},{2,6},{4,0},{6,2},{8,12},{10,14},{12,8},{14,10},{1,5},{3,7},... | collective-permute-start | bytes 245768 | tf_op jit(solution)/shard_map/ppermute | solution.py:252
  2.3 2.6 %collective-permute-start.3 = (bf16[16,2560]{1,0:T(8,128)(2,1)}, bf16[16,2560]{1,0:T(8,128)(2,1)S(1)}, u32[]{:S(2)}, u32[]{:S(2)}) collective-permute-start(bf16[16,2560]{1,0:T(8,128)(2,1)} %refs_0_.1), channel_id=1, source_target_pairs={{0,8},{2,10},{4,12},{6,14},{8,0},{10,2},{12,4},{14,6},{1,9},{3,11}... | collective-permute-start | bytes 245768 | tf_op jit(solution)/shard_map/ppermute | solution.py:252
  4.9 0.2 collective-permute-start.5
  5.1 1.1 %copy-done = bf16[16,64,320]{2,1,0:T(8,128)(2,1)S(1)} copy-done((bf16[16,64,320]{2,1,0:T(8,128)(2,1)S(1)}, bf16[16,64,320]{2,1,0:T(8,128)(2,1)}, u32[]{:S(2)}) %copy-start) | copy-done | bytes 655384
  6.2 0.9 copy-done.3
  7.1 0.7 copy-done.5
  7.8 0.7 copy-done.7
  8.4 0.7 shard_map.126.refs_0_
  9.1 0.7 collective-permute-start.23
  9.9 3.5 %collective-permute-start.24 = (bf16[384,128]{1,0:T(8,128)(2,1)S(1)}, bf16[384,128]{1,0:T(8,128)(2,1)S(1)}, u32[]{:S(2)}, u32[]{:S(2)}) collective-permute-start(bf16[384,128]{1,0:T(8,128)(2,1)S(1)} %shard_map.126.refs_0_), channel_id=1, source_target_pairs={{0,8},{2,10},{4,12},{6,14},{8,0},{10,2},{12,4},{14,6},{1,9},{3,11}... | collective-permute-start | bytes 294920 | tf_op jit(solution)/shard_map/ppermute | solution.py:252
  13.4 0.2 collective-permute-start.25
  13.6 1.5 %collective-permute-start = (bf16[16,2560]{1,0:T(8,128)(2,1)}, bf16[16,2560]{1,0:T(8,128)(2,1)S(1)}, u32[]{:S(2)}, u32[]{:S(2)}) collective-permute-start(bf16[16,2560]{1,0:T(8,128)(2,1)} %refs_0_.1), channel_id=1, source_target_pairs={{0,2},{2,0},{4,6},{6,4},{8,10},{10,8},{12,14},{14,12},{1,3},{3,1},... | collective-permute-start | bytes 245768 | tf_op jit(solution)/shard_map/ppermute | solution.py:252
  15.1 3.1 %collective-permute-done.refs_1_ = bf16[16,2560]{1,0:T(8,128)(2,1)S(1)} collective-permute-done((bf16[16,2560]{1,0:T(8,128)(2,1)}, bf16[16,2560]{1,0:T(8,128)(2,1)S(1)}, u32[]{:S(2)}, u32[]{:S(2)}) %collective-permute-start) | collective-permute-done | bytes 81952 | tf_op jit(solution)/shard_map/ppermute | solution.py:252
  18.3 1.5 %collective-permute-start.2 = (bf16[16,2560]{1,0:T(8,128)(2,1)S(1)}, bf16[16,2560]{1,0:T(8,128)(2,1)S(1)}, u32[]{:S(2)}, u32[]{:S(2)}) collective-permute-start(bf16[16,2560]{1,0:T(8,128)(2,1)S(1)} %collective-permute-done.1.refs_2_), channel_id=1, source_target_pairs={{0,2},{2,0},{4,6},{6,4},{8,10},{10,8},{12,14},{14,12},{1,3},{3,1},... | collective-permute-start | bytes 245768 | tf_op jit(solution)/shard_map/ppermute | solution.py:252
  19.8 0.5 collective-permute-start.4
  20.3 1.5 %collective-permute-start.6 = (bf16[16,2560]{1,0:T(8,128)(2,1)S(1)}, bf16[16,2560]{1,0:T(8,128)(2,1)S(1)}, u32[]{:S(2)}, u32[]{:S(2)}) collective-permute-start(bf16[16,2560]{1,0:T(8,128)(2,1)S(1)} %collective-permute-done.5.refs_6_), channel_id=1, source_target_pairs={{0,2},{2,0},{4,6},{6,4},{8,10},{10,8},{12,14},{14,12},{1,3},{3,1},... | collective-permute-start | bytes 245768 | tf_op jit(solution)/shard_map/ppermute | solution.py:252
  21.8 0.5 collective-permute-start.13
  22.3 0.4 collective-permute-done.2.refs_3_
  22.7 1.5 %collective-permute-done.4.refs_5_ = bf16[16,2560]{1,0:T(8,128)(2,1)S(1)} collective-permute-done((bf16[16,2560]{1,0:T(8,128)(2,1)S(1)}, bf16[16,2560]{1,0:T(8,128)(2,1)S(1)}, u32[]{:S(2)}, u32[]{:S(2)}) %collective-permute-start.4) | collective-permute-done | bytes 81952 | tf_op jit(solution)/shard_map/ppermute | solution.py:252
  24.2 0.9 collective-permute-done.6.refs_7_
  25.1 0.5 collective-permute-start.12
  25.6 0.1 collective-permute-start.14
  25.7 1.2 %collective-permute-start.26 = (bf16[4,384,128]{2,1,0:T(8,128)(2,1)S(1)}, bf16[4,384,128]{2,1,0:T(8,128)(2,1)S(1)}, u32[]{:S(2)}, u32[]{:S(2)}) collective-permute-start(bf16[4,384,128]{2,1,0:T(8,128)(2,1)S(1)} %shard_map.127.near), channel_id=1, source_target_pairs={{0,2},{2,0},{4,6},{6,4},{8,10},{10,8},{12,14},{14,12},{1,3},{3,1},... | collective-permute-start | bytes 1179656 | tf_op jit(solution)/shard_map/ppermute | solution.py:252
  27.0 0.9 copy-done.4
  27.9 0.1 shard_map.121
  28.0 0.0 slice-start.1
  28.0 6.1 %convolution_bitcast_fusion.1 = f32[864,128]{1,0:T(8,128)S(1)} fusion(bf16[128,5120]{1,0:T(8,128)(2,1)S(1)} %shard_map.121, bf16[5120,864]{0,1:T(8,128)(2,1)} %param.11), kind=kOutput, calls=%fused_computation.2 | convolution fusion | flops 1132462080 | bytes 10600448 | tf_op jit(solution)/shard_map/dot_general | solution.py:291
  34.2 2.5 %multiply_convert_fusion.hidden.refs_0_ = bf16[864,128]{1,0:T(8,128)(2,1)S(1)} fusion(f32[864,128]{1,0:T(8,128)S(1)} %convolution_bitcast_fusion.1, bf16[128,5120]{1,0:T(8,128)(2,1)S(1)} %shard_map.121, bf16[5120,864]{0,1:T(8,128)(2,1)S(1)} %bitcast.16), kind=kOutput, calls=%fused_computation.3 | convolution fusion | flops 1133125632 | bytes 10821632 | tf_op jit(solution)/shard_map/dot_general | solution.py:292
  36.7 1.6 %convolution_convert_fusion.base = bf16[128,5120]{1,0:T(8,128)(2,1)S(1)} fusion(bf16[864,128]{1,0:T(8,128)(2,1)S(1)} %multiply_convert_fusion.hidden.refs_0_, bf16[864,5120]{1,0:T(8,128)(2,1)S(1)} %bitcast.18), kind=kOutput, calls=%fused_computation | convolution fusion | flops 1133117440 | bytes 10379264 | tf_op jit(solution)/shard_map/dot_general | solution.py:296
  38.3 2.2 %shard_map.122 = (bf16[2624,128]{1,0:T(8,128)(2,1)S(1)}, bf16[2624,128]{1,0:T(8,128)(2,1)S(1)}) custom-call(s32[2]{0:T(128)S(1)} %copy-done.6, s32[1]{0:T(128)} %bitcast.1.core, bf16[128,5120]{1,0:T(8,128)(2,1)S(1)} %convolution_convert_fusion.base, bf16[864,128]{1,0:T(8,128)(2,1)S(1)} %multiply_convert_fusion.hidden.refs_0_, bf16[16,64,864]{2,1,0:T(8,128)(2,1)S(1)} %copy-done.2), custom_call_target="tpu_custom_call" | custom-call | flops 28311552 | bytes 2621440 | tf_op jit(solution)/shard_map/pallas_call | solution.py:301
  40.5 0.2 collective-permute-start.15
  40.7 0.1 shard_map.128.gathered
  40.8 0.4 collective-permute-start.27
  41.2 1.1 %collective-permute-start.38 = (bf16[864,128]{1,0:T(8,128)(2,1)S(1)}, bf16[864,128]{1,0:T(8,128)(2,1)}, u32[]{:S(2)}, u32[]{:S(2)}) collective-permute-start(bf16[864,128]{1,0:T(8,128)(2,1)S(1)} %multiply_convert_fusion.hidden.refs_0_), channel_id=1, source_target_pairs={{0,2},{2,0},{4,6},{6,4},{8,10},{10,8},{12,14},{14,12},{1,3},{3,1},... | collective-permute-start | bytes 663560 | tf_op jit(solution)/shard_map/ppermute | solution.py:252
  42.3 0.5 collective-permute-start.17
  42.8 4.1 %collective-permute-start.18 = (bf16[864,128]{1,0:T(8,128)(2,1)S(1)}, bf16[864,128]{1,0:T(8,128)(2,1)S(1)}, u32[]{:S(2)}, u32[]{:S(2)}) collective-permute-start(bf16[864,128]{1,0:T(8,128)(2,1)S(1)} %multiply_convert_fusion.hidden.refs_0_), channel_id=1, source_target_pairs={{0,8},{2,10},{4,12},{6,14},{8,0},{10,2},{12,4},{14,6},{1,9},{3,11}... | collective-permute-start | bytes 663560 | tf_op jit(solution)/shard_map/ppermute | solution.py:252
  46.9 0.2 shard_map.123
  47.1 1.7 %collective-permute-done.38.refs_2_ = bf16[864,128]{1,0:T(8,128)(2,1)} collective-permute-done((bf16[864,128]{1,0:T(8,128)(2,1)S(1)}, bf16[864,128]{1,0:T(8,128)(2,1)}, u32[]{:S(2)}, u32[]{:S(2)}) %collective-permute-start.38) | collective-permute-done | bytes 221216 | tf_op jit(solution)/shard_map/ppermute | solution.py:252
  48.8 1.1 %collective-permute-start.16 = (bf16[1344,128]{1,0:T(8,128)(2,1)S(1)}, bf16[1344,128]{1,0:T(8,128)(2,1)S(1)}, u32[]{:S(2)}, u32[]{:S(2)}) collective-permute-start(bf16[1344,128]{1,0:T(8,128)(2,1)S(1)} %get-tuple-element.18), channel_id=1, source_target_pairs={{0,2},{2,0},{4,6},{6,4},{8,10},{10,8},{12,14},{14,12},{1,3},{3,1},... | collective-permute-start | bytes 1032200 | tf_op jit(solution)/shard_map/ppermute | solution.py:252
  49.9 3.7 %collective-permute-done.17.refs_0_ = bf16[864,128]{1,0:T(8,128)(2,1)S(1)} collective-permute-done((bf16[864,128]{1,0:T(8,128)(2,1)S(1)}, bf16[864,128]{1,0:T(8,128)(2,1)S(1)}, u32[]{:S(2)}, u32[]{:S(2)}) %collective-permute-start.17) | collective-permute-done | bytes 221216 | tf_op jit(solution)/shard_map/ppermute | solution.py:252
  53.6 9.1 %collective-permute-done.18.refs_1_.refs_0_ = bf16[864,128]{1,0:T(8,128)(2,1)S(1)} collective-permute-done((bf16[864,128]{1,0:T(8,128)(2,1)S(1)}, bf16[864,128]{1,0:T(8,128)(2,1)S(1)}, u32[]{:S(2)}, u32[]{:S(2)}) %collective-permute-start.18) | collective-permute-done | bytes 221216 | tf_op jit(solution)/shard_map/ppermute | solution.py:252
  62.7 1.0 collective-permute-start.35
  63.7 0.6 dynamic_slice.3.mine
  64.3 0.1 pad_add_fusion.me
  64.4 0.2 collective-permute-start.34
  64.6 0.1 shard_map.124
  64.7 1.1 %collective-permute-start.32 = (bf16[864,128]{1,0:T(8,128)(2,1)S(1)}, bf16[864,128]{1,0:T(8,128)(2,1)S(1)}, u32[]{:S(2)}, u32[]{:S(2)}) collective-permute-start(bf16[864,128]{1,0:T(8,128)(2,1)S(1)} %collective-permute-done.18.refs_1_.refs_0_), channel_id=1, source_target_pairs={{0,2},{2,0},{4,6},{6,4},{8,10},{10,8},{12,14},{14,12},{1,3},{3,1},... | collective-permute-start | bytes 663560 | tf_op jit(solution)/shard_map/ppermute | solution.py:252
  65.9 1.3 %shard_map.129 = (bf16[5120,128]{1,0:T(8,128)(2,1)S(1)}, bf16[64,128]{1,0:T(8,128)(2,1)S(1)}) custom-call(s32[2]{0:T(128)S(1)} %copy-done.6, s32[1]{0:T(128)} %dynamic_slice.3.mine, s32[1]{0:T(128)} %bitcast.1.core, bf16[8,384,128]{2,1,0:T(8,128)(2,1)S(1)} %shard_map.128.gathered, bf16[8,384,128]{2,1,0:T(8,128)(2,1)S(1)} %collective-permute-done.27.gathered_other), custom_call_target="tpu_custom_call" | custom-call | bytes 2621440 | tf_op jit(solution)/shard_map/pallas_call | solution.py:327
  67.2 0.1 collective-permute-start.31
  67.3 1.0 %collective-permute-start.29 = (bf16[864,128]{1,0:T(8,128)(2,1)S(1)}, bf16[864,128]{1,0:T(8,128)(2,1)S(1)}, u32[]{:S(2)}, u32[]{:S(2)}) collective-permute-start(bf16[864,128]{1,0:T(8,128)(2,1)S(1)} %collective-permute-done.19.refs_2_.refs_0_), channel_id=1, source_target_pairs={{0,2},{2,0},{4,6},{6,4},{8,10},{10,8},{12,14},{14,12},{1,3},{3,1},... | collective-permute-start | bytes 663560 | tf_op jit(solution)/shard_map/ppermute | solution.py:252
  68.3 2.7 %collective-permute-done.35.refs_2_ = bf16[864,128]{1,0:T(8,128)(2,1)} collective-permute-done((bf16[864,128]{1,0:T(8,128)(2,1)S(1)}, bf16[864,128]{1,0:T(8,128)(2,1)}, u32[]{:S(2)}, u32[]{:S(2)}) %collective-permute-start.35) | collective-permute-done | bytes 221216 | tf_op jit(solution)/shard_map/ppermute | solution.py:252
  71.0 3.9 %shard_map.130.refs_4_ = bf16[1,64,13824]{2,1,0:T(8,128)(2,1)} custom-call(s32[2]{0:T(128)S(1)} %copy-done.6, s32[2]{0:T(128)S(1)} %copy-done.8, s32[1]{0:T(128)} %dynamic_slice.3.mine, s32[2]{0:T(128)S(1)} %pad_add_fusion.me, bf16[64,128]{1,0:T(8,128)(2,1)S(1)} %get-tuple-element.24.ranked, bf16[864,128]{1,0:T(8,128)(2,1)S(1)} %multiply_convert_fusion.hidden.refs_0_, ...), custom_call_target="tpu_custom_call" | custom-call | flops 20000000000 | bytes 1327104 | tf_op jit(solution)/shard_map/pallas_call | solution.py:348
  74.9 0.6 collective-permute-start.28
  75.5 0.2 collective-permute-done.32.refs_2_
  75.7 4.4 %collective-permute-done.29.refs_2_ = bf16[864,128]{1,0:T(8,128)(2,1)S(1)} collective-permute-done((bf16[864,128]{1,0:T(8,128)(2,1)S(1)}, bf16[864,128]{1,0:T(8,128)(2,1)S(1)}, u32[]{:S(2)}, u32[]{:S(2)}) %collective-permute-start.29) | collective-permute-done | bytes 221216 | tf_op jit(solution)/shard_map/ppermute | solution.py:252
  80.0 2.8 %collective-permute-start.20 = (bf16[384,128]{1,0:T(8,128)(2,1)S(1)}, bf16[384,128]{1,0:T(8,128)(2,1)S(1)}, u32[]{:S(2)}, u32[]{:S(2)}) collective-permute-start(bf16[384,128]{1,0:T(8,128)(2,1)S(1)} %get-tuple-element.20), channel_id=1, source_target_pairs={{0,4},{2,6},{4,0},{6,2},{8,12},{10,14},{12,8},{14,10},{1,5},{3,7},... | collective-permute-start | bytes 294920 | tf_op jit(solution)/shard_map/ppermute | solution.py:252
  82.8 4.0 %shard_map.131.refs_4_ = bf16[1,64,13824]{2,1,0:T(8,128)(2,1)} custom-call(s32[2]{0:T(128)S(1)} %copy-done.6, s32[2]{0:T(128)S(1)} %copy-done.8, s32[1]{0:T(128)} %dynamic_slice.3.mine, s32[2]{0:T(128)S(1)} %pad_add_fusion.me, bf16[64,128]{1,0:T(8,128)(2,1)S(1)} %get-tuple-element.24.ranked, ...), custom_call_target="tpu_custom_call", output_to_operand_aliasing={{}: (9, {})} | custom-call | flops 20000000000 | bytes 1327104 | tf_op jit(solution)/shard_map/pallas_call | solution.py:348
  86.8 1.0 collective-permute-start.21
  87.8 1.5 %collective-permute-start.22 = (bf16[384,128]{1,0:T(8,128)(2,1)S(1)}, bf16[384,128]{1,0:T(8,128)(2,1)S(1)}, u32[]{:S(2)}, u32[]{:S(2)}) collective-permute-start(bf16[384,128]{1,0:T(8,128)(2,1)S(1)} %get-tuple-element.22), channel_id=1, source_target_pairs={{0,12},{2,14},{4,8},{6,10},{8,4},{10,6},{12,0},{14,2},{1,13},{3,15... | collective-permute-start | bytes 294920 | tf_op jit(solution)/shard_map/ppermute | solution.py:252
  89.3 3.6 %shard_map.132.refs_4_ = bf16[1,64,13824]{2,1,0:T(8,128)(2,1)} custom-call(s32[2]{0:T(128)S(1)} %copy-done.6, s32[2]{0:T(128)S(1)} %copy-done.8, s32[1]{0:T(128)} %dynamic_slice.3.mine, s32[2]{0:T(128)S(1)} %pad_add_fusion.me, bf16[64,128]{1,0:T(8,128)(2,1)S(1)} %get-tuple-element.24.ranked, ...), custom_call_target="tpu_custom_call", output_to_operand_aliasing={{}: (9, {})} | custom-call | flops 20000000000 | bytes 1327104 | tf_op jit(solution)/shard_map/pallas_call | solution.py:348
  92.9 3.7 %shard_map.133 = bf16[1,64,13824]{2,1,0:T(8,128)(2,1)} custom-call(s32[2]{0:T(128)S(1)} %copy-done.6, s32[2]{0:T(128)S(1)} %copy-done.8, s32[1]{0:T(128)} %dynamic_slice.3.mine, s32[2]{0:T(128)S(1)} %pad_add_fusion.me, bf16[64,128]{1,0:T(8,128)(2,1)S(1)} %get-tuple-element.24.ranked, ...), custom_call_target="tpu_custom_call", output_to_operand_aliasing={{}: (9, {})} | custom-call | flops 20000000000 | bytes 1327104 | tf_op jit(solution)/shard_map/pallas_call | solution.py:348
  96.6 0.1 collective-permute-done.21.refs_2_
  96.7 2.0 %shard_map.125 = (bf16[320,128]{1,0:T(8,128)(2,1)}, bf16[64,128]{1,0:T(8,128)(2,1)S(1)}) custom-call(s32[2]{0:T(128)S(1)} %copy-done.6, s32[2]{0:T(128)S(1)} %copy-done.8, s32[1]{0:T(128)} %dynamic_slice.3.mine, bf16[16,64,320]{2,1,0:T(8,128)(2,1)S(1)} %copy-done.1, bf16[384,128]{1,0:T(8,128)(2,1)S(1)} %get-tuple-element.19.refs_0_, ...), custom_call_target="tpu_custom_call" | custom-call | flops 10485760 | bytes 671744 | tf_op jit(solution)/shard_map/pallas_call | solution.py:317
  98.7 2.6 %shard_map.134 = bf16[1,64,5120]{2,1,0:T(8,128)(2,1)} custom-call(s32[2]{0:T(128)S(1)} %copy-done.6, s32[2]{0:T(128)S(1)} %copy-done.8, s32[1]{0:T(128)} %dynamic_slice.3.mine, bf16[64,128]{1,0:T(8,128)(2,1)S(1)} %get-tuple-element.25.ranked, bf16[5120,128]{1,0:T(8,128)(2,1)S(1)} %get-tuple-element.26.features), custom_call_target="tpu_custom_call" | custom-call | flops 83886080 | bytes 1966080 | tf_op jit(solution)/shard_map/pallas_call | solution.py:337
  (69 shorter events, 0.2 us)
Async XLA Ops:
  0.6 12.7 %collective-permute-start.1 = (bf16[16,2560]{1,0:T(8,128)(2,1)}, bf16[16,2560]{1,0:T(8,128)(2,1)S(1)}, u32[]{:S(2)}, u32[]{:S(2)}) collective-permute-start(bf16[16,2560]{1,0:T(8,128)(2,1)} %refs_0_.1), channel_id=1, source_target_pairs={{0,4},{2,6},{4,0},{6,2},{8,12},{10,14},{12,8},{14,10},{1,5},{3,7},... | collective-permute-start | bytes 245768 | tf_op jit(solution)/shard_map/ppermute | solution.py:252
  2.3 11.3 %collective-permute-start.3 = (bf16[16,2560]{1,0:T(8,128)(2,1)}, bf16[16,2560]{1,0:T(8,128)(2,1)S(1)}, u32[]{:S(2)}, u32[]{:S(2)}) collective-permute-start(bf16[16,2560]{1,0:T(8,128)(2,1)} %refs_0_.1), channel_id=1, source_target_pairs={{0,8},{2,10},{4,12},{6,14},{8,0},{10,2},{12,4},{14,6},{1,9},{3,11}... | collective-permute-start | bytes 245768 | tf_op jit(solution)/shard_map/ppermute | solution.py:252
  4.9 10.3 %collective-permute-start.5 = (bf16[16,2560]{1,0:T(8,128)(2,1)}, bf16[16,2560]{1,0:T(8,128)(2,1)S(1)}, u32[]{:S(2)}, u32[]{:S(2)}) collective-permute-start(bf16[16,2560]{1,0:T(8,128)(2,1)} %refs_0_.1), channel_id=1, source_target_pairs={{0,12},{2,14},{4,8},{6,10},{8,4},{10,6},{12,0},{14,2},{1,13},{3,15... | collective-permute-start | bytes 245768 | tf_op jit(solution)/shard_map/ppermute | solution.py:252
  5.1 1.1 %copy-start = (bf16[16,64,320]{2,1,0:T(8,128)(2,1)S(1)}, bf16[16,64,320]{2,1,0:T(8,128)(2,1)}, u32[]{:S(2)}) copy-start(bf16[16,64,320]{2,1,0:T(8,128)(2,1)} %adapter_out.3) | copy-start | bytes 1966084
  6.2 0.9 copy-start.3
  7.1 0.7 copy-start.5
  7.8 0.7 copy-start.7
  9.1 11.1 %collective-permute-start.23 = (bf16[384,128]{1,0:T(8,128)(2,1)S(1)}, bf16[384,128]{1,0:T(8,128)(2,1)S(1)}, u32[]{:S(2)}, u32[]{:S(2)}) collective-permute-start(bf16[384,128]{1,0:T(8,128)(2,1)S(1)} %shard_map.126.refs_0_), channel_id=1, source_target_pairs={{0,4},{2,6},{4,0},{6,2},{8,12},{10,14},{12,8},{14,10},{1,5},{3,7},... | collective-permute-start | bytes 294920 | tf_op jit(solution)/shard_map/ppermute | solution.py:252
  9.9 11.9 %collective-permute-start.24 = (bf16[384,128]{1,0:T(8,128)(2,1)S(1)}, bf16[384,128]{1,0:T(8,128)(2,1)S(1)}, u32[]{:S(2)}, u32[]{:S(2)}) collective-permute-start(bf16[384,128]{1,0:T(8,128)(2,1)S(1)} %shard_map.126.refs_0_), channel_id=1, source_target_pairs={{0,8},{2,10},{4,12},{6,14},{8,0},{10,2},{12,4},{14,6},{1,9},{3,11}... | collective-permute-start | bytes 294920 | tf_op jit(solution)/shard_map/ppermute | solution.py:252
  13.4 8.4 %collective-permute-start.25 = (bf16[384,128]{1,0:T(8,128)(2,1)S(1)}, bf16[384,128]{1,0:T(8,128)(2,1)S(1)}, u32[]{:S(2)}, u32[]{:S(2)}) collective-permute-start(bf16[384,128]{1,0:T(8,128)(2,1)S(1)} %shard_map.126.refs_0_), channel_id=1, source_target_pairs={{0,12},{2,14},{4,8},{6,10},{8,4},{10,6},{12,0},{14,2},{1,13},{3,15... | collective-permute-start | bytes 294920 | tf_op jit(solution)/shard_map/ppermute | solution.py:252
  13.6 4.7 %collective-permute-start = (bf16[16,2560]{1,0:T(8,128)(2,1)}, bf16[16,2560]{1,0:T(8,128)(2,1)S(1)}, u32[]{:S(2)}, u32[]{:S(2)}) collective-permute-start(bf16[16,2560]{1,0:T(8,128)(2,1)} %refs_0_.1), channel_id=1, source_target_pairs={{0,2},{2,0},{4,6},{6,4},{8,10},{10,8},{12,14},{14,12},{1,3},{3,1},... | collective-permute-start | bytes 245768 | tf_op jit(solution)/shard_map/ppermute | solution.py:252
  15.1 4.7 %collective-permute-start.7 = (bf16[16,2560]{1,0:T(8,128)(2,1)}, bf16[16,2560]{1,0:T(8,128)(2,1)S(1)}, u32[]{:S(2)}, u32[]{:S(2)}) collective-permute-start(bf16[16,2560]{1,0:T(8,128)(2,1)} %refs_0_.1), channel_id=1, source_target_pairs={{0,1},{1,0},{2,3},{3,2},{4,5},{5,4},{6,7},{7,6},{8,9},{9,8},{10,11... | collective-permute-start | bytes 245768 | tf_op jit(solution)/shard_map/ppermute | solution.py:255
  18.3 4.4 %collective-permute-start.2 = (bf16[16,2560]{1,0:T(8,128)(2,1)S(1)}, bf16[16,2560]{1,0:T(8,128)(2,1)S(1)}, u32[]{:S(2)}, u32[]{:S(2)}) collective-permute-start(bf16[16,2560]{1,0:T(8,128)(2,1)S(1)} %collective-permute-done.1.refs_2_), channel_id=1, source_target_pairs={{0,2},{2,0},{4,6},{6,4},{8,10},{10,8},{12,14},{14,12},{1,3},{3,1},... | collective-permute-start | bytes 245768 | tf_op jit(solution)/shard_map/ppermute | solution.py:252
  19.8 4.4 %collective-permute-start.4 = (bf16[16,2560]{1,0:T(8,128)(2,1)S(1)}, bf16[16,2560]{1,0:T(8,128)(2,1)S(1)}, u32[]{:S(2)}, u32[]{:S(2)}) collective-permute-start(bf16[16,2560]{1,0:T(8,128)(2,1)S(1)} %collective-permute-done.3.refs_4_), channel_id=1, source_target_pairs={{0,2},{2,0},{4,6},{6,4},{8,10},{10,8},{12,14},{14,12},{1,3},{3,1},... | collective-permute-start | bytes 245768 | tf_op jit(solution)/shard_map/ppermute | solution.py:252
  20.3 4.8 %collective-permute-start.6 = (bf16[16,2560]{1,0:T(8,128)(2,1)S(1)}, bf16[16,2560]{1,0:T(8,128)(2,1)S(1)}, u32[]{:S(2)}, u32[]{:S(2)}) collective-permute-start(bf16[16,2560]{1,0:T(8,128)(2,1)S(1)} %collective-permute-done.5.refs_6_), channel_id=1, source_target_pairs={{0,2},{2,0},{4,6},{6,4},{8,10},{10,8},{12,14},{14,12},{1,3},{3,1},... | collective-permute-start | bytes 245768 | tf_op jit(solution)/shard_map/ppermute | solution.py:252
  21.8 3.3 %collective-permute-start.11 = (bf16[16,2560]{1,0:T(8,128)(2,1)S(1)}, bf16[16,2560]{1,0:T(8,128)(2,1)S(1)}, u32[]{:S(2)}, u32[]{:S(2)}) collective-permute-start(bf16[16,2560]{1,0:T(8,128)(2,1)S(1)} %collective-permute-done.3.refs_4_), channel_id=1, source_target_pairs={{0,1},{1,0},{2,3},{3,2},{4,5},{5,4},{6,7},{7,6},{8,9},{9,8},{10,11... | collective-permute-start | bytes 245768 | tf_op jit(solution)/shard_map/ppermute | solution.py:255
  21.8 3.8 %collective-permute-start.13 = (bf16[16,2560]{1,0:T(8,128)(2,1)S(1)}, bf16[16,2560]{1,0:T(8,128)(2,1)S(1)}, u32[]{:S(2)}, u32[]{:S(2)}) collective-permute-start(bf16[16,2560]{1,0:T(8,128)(2,1)S(1)} %collective-permute-done.5.refs_6_), channel_id=1, source_target_pairs={{0,1},{1,0},{2,3},{3,2},{4,5},{5,4},{6,7},{7,6},{8,9},{9,8},{10,11... | collective-permute-start | bytes 245768 | tf_op jit(solution)/shard_map/ppermute | solution.py:255
  22.7 3.0 %collective-permute-start.9 = (bf16[16,2560]{1,0:T(8,128)(2,1)S(1)}, bf16[16,2560]{1,0:T(8,128)(2,1)S(1)}, u32[]{:S(2)}, u32[]{:S(2)}) collective-permute-start(bf16[16,2560]{1,0:T(8,128)(2,1)S(1)} %collective-permute-done.1.refs_2_), channel_id=1, source_target_pairs={{0,1},{1,0},{2,3},{3,2},{4,5},{5,4},{6,7},{7,6},{8,9},{9,8},{10,11... | collective-permute-start | bytes 245768 | tf_op jit(solution)/shard_map/ppermute | solution.py:255
  24.2 2.7 %collective-permute-start.8 = (bf16[16,2560]{1,0:T(8,128)(2,1)S(1)}, bf16[16,2560]{1,0:T(8,128)(2,1)S(1)}, u32[]{:S(2)}, u32[]{:S(2)}) collective-permute-start(bf16[16,2560]{1,0:T(8,128)(2,1)S(1)} %collective-permute-done.refs_1_), channel_id=1, source_target_pairs={{0,1},{1,0},{2,3},{3,2},{4,5},{5,4},{6,7},{7,6},{8,9},{9,8},{10,11... | collective-permute-start | bytes 245768 | tf_op jit(solution)/shard_map/ppermute | solution.py:255
  25.1 1.9 %collective-permute-start.10 = (bf16[16,2560]{1,0:T(8,128)(2,1)S(1)}, bf16[16,2560]{1,0:T(8,128)(2,1)S(1)}, u32[]{:S(2)}, u32[]{:S(2)}) collective-permute-start(bf16[16,2560]{1,0:T(8,128)(2,1)S(1)} %collective-permute-done.2.refs_3_), channel_id=1, source_target_pairs={{0,1},{1,0},{2,3},{3,2},{4,5},{5,4},{6,7},{7,6},{8,9},{9,8},{10,11... | collective-permute-start | bytes 245768 | tf_op jit(solution)/shard_map/ppermute | solution.py:255
  25.1 1.9 %collective-permute-start.12 = (bf16[16,2560]{1,0:T(8,128)(2,1)S(1)}, bf16[16,2560]{1,0:T(8,128)(2,1)S(1)}, u32[]{:S(2)}, u32[]{:S(2)}) collective-permute-start(bf16[16,2560]{1,0:T(8,128)(2,1)S(1)} %collective-permute-done.4.refs_5_), channel_id=1, source_target_pairs={{0,1},{1,0},{2,3},{3,2},{4,5},{5,4},{6,7},{7,6},{8,9},{9,8},{10,11... | collective-permute-start | bytes 245768 | tf_op jit(solution)/shard_map/ppermute | solution.py:255
  25.6 1.4 %collective-permute-start.14 = (bf16[16,2560]{1,0:T(8,128)(2,1)S(1)}, bf16[16,2560]{1,0:T(8,128)(2,1)S(1)}, u32[]{:S(2)}, u32[]{:S(2)}) collective-permute-start(bf16[16,2560]{1,0:T(8,128)(2,1)S(1)} %collective-permute-done.6.refs_7_), channel_id=1, source_target_pairs={{0,1},{1,0},{2,3},{3,2},{4,5},{5,4},{6,7},{7,6},{8,9},{9,8},{10,11... | collective-permute-start | bytes 245768 | tf_op jit(solution)/shard_map/ppermute | solution.py:255
  25.7 15.0 %collective-permute-start.26 = (bf16[4,384,128]{2,1,0:T(8,128)(2,1)S(1)}, bf16[4,384,128]{2,1,0:T(8,128)(2,1)S(1)}, u32[]{:S(2)}, u32[]{:S(2)}) collective-permute-start(bf16[4,384,128]{2,1,0:T(8,128)(2,1)S(1)} %shard_map.127.near), channel_id=1, source_target_pairs={{0,2},{2,0},{4,6},{6,4},{8,10},{10,8},{12,14},{14,12},{1,3},{3,1},... | collective-permute-start | bytes 1179656 | tf_op jit(solution)/shard_map/ppermute | solution.py:252
  27.0 0.9 copy-start.4
  27.9 6.3 %slice-start = ((s8[8847360]{0:T(1024)(128)(4,1)}), s8[4194304]{0:T(1024)(128)(4,1)S(1)}, s32[]{:S(2)}) async-start(s8[8847360]{0:T(1024)(128)(4,1)} %bitcast.15), calls=%async_computation | async-start | bytes 8388608
  28.0 6.2 %slice-start.1 = ((s8[8847360]{0:T(1024)(128)(4,1)}), s8[4194304]{0:T(1024)(128)(4,1)S(1)}, s32[]{:S(2)}) async-start(s8[8847360]{0:T(1024)(128)(4,1)} %bitcast.15), calls=%async_computation.1 | async-start | bytes 8388608
  28.0 6.2 %slice-start.2 = ((s8[8847360]{0:T(1024)(128)(4,1)}), s8[458752]{0:T(1024)(128)(4,1)S(1)}, s32[]{:S(2)}) async-start(s8[8847360]{0:T(1024)(128)(4,1)} %bitcast.15), calls=%async_computation.2 | async-start | bytes 917504
  28.0 8.7 %slice-start.3 = ((s8[8847360]{0:T(1024)(128)(4,1)}), s8[4194304]{0:T(1024)(128)(4,1)S(1)}, s32[]{:S(2)}) async-start(s8[8847360]{0:T(1024)(128)(4,1)} %bitcast.17), calls=%async_computation.3 | async-start | bytes 8388608
  28.0 8.7 %slice-start.4 = ((s8[8847360]{0:T(1024)(128)(4,1)}), s8[4194304]{0:T(1024)(128)(4,1)S(1)}, s32[]{:S(2)}) async-start(s8[8847360]{0:T(1024)(128)(4,1)} %bitcast.17), calls=%async_computation.4 | async-start | bytes 8388608
  34.2 2.5 %slice-start.5 = ((s8[8847360]{0:T(1024)(128)(4,1)}), s8[458752]{0:T(1024)(128)(4,1)S(1)}, s32[]{:S(2)}) async-start(s8[8847360]{0:T(1024)(128)(4,1)} %bitcast.17), calls=%async_computation.5 | async-start | bytes 917504
  36.7 1.6 %copy-start.2 = (bf16[16,64,864]{2,1,0:T(8,128)(2,1)S(1)}, bf16[16,64,864]{2,1,0:T(8,128)(2,1)}, u32[]{:S(2)}) copy-start(bf16[16,64,864]{2,1,0:T(8,128)(2,1)} %adapter_in.1) | copy-start | bytes 5308420
  36.7 1.6 %copy-start.6 = (s32[2]{0:T(128)S(1)}, s32[2]{0:T(128)}, u32[]{:S(2)}) copy-start(s32[2]{0:T(128)} %owner.17) | copy-start | bytes 28
  40.5 23.2 %copy-start.9 = (s32[16]{0:T(128)S(1)}, s32[16]{0:T(128)}, u32[]{:S(2)}) copy-start(s32[16]{0:T(128)} %param.19) | copy-start | bytes 196
  40.5 6.4 %collective-permute-start.15 = (bf16[2624,128]{1,0:T(8,128)(2,1)S(1)}, bf16[2624,128]{1,0:T(8,128)(2,1)S(1)}, u32[]{:S(2)}, u32[]{:S(2)}) collective-permute-start(bf16[2624,128]{1,0:T(8,128)(2,1)S(1)} %get-tuple-element.16), channel_id=1, source_target_pairs={{0,1},{1,0},{2,3},{3,2},{4,5},{5,4},{6,7},{7,6},{8,9},{9,8},{10,11... | collective-permute-start | bytes 2015240 | tf_op jit(solution)/shard_map/ppermute | solution.py:255
  40.8 23.9 %collective-permute-start.27 = (bf16[8,384,128]{2,1,0:T(8,128)(2,1)S(1)}, bf16[8,384,128]{2,1,0:T(8,128)(2,1)S(1)}, u32[]{:S(2)}, u32[]{:S(2)}) collective-permute-start(bf16[8,384,128]{2,1,0:T(8,128)(2,1)S(1)} %shard_map.128.gathered), channel_id=1, source_target_pairs={{0,1},{1,0},{2,3},{3,2},{4,5},{5,4},{6,7},{7,6},{8,9},{9,8},{10,11... | collective-permute-start | bytes 2359304 | tf_op jit(solution)/shard_map/ppermute | solution.py:255
  41.2 7.6 %collective-permute-start.38 = (bf16[864,128]{1,0:T(8,128)(2,1)S(1)}, bf16[864,128]{1,0:T(8,128)(2,1)}, u32[]{:S(2)}, u32[]{:S(2)}) collective-permute-start(bf16[864,128]{1,0:T(8,128)(2,1)S(1)} %multiply_convert_fusion.hidden.refs_0_), channel_id=1, source_target_pairs={{0,2},{2,0},{4,6},{6,4},{8,10},{10,8},{12,14},{14,12},{1,3},{3,1},... | collective-permute-start | bytes 663560 | tf_op jit(solution)/shard_map/ppermute | solution.py:252
  42.3 11.3 %collective-permute-start.17 = (bf16[864,128]{1,0:T(8,128)(2,1)S(1)}, bf16[864,128]{1,0:T(8,128)(2,1)S(1)}, u32[]{:S(2)}, u32[]{:S(2)}) collective-permute-start(bf16[864,128]{1,0:T(8,128)(2,1)S(1)} %multiply_convert_fusion.hidden.refs_0_), channel_id=1, source_target_pairs={{0,4},{2,6},{4,0},{6,2},{8,12},{10,14},{12,8},{14,10},{1,5},{3,7},... | collective-permute-start | bytes 663560 | tf_op jit(solution)/shard_map/ppermute | solution.py:252
  42.8 19.9 %collective-permute-start.18 = (bf16[864,128]{1,0:T(8,128)(2,1)S(1)}, bf16[864,128]{1,0:T(8,128)(2,1)S(1)}, u32[]{:S(2)}, u32[]{:S(2)}) collective-permute-start(bf16[864,128]{1,0:T(8,128)(2,1)S(1)} %multiply_convert_fusion.hidden.refs_0_), channel_id=1, source_target_pairs={{0,8},{2,10},{4,12},{6,14},{8,0},{10,2},{12,4},{14,6},{1,9},{3,11}... | collective-permute-start | bytes 663560 | tf_op jit(solution)/shard_map/ppermute | solution.py:252
  46.9 15.8 %collective-permute-start.19 = (bf16[864,128]{1,0:T(8,128)(2,1)S(1)}, bf16[864,128]{1,0:T(8,128)(2,1)S(1)}, u32[]{:S(2)}, u32[]{:S(2)}) collective-permute-start(bf16[864,128]{1,0:T(8,128)(2,1)S(1)} %multiply_convert_fusion.hidden.refs_0_), channel_id=1, source_target_pairs={{0,12},{2,14},{4,8},{6,10},{8,4},{10,6},{12,0},{14,2},{1,13},{3,15... | collective-permute-start | bytes 663560 | tf_op jit(solution)/shard_map/ppermute | solution.py:252
  46.9 24.1 %copy-start.8 = (s32[2]{0:T(128)S(1)}, s32[2]{0:T(128)}, u32[]{:S(2)}) copy-start(s32[2]{0:T(128)} %length.13) | copy-start | bytes 28
  48.8 15.6 %collective-permute-start.16 = (bf16[1344,128]{1,0:T(8,128)(2,1)S(1)}, bf16[1344,128]{1,0:T(8,128)(2,1)S(1)}, u32[]{:S(2)}, u32[]{:S(2)}) collective-permute-start(bf16[1344,128]{1,0:T(8,128)(2,1)S(1)} %get-tuple-element.18), channel_id=1, source_target_pairs={{0,2},{2,0},{4,6},{6,4},{8,10},{10,8},{12,14},{14,12},{1,3},{3,1},... | collective-permute-start | bytes 1032200 | tf_op jit(solution)/shard_map/ppermute | solution.py:252
  53.6 13.6 %collective-permute-start.37 = (bf16[864,128]{1,0:T(8,128)(2,1)S(1)}, bf16[864,128]{1,0:T(8,128)(2,1)}, u32[]{:S(2)}, u32[]{:S(2)}) collective-permute-start(bf16[864,128]{1,0:T(8,128)(2,1)S(1)} %multiply_convert_fusion.hidden.refs_0_), channel_id=1, source_target_pairs={{0,1},{1,0},{2,3},{3,2},{4,5},{5,4},{6,7},{7,6},{8,9},{9,8},{10,11... | collective-permute-start | bytes 663560 | tf_op jit(solution)/shard_map/ppermute | solution.py:255
  62.7 4.6 %collective-permute-start.39 = (bf16[864,128]{1,0:T(8,128)(2,1)}, bf16[864,128]{1,0:T(8,128)(2,1)}, u32[]{:S(2)}, u32[]{:S(2)}) collective-permute-start(bf16[864,128]{1,0:T(8,128)(2,1)} %collective-permute-done.38.refs_2_), channel_id=1, source_target_pairs={{0,1},{1,0},{2,3},{3,2},{4,5},{5,4},{6,7},{7,6},{8,9},{9,8},{10,11... | collective-permute-start | bytes 663560 | tf_op jit(solution)/shard_map/ppermute | solution.py:255
  62.7 8.3 %collective-permute-start.35 = (bf16[864,128]{1,0:T(8,128)(2,1)S(1)}, bf16[864,128]{1,0:T(8,128)(2,1)}, u32[]{:S(2)}, u32[]{:S(2)}) collective-permute-start(bf16[864,128]{1,0:T(8,128)(2,1)S(1)} %collective-permute-done.17.refs_0_), channel_id=1, source_target_pairs={{0,2},{2,0},{4,6},{6,4},{8,10},{10,8},{12,14},{14,12},{1,3},{3,1},... | collective-permute-start | bytes 663560 | tf_op jit(solution)/shard_map/ppermute | solution.py:252
  64.4 10.5 %collective-permute-start.34 = (bf16[864,128]{1,0:T(8,128)(2,1)S(1)}, bf16[864,128]{1,0:T(8,128)(2,1)S(1)}, u32[]{:S(2)}, u32[]{:S(2)}) collective-permute-start(bf16[864,128]{1,0:T(8,128)(2,1)S(1)} %collective-permute-done.17.refs_0_), channel_id=1, source_target_pairs={{0,1},{1,0},{2,3},{3,2},{4,5},{5,4},{6,7},{7,6},{8,9},{9,8},{10,11... | collective-permute-start | bytes 663560 | tf_op jit(solution)/shard_map/ppermute | solution.py:255
  64.7 10.9 %collective-permute-start.32 = (bf16[864,128]{1,0:T(8,128)(2,1)S(1)}, bf16[864,128]{1,0:T(8,128)(2,1)S(1)}, u32[]{:S(2)}, u32[]{:S(2)}) collective-permute-start(bf16[864,128]{1,0:T(8,128)(2,1)S(1)} %collective-permute-done.18.refs_1_.refs_0_), channel_id=1, source_target_pairs={{0,2},{2,0},{4,6},{6,4},{8,10},{10,8},{12,14},{14,12},{1,3},{3,1},... | collective-permute-start | bytes 663560 | tf_op jit(solution)/shard_map/ppermute | solution.py:252
  67.2 19.6 %collective-permute-start.31 = (bf16[864,128]{1,0:T(8,128)(2,1)S(1)}, bf16[864,128]{1,0:T(8,128)(2,1)S(1)}, u32[]{:S(2)}, u32[]{:S(2)}) collective-permute-start(bf16[864,128]{1,0:T(8,128)(2,1)S(1)} %collective-permute-done.18.refs_1_.refs_0_), channel_id=1, source_target_pairs={{0,1},{1,0},{2,3},{3,2},{4,5},{5,4},{6,7},{7,6},{8,9},{9,8},{10,11... | collective-permute-start | bytes 663560 | tf_op jit(solution)/shard_map/ppermute | solution.py:255
  67.3 12.8 %collective-permute-start.29 = (bf16[864,128]{1,0:T(8,128)(2,1)S(1)}, bf16[864,128]{1,0:T(8,128)(2,1)S(1)}, u32[]{:S(2)}, u32[]{:S(2)}) collective-permute-start(bf16[864,128]{1,0:T(8,128)(2,1)S(1)} %collective-permute-done.19.refs_2_.refs_0_), channel_id=1, source_target_pairs={{0,2},{2,0},{4,6},{6,4},{8,10},{10,8},{12,14},{14,12},{1,3},{3,1},... | collective-permute-start | bytes 663560 | tf_op jit(solution)/shard_map/ppermute | solution.py:252
  71.0 9.0 %collective-permute-start.36 = (bf16[864,128]{1,0:T(8,128)(2,1)}, bf16[864,128]{1,0:T(8,128)(2,1)S(1)}, u32[]{:S(2)}, u32[]{:S(2)}) collective-permute-start(bf16[864,128]{1,0:T(8,128)(2,1)} %collective-permute-done.35.refs_2_), channel_id=1, source_target_pairs={{0,1},{1,0},{2,3},{3,2},{4,5},{5,4},{6,7},{7,6},{8,9},{9,8},{10,11... | collective-permute-start | bytes 663560 | tf_op jit(solution)/shard_map/ppermute | solution.py:255
  74.9 18.0 %collective-permute-start.28 = (bf16[864,128]{1,0:T(8,128)(2,1)S(1)}, bf16[864,128]{1,0:T(8,128)(2,1)S(1)}, u32[]{:S(2)}, u32[]{:S(2)}) collective-permute-start(bf16[864,128]{1,0:T(8,128)(2,1)S(1)} %collective-permute-done.19.refs_2_.refs_0_), channel_id=1, source_target_pairs={{0,1},{1,0},{2,3},{3,2},{4,5},{5,4},{6,7},{7,6},{8,9},{9,8},{10,11... | collective-permute-start | bytes 663560 | tf_op jit(solution)/shard_map/ppermute | solution.py:255
  75.7 12.1 %collective-permute-start.33 = (bf16[864,128]{1,0:T(8,128)(2,1)S(1)}, bf16[864,128]{1,0:T(8,128)(2,1)S(1)}, u32[]{:S(2)}, u32[]{:S(2)}) collective-permute-start(bf16[864,128]{1,0:T(8,128)(2,1)S(1)} %collective-permute-done.32.refs_2_), channel_id=1, source_target_pairs={{0,1},{1,0},{2,3},{3,2},{4,5},{5,4},{6,7},{7,6},{8,9},{9,8},{10,11... | collective-permute-start | bytes 663560 | tf_op jit(solution)/shard_map/ppermute | solution.py:255
  80.0 12.9 %collective-permute-start.30 = (bf16[864,128]{1,0:T(8,128)(2,1)S(1)}, bf16[864,128]{1,0:T(8,128)(2,1)S(1)}, u32[]{:S(2)}, u32[]{:S(2)}) collective-permute-start(bf16[864,128]{1,0:T(8,128)(2,1)S(1)} %collective-permute-done.29.refs_2_), channel_id=1, source_target_pairs={{0,1},{1,0},{2,3},{3,2},{4,5},{5,4},{6,7},{7,6},{8,9},{9,8},{10,11... | collective-permute-start | bytes 663560 | tf_op jit(solution)/shard_map/ppermute | solution.py:255
  80.0 16.6 %collective-permute-start.20 = (bf16[384,128]{1,0:T(8,128)(2,1)S(1)}, bf16[384,128]{1,0:T(8,128)(2,1)S(1)}, u32[]{:S(2)}, u32[]{:S(2)}) collective-permute-start(bf16[384,128]{1,0:T(8,128)(2,1)S(1)} %get-tuple-element.20), channel_id=1, source_target_pairs={{0,4},{2,6},{4,0},{6,2},{8,12},{10,14},{12,8},{14,10},{1,5},{3,7},... | collective-permute-start | bytes 294920 | tf_op jit(solution)/shard_map/ppermute | solution.py:252
  86.8 9.9 %collective-permute-start.21 = (bf16[384,128]{1,0:T(8,128)(2,1)S(1)}, bf16[384,128]{1,0:T(8,128)(2,1)S(1)}, u32[]{:S(2)}, u32[]{:S(2)}) collective-permute-start(bf16[384,128]{1,0:T(8,128)(2,1)S(1)} %get-tuple-element.21), channel_id=1, source_target_pairs={{0,8},{2,10},{4,12},{6,14},{8,0},{10,2},{12,4},{14,6},{1,9},{3,11}... | collective-permute-start | bytes 294920 | tf_op jit(solution)/shard_map/ppermute | solution.py:252
  87.8 8.9 %collective-permute-start.22 = (bf16[384,128]{1,0:T(8,128)(2,1)S(1)}, bf16[384,128]{1,0:T(8,128)(2,1)S(1)}, u32[]{:S(2)}, u32[]{:S(2)}) collective-permute-start(bf16[384,128]{1,0:T(8,128)(2,1)S(1)} %get-tuple-element.22), channel_id=1, source_target_pairs={{0,12},{2,14},{4,8},{6,10},{8,4},{10,6},{12,0},{14,2},{1,13},{3,15... | collective-permute-start | bytes 294920 | tf_op jit(solution)/shard_map/ppermute | solution.py:252
  92.9 3.8 %copy-start.1 = (bf16[16,64,320]{2,1,0:T(8,128)(2,1)S(1)}, bf16[16,64,320]{2,1,0:T(8,128)(2,1)}, u32[]{:S(2)}) copy-start(bf16[16,64,320]{2,1,0:T(8,128)(2,1)} %adapter_out.3) | copy-start | bytes 1966084

commit v3 on v1

--- a/solution.py
+++ b/solution.py
@@ -1,9 +1,396 @@
+import functools
+
 import jax
 import jax.numpy as jnp
 from jax import lax
+from jax.experimental import pallas as pl
+from jax.experimental.pallas import tpu as pltpu
 from jax.sharding import PartitionSpec as P
 
 lowrank_adapter_scale = 2.0
+
+ROWS_BY_ROWS = (((1,), (1,)), ((), ()))
+ASSEMBLE_FLOPS = 0
+GRAD_FLOPS = 20000000000
+FINAL_FLOPS = 20000000000
+ADD_FLOPS = 0
+PAIR_FLOPS = 0
+SPLIT_FLOPS = 0
+IN_VMEM = pl.BlockSpec(memory_space=pltpu.VMEM)
+IN_HBM = pl.BlockSpec(memory_space=pl.ANY)
+IN_SMEM = pl.BlockSpec(memory_space=pltpu.SMEM)
+
+
+def kernel_call(
+    body, out_shape, in_specs, scratch=(), out_specs=None, limit=16, aliases=None, flops=0
+):
+    return pl.pallas_call(
+        body,
+        out_shape=out_shape,
+        in_specs=in_specs,
+        out_specs=jax.tree.map(lambda _: IN_VMEM, out_shape) if out_specs is None else out_specs,
+        scratch_shapes=list(scratch),
+        input_output_aliases=aliases or {},
+        compiler_params=pltpu.CompilerParams(vmem_limit_bytes=limit << 20),
+        cost_estimate=pl.CostEstimate(flops=flops, bytes_accessed=0, transcendentals=0),
+    )
+
+
+class Facts:
+    def __init__(self, ref):
+        self.ref = ref
+        self.blocks = (ref.shape[0] - 3) // 2
+        self.batch, self.core, self.slot_owner = ref[0], ref[1], ref[2]
+
+    def owner(self, block):
+        return self.ref[3 + block]
+
+    def length(self, block):
+        return self.ref[3 + self.blocks + block]
+
+    def lanes(self, token_count):
+        lane = lax.broadcasted_iota(jnp.int32, (1, token_count), 1)
+        size = token_count // self.blocks
+        return lane, size, [(lane >= b * size) & (lane < (b + 1) * size) for b in range(self.blocks)]
+
+    def live(self, token_count):
+        lane, size, blocks = self.lanes(token_count)
+        live = lane < 0
+        for b in range(self.blocks):
+            live = live | (blocks[b] & (lane < b * size + self.length(b)))
+        return live
+
+    def chosen(self, token_count):
+        lane, _, blocks = self.lanes(token_count)
+        chosen = lane < 0
+        for b in range(self.blocks):
+            mine = jnp.where(self.owner(b) == self.slot_owner, token_count, 0)
+            chosen = chosen | (blocks[b] & (lane < mine))
+        return chosen
+
+    def coefficient(self):
+        count = jnp.int32(0)
+        for b in range(self.blocks):
+            count = count + jnp.where(self.owner(b) == self.slot_owner, self.length(b), 0)
+        return lowrank_adapter_scale / jnp.maximum(count, 1).astype(jnp.float32)
+
+
+def prepare_body(owner, length, placement, adapter_out, adapter_in, cot, piece, *refs):
+    facts, cot_and_back, out_blocks, in_blocks, passed, sems = refs
+    passed[...] = piece[...]
+    block_count = owner.shape[0]
+    facts[0], facts[1] = lax.axis_index("batch"), lax.axis_index("tensor")
+    facts[2] = placement[lax.axis_index("batch") * 2 + lax.axis_index("tensor")]
+    for b in range(block_count):
+        facts[3 + b] = owner[b]
+        facts[3 + block_count + b] = length[b]
+    facts = Facts(facts)
+    copies = []
+    for b in range(facts.blocks):
+        for i, (source, target) in enumerate(((adapter_out, out_blocks), (adapter_in, in_blocks))):
+            copies.append(
+                pltpu.make_async_copy(source.at[facts.owner(b)], target.at[b], sems.at[i, b])
+            )
+    for copy in copies:
+        copy.start()
+    columns, token_count = cot.shape
+    for b in range(cot_and_back.shape[0]):
+        cot_and_back[b, :columns] = cot[...]
+    for copy in copies:
+        copy.wait()
+    _, _, blocks = facts.lanes(token_count)
+    total = jnp.zeros((out_blocks.shape[1], token_count), jnp.float32)
+    for b in range(facts.blocks):
+        every = jnp.dot(out_blocks[b], cot[...], preferred_element_type=jnp.float32)
+        total = jnp.where(blocks[b], every, total)
+    total = jnp.where(facts.live(token_count), total, 0.0)
+    for b in range(cot_and_back.shape[0]):
+        cot_and_back[b, columns:] = total.astype(cot_and_back.dtype)
+
+
+def run_copies(pairs, sems):
+    copies = [
+        pltpu.make_async_copy(source, target, sems.at[i])
+        for i, (source, target) in enumerate(pairs)
+    ]
+    for copy in copies:
+        copy.start()
+    for copy in copies:
+        copy.wait()
+
+
+def assemble_body(facts, *refs):
+    facts, pieces, out = Facts(facts), refs[:-1], refs[-1]
+    count = len(pieces) // 2
+    rows, half = pieces[0].shape
+    for i, piece in enumerate(pieces):
+        row = pl.multiple_of((facts.batch ^ (i % count)) * rows, rows)
+        core = facts.core if i < count else 1 - facts.core
+        out[pl.ds(row, rows), pl.ds(pl.multiple_of(core * half, 128), half)] = piece[...]
+
+
+def split_body(facts, base, hidden, in_blocks, *refs):
+    facts, kept, leaving = Facts(facts), refs[-2], refs[-1]
+    token_count = base.shape[0]
+    rank = in_blocks.shape[1]
+    columns = (kept.shape[0] - rank) // 8
+    for b in range(8):
+        both = base[:, b * 2 * columns : (b + 1) * 2 * columns].astype(jnp.float32).T
+        both = both.astype(kept.dtype)
+        here = pl.ds(b * columns, columns)
+
+        @pl.when(facts.core == 0)
+        def _():
+            kept[here] = both[:columns]
+            leaving[here] = both[columns:]
+
+        @pl.when(facts.core != 0)
+        def _():
+            kept[here] = both[columns:]
+            leaving[here] = both[:columns]
+
+    _, _, blocks = facts.lanes(token_count)
+    low = jnp.zeros((rank, token_count), jnp.float32)
+    for b in range(facts.blocks):
+        every = jnp.dot(in_blocks[b], hidden[...], preferred_element_type=jnp.float32)
+        low = jnp.where(blocks[b], every, low)
+    tail = pl.ds(8 * columns, rank)
+    kept[tail] = low.astype(kept.dtype)
+    leaving[tail] = low.astype(kept.dtype)
+
+
+def add_body(facts, kept, arrived, own, leaving):
+    rank = own.shape[0] - (kept.shape[0] - own.shape[0])
+    columns = (own.shape[0] - rank) // 4
+    side = Facts(facts).batch % 2
+
+    def added(first, count):
+        here = pl.ds(first, count)
+        total = kept[here].astype(jnp.float32) + arrived[here].astype(jnp.float32)
+        return total.astype(own.dtype)
+
+    for z in range(4):
+        here = pl.ds(z * columns, columns)
+        own[here] = added(pl.multiple_of((2 * z + side) * columns, 16), columns)
+        leaving[here] = added(pl.multiple_of((2 * z + 1 - side) * columns, 16), columns)
+    low = added(8 * columns, rank)
+    own[4 * columns :] = low
+    leaving[4 * columns :] = low
+
+
+def add_pair_body(facts, own, arrived, *refs):
+    outs = refs[-4:]
+    columns = (own.shape[0] - outs[0].shape[0]) // 3
+    place = Facts(facts).batch // 2
+
+    def added(first, count):
+        here = pl.ds(first, count)
+        total = own[here].astype(jnp.float32) + arrived[here].astype(jnp.float32)
+        return total.astype(own.dtype)
+
+    low = added(4 * columns, own.shape[0] - 4 * columns)
+    for flip, out in enumerate(outs):
+        out[:columns] = added(pl.multiple_of((place ^ flip) * columns, 16), columns)
+        out[columns:] = low
+
+
+def final_body(facts, out_blocks, gathered, gathered_other, *refs):
+    facts, arrived, (mixed, grad, ranked, features) = Facts(facts), refs[:-4], refs[-4:]
+    columns, token_count = mixed.shape
+    total = arrived[0][...].astype(jnp.float32)
+    for share in arrived[1:]:
+        total = total + share[...].astype(jnp.float32)
+    low = total[columns:]
+    _, _, blocks = facts.lanes(token_count)
+    contribution = jnp.zeros(mixed.shape, jnp.float32)
+    for b in range(facts.blocks):
+        every = lax.dot_general(
+            out_blocks[b],
+            low.astype(jnp.bfloat16),
+            (((0,), (0,)), ((), ())),
+            preferred_element_type=jnp.float32,
+        )
+        contribution = jnp.where(blocks[b], every, contribution)
+    mixed[...] = (total[:columns] + lowrank_adapter_scale * contribution).astype(mixed.dtype)
+    chosen = facts.chosen(token_count) & facts.live(token_count)
+    ranked[...] = jnp.where(chosen, low, 0.0).astype(ranked.dtype)
+    for half, pieces in ((facts.core, gathered), (1 - facts.core, gathered_other)):
+        for b in range(pieces.shape[0]):
+            here = pl.ds(pl.multiple_of((2 * b + half) * columns, 16), columns)
+            features[here] = pieces[b, :columns]
+    total = lax.dot_general(
+        ranked[...], features[...], ROWS_BY_ROWS, preferred_element_type=jnp.float32
+    )
+    grad[0] = (facts.coefficient() * total).astype(grad.dtype)
+
+
+def pass_body(*refs):
+    pass
+
+
+def back_body(facts, gathered, gathered_other, ranked):
+    back = jnp.zeros(ranked.shape, jnp.float32)
+    first = gathered.shape[1] - ranked.shape[0]
+    for pieces in (gathered, gathered_other):
+        for b in range(pieces.shape[0]):
+            back = back + pieces[b, first:].astype(jnp.float32)
+    chosen = Facts(facts).chosen(ranked.shape[1])
+    ranked[...] = jnp.where(chosen, back, 0.0).astype(ranked.dtype)
+
+
+def in_grad_body(facts, ranked, *refs, flips):
+    pieces, (out, features, result, sems) = refs[:8], refs[-4:]
+    facts = Facts(facts)
+    rows = pieces[0].shape[0]
+    side = facts.batch % 2
+    factor = facts.coefficient()
+    leaving = []
+    for i, flip in enumerate(flips):
+        for j in range(4):
+            y = side if j < 2 else 1 - side
+            core = facts.core if j % 2 == 0 else 1 - facts.core
+            here = pl.ds(pl.multiple_of((y * 2 + core) * rows, 16), rows)
+            features[i, here] = pieces[4 * i + j][...]
+        total = lax.dot_general(
+            ranked[...], features[i], ROWS_BY_ROWS, preferred_element_type=jnp.float32
+        )
+        result[i] = (factor * total).astype(result.dtype)
+        columns = 4 * rows
+        first = ((facts.batch ^ flip) // 2) * columns
+        target = out.at[0, :, pl.ds(pl.multiple_of(first, 128), columns)]
+        leaving.append(pltpu.make_async_copy(result.at[i], target, sems.at[i]))
+        leaving[-1].start()
+    for copy in leaving:
+        copy.wait()
+
+
+def on_chips(
+    tokens,
+    gate_weight,
+    up_weight,
+    down_weight,
+    adapter_in,
+    adapter_out,
+    cotangent,
+    block_owner,
+    block_length,
+    placement,
+):
+    f32, bf16 = jnp.float32, jnp.bfloat16
+    width = gate_weight.shape[1]
+    model_width = gate_weight.shape[0]
+    token_count, columns = cotangent.shape
+    rank = adapter_in.shape[1]
+    block_count = block_owner.shape[0]
+    def array(*shape):
+        return jax.ShapeDtypeStruct(shape, bf16)
+
+    def flip(piece, k):
+        return lax.ppermute(piece, "batch", [(i, i ^ k) for i in range(8)])
+
+    def to_other_core(piece):
+        return lax.ppermute(piece, "tensor", [(0, 1), (1, 0)])
+
+    def along_z(piece):
+        return {0: piece, **{k: flip(piece, k) for k in (2, 4, 6)}}
+
+    def then_along_y(line):
+        return [line[k] if k in line else flip(line[k ^ 1], 1) for k in range(8)]
+
+    line = along_z(tokens)
+    facts, cot_and_back, out_blocks, in_blocks, line[2] = kernel_call(
+        prepare_body,
+        [
+            jax.ShapeDtypeStruct((3 + 2 * block_count,), jnp.int32),
+            array(8, columns + rank, token_count),
+            array(block_count, rank, columns),
+            array(block_count, rank, width),
+            array(*tokens.shape),
+        ],
+        [IN_SMEM] * 3 + [IN_HBM, IN_HBM, IN_VMEM, IN_VMEM],
+        out_specs=[IN_SMEM] + [IN_VMEM] * 4,
+        scratch=[pltpu.SemaphoreType.DMA((2, block_count))],
+        limit=56,
+    )(block_owner, block_length, placement, adapter_out, adapter_in, cotangent.T, line[2])
+    own = then_along_y(line)
+    other = [to_other_core(piece) for piece in own]
+    gathered = lax.all_to_all(
+        cot_and_back, "batch", split_axis=0, concat_axis=0, tiled=True
+    )
+    rows = kernel_call(
+        assemble_body,
+        array(token_count, model_width),
+        [IN_SMEM] + [IN_VMEM] * 16,
+        flops=ASSEMBLE_FLOPS,
+    )(facts, *own, *other)
+    gate_value = lax.dot_general(gate_weight.T, rows, ROWS_BY_ROWS, preferred_element_type=f32)
+    up_value = lax.dot_general(up_weight.T, rows, ROWS_BY_ROWS, preferred_element_type=f32)
+    hidden = (jax.nn.silu(gate_value) * up_value).astype(bf16)
+    base_part = lax.dot_general(
+        hidden, down_weight, (((0,), (0,)), ((), ())), preferred_element_type=f32
+    ).astype(bf16)
+    kept, leaving = kernel_call(
+        split_body,
+        [array(8 * columns + rank, token_count)] * 2,
+        [IN_SMEM] + [IN_VMEM] * 3,
+        flops=SPLIT_FLOPS,
+    )(facts, base_part, hidden, in_blocks)
+    stays, leaving = kernel_call(
+        add_body,
+        [array(4 * columns + rank, token_count)] * 2,
+        [IN_SMEM] + [IN_VMEM] * 2,
+        flops=ADD_FLOPS,
+    )(facts, kept, to_other_core(leaving))
+    line = along_z(hidden)
+    gathered = kernel_call(
+        pass_body,
+        array(8, columns + rank, token_count),
+        [IN_HBM] * 2,
+        out_specs=IN_HBM,
+        aliases={0: 0},
+    )(gathered, stays)
+    gathered_other = to_other_core(gathered)
+    hidden_own = then_along_y(line)
+    hidden_other = [to_other_core(piece) for piece in hidden_own]
+    shares = kernel_call(
+        add_pair_body,
+        [array(columns + rank, token_count)] * 4,
+        [IN_SMEM] + [IN_VMEM] * 2 + [IN_HBM] * 3,
+        flops=PAIR_FLOPS,
+    )(facts, stays, flip(leaving, 1), *[line[k] for k in (2, 4, 6)])
+    shares = [shares[0]] + [flip(shares[z], 2 * z) for z in (1, 2, 3)]
+    mixed, grad_out, low_chosen = kernel_call(
+        final_body,
+        [array(columns, token_count), array(1, rank, model_width), array(rank, token_count)],
+        [IN_SMEM] + [IN_VMEM] * 7,
+        scratch=[pltpu.VMEM((model_width, token_count), bf16)],
+        flops=FINAL_FLOPS,
+    )(facts, out_blocks, gathered, gathered_other, *shares)
+    back_chosen = kernel_call(back_body, array(rank, token_count), [IN_SMEM] + [IN_VMEM] * 2)(
+        facts, gathered, gathered_other
+    )
+    grad_in = None
+    for flips in ((0, 2), (4, 6)):
+        order = [p for k in flips for p in (k, k ^ 1)]
+        pieces = [p for k in order for p in (hidden_own[k], hidden_other[k])]
+        if grad_in is None:
+            last, aliases = [], {}
+        else:
+            last, aliases = [grad_in, low_chosen], {10: 0}
+        grad_in = kernel_call(
+            functools.partial(in_grad_body, flips=flips),
+            array(1, rank, 16 * width),
+            [IN_SMEM] + [IN_VMEM] * 9 + [IN_HBM] * len(last),
+            scratch=[
+                pltpu.VMEM((2, 4 * width, token_count), bf16),
+                pltpu.VMEM((2, rank, 4 * width), bf16),
+                pltpu.SemaphoreType.DMA((2,)),
+            ],
+            out_specs=IN_HBM,
+            aliases=aliases,
+            flops=GRAD_FLOPS,
+        )(facts, back_chosen, *pieces, *last)
+    return mixed.T, grad_in, grad_out
 
 
 def partner_shifts(count):
@@ -45,7 +432,7 @@
     return jnp.stack([jnp.where(mine_first, piece, other), jnp.where(mine_first, other, piece)])
 
 
-def on_device(
+def on_any_mesh(
     tokens,
     gate_weight,
     up_weight,
@@ -164,6 +551,9 @@
         P("groups"),
         P("groups"),
     )
+    on_device = on_any_mesh
+    if mesh.shape["batch"] == 8 and mesh.shape["tensor"] == 2:
+        on_device = on_chips
     return jax.shard_map(
         on_device,
         mesh=mesh,

time: 136 us -> 89.9 us (0.66)
  starting transfers between devices: 56.1 us -> 32 us
  local copies, waits for them, and re-layouts: 23.9 us -> 2.19 us
  Pallas kernels: 0 us -> 13.9 us
  other arithmetic: 6.76 us -> 0.01 us
  matrix products: 16 us -> 10.3 us
  waiting for transfers between devices: 30.8 us -> 28.8 us
    ppermute x33 -> x36, starting transfers between devices: 56.1 us -> 27 us  [the longest x18 24.3 us: flip(): return lax.ppermute(piece, 'batch', [(i, i ^ k) for i in range(8)])]
    dynamic_update_slice x23 -> x0, local copies, waits for them, and re-layouts: 14.7 us -> none  [the longest x21 13.2 us: gather_pieces(): whole = lax.dynamic_update_index_in_dim(whole, arrived, me ^ k, 0)]
    pallas_call x0 -> x10, Pallas kernels: none -> 13.9 us  [the longest x2 4.19 us: on_chips(): kernel_call(functools.partial(in_grad_body, flips=flips), array(1, rank,...]
    dot_general x8 -> x3, matrix products: 16 us -> 10.3 us  [the longest x1 6.3 us: on_chips(): lax.dot_general(gate_weight.T, rows, ROWS_BY_ROWS, preferred_element_type...]
    all_to_all x0 -> x1, starting transfers between devices: none -> 4.97 us  [on_chips(): lax.all_to_all(cot_and_back, 'batch', split_axis=0, concat_axis=0, tiled=...]
    ppermute x33 -> x36, waiting for transfers between devices: 30.8 us -> 26 us  [the longest x18 23.9 us: flip(): return lax.ppermute(piece, 'batch', [(i, i ^ k) for i in range(8)])]
    another operation x5 -> x0, other arithmetic: 3.66 us -> none  [the longest x4 3.53 us: pair_gather(): jnp.stack([jnp.where(mine_first, piece, other), jnp.where(mine_first, oth...]
    all_to_all x0 -> x1, waiting for transfers between devices: none -> 2.75 us  [on_chips(): lax.all_to_all(cot_and_back, 'batch', split_axis=0, concat_axis=0, tiled=...]
  transfers between devices with their start and end apart: 33 -> 37, of which waited for: 9 -> 10; matrix products, arithmetic and copies ran while one was open for 31% -> 12% of each run, Pallas kernels for 0% -> 13%
where the time goes in v3:
time: 89.9 us; the launch traced here: 88.1 us
  starting transfers between devices  32 us (36%)
  waiting for transfers between devices  28.8 us (32%)
  Pallas kernels  13.9 us (15%)
  matrix products  10.3 us (11%)
  local copies, waits for them, and re-layouts  2.19 us (2%)
  between operations  0.98 us (1%)
    ppermute x18, starting transfers between devices, flip(): return lax.ppermute(piece, 'batch', [(i, i ^ k) for i in range(8)])  24.3 us
    ppermute x18, waiting for transfers between devices, flip(): return lax.ppermute(piece, 'batch', [(i, i ^ k) for i in range(8)])  23.9 us
    dot_general x1, matrix products, on_chips(): lax.dot_general(gate_weight.T, rows, ROWS_BY_ROWS, preferred_element_type...  6.3 us
    all_to_all x1, starting transfers between devices, on_chips(): lax.all_to_all(cot_and_back, 'batch', split_axis=0, concat_axis=0, tiled=...  4.97 us
    pallas_call x2, Pallas kernels, on_chips(): kernel_call(functools.partial(in_grad_body, flips=flips), array(1, rank,...  4.19 us
    pallas_call x1, Pallas kernels, on_chips(): kernel_call(prepare_body, [jax.ShapeDtypeStruct((3 + 2 * block_count,), j...  3.06 us
    all_to_all x1, waiting for transfers between devices, on_chips(): lax.all_to_all(cot_and_back, 'batch', split_axis=0, concat_axis=0, tiled=...  2.75 us
    ppermute x18, starting transfers between devices, to_other_core(): return lax.ppermute(piece, 'tensor', [(0, 1), (1, 0)])  2.71 us
  transfers between devices with their start and end apart: 37, of which 10 were waited for; matrix products, arithmetic and copies ran while one was open for 12% of the time, Pallas kernels for 13%

profile of v3, /device:TPU:2, one launch (start us, length us, event | category | flops | bytes accessed | tf_op | source)
XLA Modules:
  0.0 88.1 jit_solution(7482163413181318569)
XLA Ops:
  0.6 1.6 %collective-permute-start = (bf16[16,2560]{1,0:T(8,128)(2,1)}, bf16[16,2560]{1,0:T(8,128)(2,1)S(1)}, u32[]{:S(2)}, u32[]{:S(2)}) collective-permute-start(bf16[16,2560]{1,0:T(8,128)(2,1)} %refs_0_.1), channel_id=1, source_target_pairs={{0,4},{2,6},{4,0},{6,2},{8,12},{10,14},{12,8},{14,10},{1,5},{3,7},... | collective-permute-start | bytes 245768 | tf_op jit(solution)/shard_map/ppermute | solution.py:289
  2.3 2.6 %collective-permute-start.3 = (bf16[16,2560]{1,0:T(8,128)(2,1)}, bf16[16,2560]{1,0:T(8,128)(2,1)S(1)}, u32[]{:S(2)}, u32[]{:S(2)}) collective-permute-start(bf16[16,2560]{1,0:T(8,128)(2,1)} %refs_0_.1), channel_id=1, source_target_pairs={{0,8},{2,10},{4,12},{6,14},{8,0},{10,2},{12,4},{14,6},{1,9},{3,11}... | collective-permute-start | bytes 245768 | tf_op jit(solution)/shard_map/ppermute | solution.py:289
  4.9 0.2 collective-permute-start.5
  5.1 1.5 %collective-permute-start.1 = (bf16[16,2560]{1,0:T(8,128)(2,1)}, bf16[16,2560]{1,0:T(8,128)(2,1)S(1)}, u32[]{:S(2)}, u32[]{:S(2)}) collective-permute-start(bf16[16,2560]{1,0:T(8,128)(2,1)} %refs_0_.1), channel_id=1, source_target_pairs={{0,2},{2,0},{4,6},{6,4},{8,10},{10,8},{12,14},{14,12},{1,3},{3,1},... | collective-permute-start | bytes 245768 | tf_op jit(solution)/shard_map/ppermute | solution.py:289
  6.6 0.6 copy-done.6
  7.3 3.1 %shard_map.121 = (s32[7]{0:T(128)}, bf16[8,384,128]{2,1,0:T(8,128)(2,1)}, bf16[2,64,320]{2,1,0:T(8,128)(2,1)}, bf16[2,64,864]{2,1,0:T(8,128)(2,1)}, bf16[16,2560]{1,0:T(8,128)(2,1)}) custom-call(s32[2]{0:T(128)} %owner.1, s32[2]{0:T(128)} %length.1, s32[16]{0:T(128)} %placement.1, bf16[16,64,320]{2,1,0:T(8,128)(2,1)} %adapter_out.1, ...), custom_call_target="tpu_custom_call" | custom-call | tf_op jit(solution)/shard_map/pallas_call | solution.py:301
  10.3 0.6 collective-permute-start.2
  10.9 0.8 collective-permute-done.3.refs_4_
  11.7 0.0 collective-permute-start.9
  11.7 0.0 collective-permute-done.5.refs_6_
  11.7 1.5 %collective-permute-start.4 = (bf16[16,2560]{1,0:T(8,128)(2,1)S(1)}, bf16[16,2560]{1,0:T(8,128)(2,1)S(1)}, u32[]{:S(2)}, u32[]{:S(2)}) collective-permute-start(bf16[16,2560]{1,0:T(8,128)(2,1)S(1)} %collective-permute-done.3.refs_4_), channel_id=1, source_target_pairs={{0,2},{2,0},{4,6},{6,4},{8,10},{10,8},{12,14},{14,12},{1,3},{3,1},... | collective-permute-start | bytes 245768 | tf_op jit(solution)/shard_map/ppermute | solution.py:289
  13.2 0.0 collective-permute-done.1.refs_1_
  13.2 0.5 collective-permute-start.6
  13.7 0.0 collective-permute-done.7.refs_8_
  13.7 0.0 collective-permute-start.11
  13.7 2.1 %collective-permute-done.2.refs_3_ = bf16[16,2560]{1,0:T(8,128)(2,1)S(1)} collective-permute-done((bf16[16,2560]{1,0:T(8,128)(2,1)}, bf16[16,2560]{1,0:T(8,128)(2,1)S(1)}, u32[]{:S(2)}, u32[]{:S(2)}) %collective-permute-start.2) | collective-permute-done | bytes 81952 | tf_op jit(solution)/shard_map/ppermute | solution.py:289
  15.9 0.5 collective-permute-start.8
  16.4 1.2 %collective-permute-done.4.refs_5_ = bf16[16,2560]{1,0:T(8,128)(2,1)S(1)} collective-permute-done((bf16[16,2560]{1,0:T(8,128)(2,1)S(1)}, bf16[16,2560]{1,0:T(8,128)(2,1)S(1)}, u32[]{:S(2)}, u32[]{:S(2)}) %collective-permute-start.4) | collective-permute-done | bytes 81952 | tf_op jit(solution)/shard_map/ppermute | solution.py:289
  17.6 0.0 collective-permute-start.10
  17.6 1.4 %collective-permute-done.6.refs_7_ = bf16[16,2560]{1,0:T(8,128)(2,1)S(1)} collective-permute-done((bf16[16,2560]{1,0:T(8,128)(2,1)S(1)}, bf16[16,2560]{1,0:T(8,128)(2,1)S(1)}, u32[]{:S(2)}, u32[]{:S(2)}) %collective-permute-start.6) | collective-permute-done | bytes 81952 | tf_op jit(solution)/shard_map/ppermute | solution.py:289
  19.0 0.5 collective-permute-start.14
  19.5 5.0 %all-to-all-start = ((bf16[8,384,128]{2,1,0:T(8,128)(2,1)}), bf16[8,384,128]{2,1,0:T(8,128)(2,1)S(1)}, u32[]{:S(2)}, u32[]{:S(2)}) async-start(bf16[8,384,128]{2,1,0:T(8,128)(2,1)} %get-tuple-element.21), calls=%async_computation | async-start | bytes 1572864 | tf_op jit(solution)/shard_map/all_to_all | solution.py:317
  24.5 0.0 collective-permute-done.8.refs_9_
  24.5 0.9 copy-done.2
  25.4 0.6 copy-done.3
  26.0 0.6 shard_map.122
  26.7 0.0 slice-start.1
  26.7 0.0 slice-start.3
  26.7 0.0 slice-start.4
  26.7 6.3 %convolution_bitcast_fusion.1 = f32[864,128]{1,0:T(8,128)S(1)} fusion(bf16[128,5120]{1,0:T(8,128)(2,1)S(1)} %shard_map.122, bf16[5120,864]{0,1:T(8,128)(2,1)} %param.11), kind=kOutput, calls=%fused_computation.2 | convolution fusion | flops 1132462080 | bytes 10600448 | tf_op jit(solution)/shard_map/dot_general | solution.py:326
  33.1 0.0 slice-start.5
  33.1 2.5 %multiply_convert_fusion.hidden.refs_0_ = bf16[864,128]{1,0:T(8,128)(2,1)S(1)} fusion(f32[864,128]{1,0:T(8,128)S(1)} %convolution_bitcast_fusion.1, bf16[128,5120]{1,0:T(8,128)(2,1)S(1)} %shard_map.122, bf16[5120,864]{0,1:T(8,128)(2,1)S(1)} %bitcast.13), kind=kOutput, calls=%fused_computation.3 | convolution fusion | flops 1133125632 | bytes 10821632 | tf_op jit(solution)/shard_map/dot_general | solution.py:327
  35.6 0.0 copy-start
  35.6 1.6 %convolution_convert_fusion.base = bf16[128,5120]{1,0:T(8,128)(2,1)S(1)} fusion(bf16[864,128]{1,0:T(8,128)(2,1)S(1)} %multiply_convert_fusion.hidden.refs_0_, bf16[864,5120]{1,0:T(8,128)(2,1)S(1)} %bitcast.15), kind=kOutput, calls=%fused_computation | convolution fusion | flops 1133117440 | bytes 10379264 | tf_op jit(solution)/shard_map/dot_general | solution.py:329
  37.2 2.0 %shard_map.123 = (bf16[2624,128]{1,0:T(8,128)(2,1)S(1)}, bf16[2624,128]{1,0:T(8,128)(2,1)S(1)}) custom-call(s32[7]{0:T(128)S(1)} %copy-done.4, bf16[128,5120]{1,0:T(8,128)(2,1)S(1)} %convolution_convert_fusion.base, bf16[864,128]{1,0:T(8,128)(2,1)S(1)} %multiply_convert_fusion.hidden.refs_0_, bf16[2,64,864]{2,1,0:T(8,128)(2,1)S(1)} %copy-done), custom_call_target="tpu_custom_call" | custom-call | tf_op jit(solution)/shard_map/pallas_call | solution.py:332
  39.2 0.1 collective-permute-start.15
  39.3 2.1 %collective-permute-done.15.arrived = bf16[2624,128]{1,0:T(8,128)(2,1)S(1)} collective-permute-done((bf16[2624,128]{1,0:T(8,128)(2,1)S(1)}, bf16[2624,128]{1,0:T(8,128)(2,1)S(1)}, u32[]{:S(2)}, u32[]{:S(2)}) %collective-permute-start.15) | collective-permute-done | bytes 671776 | tf_op jit(solution)/shard_map/ppermute | solution.py:292
  41.4 0.7 shard_map.124
  42.1 2.7 %all-to-all-done.refs_0_ = bf16[8,384,128]{2,1,0:T(8,128)(2,1)S(1)} async-done(((bf16[8,384,128]{2,1,0:T(8,128)(2,1)}), bf16[8,384,128]{2,1,0:T(8,128)(2,1)S(1)}, u32[]{:S(2)}, u32[]{:S(2)}) %all-to-all-start) | async-done | bytes 786464 | tf_op jit(solution)/shard_map/all_to_all | solution.py:317
  44.8 0.3 collective-permute-start.18
  45.1 1.1 %collective-permute-start.31 = (bf16[864,128]{1,0:T(8,128)(2,1)S(1)}, bf16[864,128]{1,0:T(8,128)(2,1)S(1)}, u32[]{:S(2)}, u32[]{:S(2)}) collective-permute-start(bf16[864,128]{1,0:T(8,128)(2,1)S(1)} %multiply_convert_fusion.hidden.refs_0_), channel_id=1, source_target_pairs={{0,2},{2,0},{4,6},{6,4},{8,10},{10,8},{12,14},{14,12},{1,3},{3,1},... | collective-permute-start | bytes 663560 | tf_op jit(solution)/shard_map/ppermute | solution.py:289
  46.3 0.9 %collective-permute-start.17 = (bf16[1344,128]{1,0:T(8,128)(2,1)S(1)}, bf16[1344,128]{1,0:T(8,128)(2,1)S(1)}, u32[]{:S(2)}, u32[]{:S(2)}) collective-permute-start(bf16[1344,128]{1,0:T(8,128)(2,1)S(1)} %get-tuple-element.27), channel_id=1, source_target_pairs={{0,2},{2,0},{4,6},{6,4},{8,10},{10,8},{12,14},{14,12},{1,3},{3,1},... | collective-permute-start | bytes 1032200 | tf_op jit(solution)/shard_map/ppermute | solution.py:289
  47.1 1.6 %collective-permute-start.19 = (bf16[864,128]{1,0:T(8,128)(2,1)S(1)}, bf16[864,128]{1,0:T(8,128)(2,1)S(1)}, u32[]{:S(2)}, u32[]{:S(2)}) collective-permute-start(bf16[864,128]{1,0:T(8,128)(2,1)S(1)} %multiply_convert_fusion.hidden.refs_0_), channel_id=1, source_target_pairs={{0,8},{2,10},{4,12},{6,14},{8,0},{10,2},{12,4},{14,6},{1,9},{3,11}... | collective-permute-start | bytes 663560 | tf_op jit(solution)/shard_map/ppermute | solution.py:289
  48.7 6.0 %collective-permute-done.18.refs_0_.refs_4_ = bf16[864,128]{1,0:T(8,128)(2,1)S(1)} collective-permute-done((bf16[864,128]{1,0:T(8,128)(2,1)S(1)}, bf16[864,128]{1,0:T(8,128)(2,1)S(1)}, u32[]{:S(2)}, u32[]{:S(2)}) %collective-permute-start.18) | collective-permute-done | bytes 221216 | tf_op jit(solution)/shard_map/ppermute | solution.py:289
  54.8 2.1 %collective-permute-start.20 = (bf16[864,128]{1,0:T(8,128)(2,1)S(1)}, bf16[864,128]{1,0:T(8,128)(2,1)S(1)}, u32[]{:S(2)}, u32[]{:S(2)}) collective-permute-start(bf16[864,128]{1,0:T(8,128)(2,1)S(1)} %multiply_convert_fusion.hidden.refs_0_), channel_id=1, source_target_pairs={{0,12},{2,14},{4,8},{6,10},{8,4},{10,6},{12,0},{14,2},{1,13},{3,15... | collective-permute-start | bytes 663560 | tf_op jit(solution)/shard_map/ppermute | solution.py:289
  56.9 1.6 %collective-permute-start.34 = (bf16[864,128]{1,0:T(8,128)(2,1)S(1)}, bf16[864,128]{1,0:T(8,128)(2,1)S(1)}, u32[]{:S(2)}, u32[]{:S(2)}) collective-permute-start(bf16[864,128]{1,0:T(8,128)(2,1)S(1)} %collective-permute-done.18.refs_0_.refs_4_), channel_id=1, source_target_pairs={{0,2},{2,0},{4,6},{6,4},{8,10},{10,8},{12,14},{14,12},{1,3},{3,1},... | collective-permute-start | bytes 663560 | tf_op jit(solution)/shard_map/ppermute | solution.py:289
  58.5 7.4 %collective-permute-done.19.refs_1_.refs_0_ = bf16[864,128]{1,0:T(8,128)(2,1)S(1)} collective-permute-done((bf16[864,128]{1,0:T(8,128)(2,1)S(1)}, bf16[864,128]{1,0:T(8,128)(2,1)S(1)}, u32[]{:S(2)}, u32[]{:S(2)}) %collective-permute-start.19) | collective-permute-done | bytes 221216 | tf_op jit(solution)/shard_map/ppermute | solution.py:289
  65.9 0.5 collective-permute-start.32
  66.4 0.1 collective-permute-start.33
  66.5 0.4 collective-permute-start.35
  66.9 0.6 shard_map.126
  67.5 1.2 %collective-permute-start.25 = (bf16[864,128]{1,0:T(8,128)(2,1)S(1)}, bf16[864,128]{1,0:T(8,128)(2,1)S(1)}, u32[]{:S(2)}, u32[]{:S(2)}) collective-permute-start(bf16[864,128]{1,0:T(8,128)(2,1)S(1)} %collective-permute-done.19.refs_1_.refs_0_), channel_id=1, source_target_pairs={{0,2},{2,0},{4,6},{6,4},{8,10},{10,8},{12,14},{14,12},{1,3},{3,1},... | collective-permute-start | bytes 663560 | tf_op jit(solution)/shard_map/ppermute | solution.py:289
  68.7 0.6 shard_map.128.ranked
  69.3 1.0 %collective-permute-start.28 = (bf16[864,128]{1,0:T(8,128)(2,1)S(1)}, bf16[864,128]{1,0:T(8,128)(2,1)S(1)}, u32[]{:S(2)}, u32[]{:S(2)}) collective-permute-start(bf16[864,128]{1,0:T(8,128)(2,1)S(1)} %collective-permute-done.20.refs_2_.refs_4_), channel_id=1, source_target_pairs={{0,2},{2,0},{4,6},{6,4},{8,10},{10,8},{12,14},{14,12},{1,3},{3,1},... | collective-permute-start | bytes 663560 | tf_op jit(solution)/shard_map/ppermute | solution.py:289
  70.3 3.6 %collective-permute-start.21 = (bf16[384,128]{1,0:T(8,128)(2,1)S(1)}, bf16[384,128]{1,0:T(8,128)(2,1)S(1)}, u32[]{:S(2)}, u32[]{:S(2)}) collective-permute-start(bf16[384,128]{1,0:T(8,128)(2,1)S(1)} %get-tuple-element.29), channel_id=1, source_target_pairs={{0,4},{2,6},{4,0},{6,2},{8,12},{10,14},{12,8},{14,10},{1,5},{3,7},... | collective-permute-start | bytes 294920 | tf_op jit(solution)/shard_map/ppermute | solution.py:289
  73.9 0.1 collective-permute-start.22
  73.9 2.4 %collective-permute-start.23 = (bf16[384,128]{1,0:T(8,128)(2,1)S(1)}, bf16[384,128]{1,0:T(8,128)(2,1)S(1)}, u32[]{:S(2)}, u32[]{:S(2)}) collective-permute-start(bf16[384,128]{1,0:T(8,128)(2,1)S(1)} %get-tuple-element.31), channel_id=1, source_target_pairs={{0,12},{2,14},{4,8},{6,10},{8,4},{10,6},{12,0},{14,2},{1,13},{3,15... | collective-permute-start | bytes 294920 | tf_op jit(solution)/shard_map/ppermute | solution.py:289
  76.3 2.1 %shard_map.129.refs_8_ = bf16[1,64,13824]{2,1,0:T(8,128)(2,1)} custom-call(s32[7]{0:T(128)S(1)} %copy-done.4, bf16[64,128]{1,0:T(8,128)(2,1)S(1)} %shard_map.128.ranked, bf16[864,128]{1,0:T(8,128)(2,1)S(1)} %multiply_convert_fusion.hidden.refs_0_, bf16[864,128]{1,0:T(8,128)(2,1)S(1)} %collective-permute-done.30.refs_1_, ...), custom_call_target="tpu_custom_call" | custom-call | flops 20000000000 | tf_op jit(solution)/shard_map/pallas_call | solution.py:380
  78.4 0.1 collective-permute-start.24
  78.5 1.3 %collective-permute-done.28.refs_6_ = bf16[864,128]{1,0:T(8,128)(2,1)S(1)} collective-permute-done((bf16[864,128]{1,0:T(8,128)(2,1)S(1)}, bf16[864,128]{1,0:T(8,128)(2,1)S(1)}, u32[]{:S(2)}, u32[]{:S(2)}) %collective-permute-start.28) | collective-permute-done | bytes 221216 | tf_op jit(solution)/shard_map/ppermute | solution.py:289
  79.8 0.5 collective-permute-start.26
  80.3 3.7 %collective-permute-done.22.refs_2_ = bf16[384,128]{1,0:T(8,128)(2,1)S(1)} collective-permute-done((bf16[384,128]{1,0:T(8,128)(2,1)S(1)}, bf16[384,128]{1,0:T(8,128)(2,1)S(1)}, u32[]{:S(2)}, u32[]{:S(2)}) %collective-permute-start.22) | collective-permute-done | bytes 98336 | tf_op jit(solution)/shard_map/ppermute | solution.py:289
  83.9 2.1 %shard_map.127 = (bf16[320,128]{1,0:T(8,128)(2,1)}, bf16[1,64,5120]{2,1,0:T(8,128)(2,1)}, bf16[64,128]{1,0:T(8,128)(2,1)S(1)}) custom-call(s32[7]{0:T(128)S(1)} %copy-done.4, bf16[2,64,320]{2,1,0:T(8,128)(2,1)S(1)} %copy-done.5, bf16[8,384,128]{2,1,0:T(8,128)(2,1)S(1)} %shard_map.125.gathered, ...), custom_call_target="tpu_custom_call" | custom-call | flops 20000000000 | tf_op jit(solution)/shard_map/pallas_call | solution.py:362
  86.0 2.1 %shard_map.130 = bf16[1,64,13824]{2,1,0:T(8,128)(2,1)} custom-call(s32[7]{0:T(128)S(1)} %copy-done.4, bf16[64,128]{1,0:T(8,128)(2,1)S(1)} %shard_map.128.ranked, bf16[864,128]{1,0:T(8,128)(2,1)S(1)} %collective-permute-done.19.refs_1_.refs_0_, bf16[864,128]{1,0:T(8,128)(2,1)S(1)} %collective-permute-done.24.refs_1_, ...), custom_call_target="tpu_custom_call", output_to_operand_aliasing={{}: (10, {})} | custom-call | flops 20000000000 | tf_op jit(solution)/shard_map/pallas_call | solution.py:380
  (51 shorter events, 0.1 us)
Async XLA Ops:
  0.6 23.9 %copy-start.1 = (bf16[16,2560]{1,0:T(8,128)(2,1)S(1)}, bf16[16,2560]{1,0:T(8,128)(2,1)}, u32[]{:S(2)}) copy-start(bf16[16,2560]{1,0:T(8,128)(2,1)} %refs_0_.1) | copy-start | bytes 245764
  0.6 6.0 %collective-permute-start = (bf16[16,2560]{1,0:T(8,128)(2,1)}, bf16[16,2560]{1,0:T(8,128)(2,1)S(1)}, u32[]{:S(2)}, u32[]{:S(2)}) collective-permute-start(bf16[16,2560]{1,0:T(8,128)(2,1)} %refs_0_.1), channel_id=1, source_target_pairs={{0,4},{2,6},{4,0},{6,2},{8,12},{10,14},{12,8},{14,10},{1,5},{3,7},... | collective-permute-start | bytes 245768 | tf_op jit(solution)/shard_map/ppermute | solution.py:289
  2.3 9.4 %collective-permute-start.3 = (bf16[16,2560]{1,0:T(8,128)(2,1)}, bf16[16,2560]{1,0:T(8,128)(2,1)S(1)}, u32[]{:S(2)}, u32[]{:S(2)}) collective-permute-start(bf16[16,2560]{1,0:T(8,128)(2,1)} %refs_0_.1), channel_id=1, source_target_pairs={{0,8},{2,10},{4,12},{6,14},{8,0},{10,2},{12,4},{14,6},{1,9},{3,11}... | collective-permute-start | bytes 245768 | tf_op jit(solution)/shard_map/ppermute | solution.py:289
  4.9 6.8 %collective-permute-start.5 = (bf16[16,2560]{1,0:T(8,128)(2,1)}, bf16[16,2560]{1,0:T(8,128)(2,1)S(1)}, u32[]{:S(2)}, u32[]{:S(2)}) collective-permute-start(bf16[16,2560]{1,0:T(8,128)(2,1)} %refs_0_.1), channel_id=1, source_target_pairs={{0,12},{2,14},{4,8},{6,10},{8,4},{10,6},{12,0},{14,2},{1,13},{3,15... | collective-permute-start | bytes 245768 | tf_op jit(solution)/shard_map/ppermute | solution.py:289
  5.1 8.1 %collective-permute-start.1 = (bf16[16,2560]{1,0:T(8,128)(2,1)}, bf16[16,2560]{1,0:T(8,128)(2,1)S(1)}, u32[]{:S(2)}, u32[]{:S(2)}) collective-permute-start(bf16[16,2560]{1,0:T(8,128)(2,1)} %refs_0_.1), channel_id=1, source_target_pairs={{0,2},{2,0},{4,6},{6,4},{8,10},{10,8},{12,14},{14,12},{1,3},{3,1},... | collective-permute-start | bytes 245768 | tf_op jit(solution)/shard_map/ppermute | solution.py:289
  6.6 7.1 %collective-permute-start.7 = (bf16[16,2560]{1,0:T(8,128)(2,1)}, bf16[16,2560]{1,0:T(8,128)(2,1)S(1)}, u32[]{:S(2)}, u32[]{:S(2)}) collective-permute-start(bf16[16,2560]{1,0:T(8,128)(2,1)} %refs_0_.1), channel_id=1, source_target_pairs={{0,1},{1,0},{2,3},{3,2},{4,5},{5,4},{6,7},{7,6},{8,9},{9,8},{10,11... | collective-permute-start | bytes 245768 | tf_op jit(solution)/shard_map/ppermute | solution.py:292
  6.6 0.6 copy-start.6
  10.3 5.5 %collective-permute-start.2 = (bf16[16,2560]{1,0:T(8,128)(2,1)}, bf16[16,2560]{1,0:T(8,128)(2,1)S(1)}, u32[]{:S(2)}, u32[]{:S(2)}) collective-permute-start(bf16[16,2560]{1,0:T(8,128)(2,1)} %get-tuple-element.22.refs_2_), channel_id=1, source_target_pairs={{0,2},{2,0},{4,6},{6,4},{8,10},{10,8},{12,14},{14,12},{1,3},{3,1},... | collective-permute-start | bytes 245768 | tf_op jit(solution)/shard_map/ppermute | solution.py:289
  11.7 4.2 %collective-permute-start.9 = (bf16[16,2560]{1,0:T(8,128)(2,1)}, bf16[16,2560]{1,0:T(8,128)(2,1)S(1)}, u32[]{:S(2)}, u32[]{:S(2)}) collective-permute-start(bf16[16,2560]{1,0:T(8,128)(2,1)} %get-tuple-element.22.refs_2_), channel_id=1, source_target_pairs={{0,1},{1,0},{2,3},{3,2},{4,5},{5,4},{6,7},{7,6},{8,9},{9,8},{10,11... | collective-permute-start | bytes 245768 | tf_op jit(solution)/shard_map/ppermute | solution.py:292
  11.7 5.9 %collective-permute-start.4 = (bf16[16,2560]{1,0:T(8,128)(2,1)S(1)}, bf16[16,2560]{1,0:T(8,128)(2,1)S(1)}, u32[]{:S(2)}, u32[]{:S(2)}) collective-permute-start(bf16[16,2560]{1,0:T(8,128)(2,1)S(1)} %collective-permute-done.3.refs_4_), channel_id=1, source_target_pairs={{0,2},{2,0},{4,6},{6,4},{8,10},{10,8},{12,14},{14,12},{1,3},{3,1},... | collective-permute-start | bytes 245768 | tf_op jit(solution)/shard_map/ppermute | solution.py:289
  13.2 5.7 %collective-permute-start.6 = (bf16[16,2560]{1,0:T(8,128)(2,1)S(1)}, bf16[16,2560]{1,0:T(8,128)(2,1)S(1)}, u32[]{:S(2)}, u32[]{:S(2)}) collective-permute-start(bf16[16,2560]{1,0:T(8,128)(2,1)S(1)} %collective-permute-done.5.refs_6_), channel_id=1, source_target_pairs={{0,2},{2,0},{4,6},{6,4},{8,10},{10,8},{12,14},{14,12},{1,3},{3,1},... | collective-permute-start | bytes 245768 | tf_op jit(solution)/shard_map/ppermute | solution.py:289
  13.7 5.2 %collective-permute-start.11 = (bf16[16,2560]{1,0:T(8,128)(2,1)S(1)}, bf16[16,2560]{1,0:T(8,128)(2,1)S(1)}, u32[]{:S(2)}, u32[]{:S(2)}) collective-permute-start(bf16[16,2560]{1,0:T(8,128)(2,1)S(1)} %collective-permute-done.3.refs_4_), channel_id=1, source_target_pairs={{0,1},{1,0},{2,3},{3,2},{4,5},{5,4},{6,7},{7,6},{8,9},{9,8},{10,11... | collective-permute-start | bytes 245768 | tf_op jit(solution)/shard_map/ppermute | solution.py:292
  15.8 8.6 %collective-permute-start.13 = (bf16[16,2560]{1,0:T(8,128)(2,1)S(1)}, bf16[16,2560]{1,0:T(8,128)(2,1)S(1)}, u32[]{:S(2)}, u32[]{:S(2)}) collective-permute-start(bf16[16,2560]{1,0:T(8,128)(2,1)S(1)} %collective-permute-done.5.refs_6_), channel_id=1, source_target_pairs={{0,1},{1,0},{2,3},{3,2},{4,5},{5,4},{6,7},{7,6},{8,9},{9,8},{10,11... | collective-permute-start | bytes 245768 | tf_op jit(solution)/shard_map/ppermute | solution.py:292
  15.9 8.6 %collective-permute-start.8 = (bf16[16,2560]{1,0:T(8,128)(2,1)S(1)}, bf16[16,2560]{1,0:T(8,128)(2,1)S(1)}, u32[]{:S(2)}, u32[]{:S(2)}) collective-permute-start(bf16[16,2560]{1,0:T(8,128)(2,1)S(1)} %collective-permute-done.1.refs_1_), channel_id=1, source_target_pairs={{0,1},{1,0},{2,3},{3,2},{4,5},{5,4},{6,7},{7,6},{8,9},{9,8},{10,11... | collective-permute-start | bytes 245768 | tf_op jit(solution)/shard_map/ppermute | solution.py:292
  17.6 6.9 %collective-permute-start.10 = (bf16[16,2560]{1,0:T(8,128)(2,1)S(1)}, bf16[16,2560]{1,0:T(8,128)(2,1)S(1)}, u32[]{:S(2)}, u32[]{:S(2)}) collective-permute-start(bf16[16,2560]{1,0:T(8,128)(2,1)S(1)} %collective-permute-done.2.refs_3_), channel_id=1, source_target_pairs={{0,1},{1,0},{2,3},{3,2},{4,5},{5,4},{6,7},{7,6},{8,9},{9,8},{10,11... | collective-permute-start | bytes 245768 | tf_op jit(solution)/shard_map/ppermute | solution.py:292
  19.0 5.5 %collective-permute-start.12 = (bf16[16,2560]{1,0:T(8,128)(2,1)S(1)}, bf16[16,2560]{1,0:T(8,128)(2,1)S(1)}, u32[]{:S(2)}, u32[]{:S(2)}) collective-permute-start(bf16[16,2560]{1,0:T(8,128)(2,1)S(1)} %collective-permute-done.4.refs_5_), channel_id=1, source_target_pairs={{0,1},{1,0},{2,3},{3,2},{4,5},{5,4},{6,7},{7,6},{8,9},{9,8},{10,11... | collective-permute-start | bytes 245768 | tf_op jit(solution)/shard_map/ppermute | solution.py:292
  19.0 5.5 %collective-permute-start.14 = (bf16[16,2560]{1,0:T(8,128)(2,1)S(1)}, bf16[16,2560]{1,0:T(8,128)(2,1)S(1)}, u32[]{:S(2)}, u32[]{:S(2)}) collective-permute-start(bf16[16,2560]{1,0:T(8,128)(2,1)S(1)} %collective-permute-done.6.refs_7_), channel_id=1, source_target_pairs={{0,1},{1,0},{2,3},{3,2},{4,5},{5,4},{6,7},{7,6},{8,9},{9,8},{10,11... | collective-permute-start | bytes 245768 | tf_op jit(solution)/shard_map/ppermute | solution.py:292
  19.5 25.3 %all-to-all-start = ((bf16[8,384,128]{2,1,0:T(8,128)(2,1)}), bf16[8,384,128]{2,1,0:T(8,128)(2,1)S(1)}, u32[]{:S(2)}, u32[]{:S(2)}) async-start(bf16[8,384,128]{2,1,0:T(8,128)(2,1)} %get-tuple-element.21), calls=%async_computation | async-start | bytes 1572864 | tf_op jit(solution)/shard_map/all_to_all | solution.py:317
  24.5 0.9 %copy-start.2 = (bf16[16,2560]{1,0:T(8,128)(2,1)S(1)}, bf16[16,2560]{1,0:T(8,128)(2,1)}, u32[]{:S(2)}) copy-start(bf16[16,2560]{1,0:T(8,128)(2,1)} %get-tuple-element.22.refs_2_) | copy-start | bytes 245764
  25.4 0.6 copy-start.3
  26.0 7.0 %slice-start = ((s8[8847360]{0:T(1024)(128)(4,1)}), s8[4194304]{0:T(1024)(128)(4,1)S(1)}, s32[]{:S(2)}) async-start(s8[8847360]{0:T(1024)(128)(4,1)} %bitcast.12), calls=%async_computation.1 | async-start | bytes 8388608
  26.7 6.4 %slice-start.1 = ((s8[8847360]{0:T(1024)(128)(4,1)}), s8[4194304]{0:T(1024)(128)(4,1)S(1)}, s32[]{:S(2)}) async-start(s8[8847360]{0:T(1024)(128)(4,1)} %bitcast.12), calls=%async_computation.2 | async-start | bytes 8388608
  26.7 6.4 %slice-start.2 = ((s8[8847360]{0:T(1024)(128)(4,1)}), s8[458752]{0:T(1024)(128)(4,1)S(1)}, s32[]{:S(2)}) async-start(s8[8847360]{0:T(1024)(128)(4,1)} %bitcast.12), calls=%async_computation.3 | async-start | bytes 917504
  26.7 8.8 %slice-start.3 = ((s8[8847360]{0:T(1024)(128)(4,1)}), s8[4194304]{0:T(1024)(128)(4,1)S(1)}, s32[]{:S(2)}) async-start(s8[8847360]{0:T(1024)(128)(4,1)} %bitcast.14), calls=%async_computation.4 | async-start | bytes 8388608
  26.7 8.8 %slice-start.4 = ((s8[8847360]{0:T(1024)(128)(4,1)}), s8[4194304]{0:T(1024)(128)(4,1)S(1)}, s32[]{:S(2)}) async-start(s8[8847360]{0:T(1024)(128)(4,1)} %bitcast.14), calls=%async_computation.5 | async-start | bytes 8388608
  33.1 2.5 %slice-start.5 = ((s8[8847360]{0:T(1024)(128)(4,1)}), s8[458752]{0:T(1024)(128)(4,1)S(1)}, s32[]{:S(2)}) async-start(s8[8847360]{0:T(1024)(128)(4,1)} %bitcast.14), calls=%async_computation.6 | async-start | bytes 917504
  35.6 1.6 %copy-start = (bf16[2,64,864]{2,1,0:T(8,128)(2,1)S(1)}, bf16[2,64,864]{2,1,0:T(8,128)(2,1)}, u32[]{:S(2)}) copy-start(bf16[2,64,864]{2,1,0:T(8,128)(2,1)} %get-tuple-element.23.in_blocks) | copy-start | bytes 663556
  35.6 1.6 %copy-start.4 = (s32[7]{0:T(128)S(1)}, s32[7]{0:T(128)}, u32[]{:S(2)}) copy-start(s32[7]{0:T(128)} %get-tuple-element.19.facts) | copy-start | bytes 88
  39.2 2.2 %collective-permute-start.15 = (bf16[2624,128]{1,0:T(8,128)(2,1)S(1)}, bf16[2624,128]{1,0:T(8,128)(2,1)S(1)}, u32[]{:S(2)}, u32[]{:S(2)}) collective-permute-start(bf16[2624,128]{1,0:T(8,128)(2,1)S(1)} %get-tuple-element.25), channel_id=1, source_target_pairs={{0,1},{1,0},{2,3},{3,2},{4,5},{5,4},{6,7},{7,6},{8,9},{9,8},{10,11... | collective-permute-start | bytes 2015240 | tf_op jit(solution)/shard_map/ppermute | solution.py:292
  44.8 22.7 %collective-permute-start.16 = (bf16[8,384,128]{2,1,0:T(8,128)(2,1)S(1)}, bf16[8,384,128]{2,1,0:T(8,128)(2,1)S(1)}, u32[]{:S(2)}, u32[]{:S(2)}) collective-permute-start(bf16[8,384,128]{2,1,0:T(8,128)(2,1)S(1)} %shard_map.125.gathered), channel_id=1, source_target_pairs={{0,1},{1,0},{2,3},{3,2},{4,5},{5,4},{6,7},{7,6},{8,9},{9,8},{10,11... | collective-permute-start | bytes 2359304 | tf_op jit(solution)/shard_map/ppermute | solution.py:292
  44.8 9.9 %collective-permute-start.18 = (bf16[864,128]{1,0:T(8,128)(2,1)S(1)}, bf16[864,128]{1,0:T(8,128)(2,1)S(1)}, u32[]{:S(2)}, u32[]{:S(2)}) collective-permute-start(bf16[864,128]{1,0:T(8,128)(2,1)S(1)} %multiply_convert_fusion.hidden.refs_0_), channel_id=1, source_target_pairs={{0,4},{2,6},{4,0},{6,2},{8,12},{10,14},{12,8},{14,10},{1,5},{3,7},... | collective-permute-start | bytes 663560 | tf_op jit(solution)/shard_map/ppermute | solution.py:289
  45.1 11.8 %collective-permute-start.31 = (bf16[864,128]{1,0:T(8,128)(2,1)S(1)}, bf16[864,128]{1,0:T(8,128)(2,1)S(1)}, u32[]{:S(2)}, u32[]{:S(2)}) collective-permute-start(bf16[864,128]{1,0:T(8,128)(2,1)S(1)} %multiply_convert_fusion.hidden.refs_0_), channel_id=1, source_target_pairs={{0,2},{2,0},{4,6},{6,4},{8,10},{10,8},{12,14},{14,12},{1,3},{3,1},... | collective-permute-start | bytes 663560 | tf_op jit(solution)/shard_map/ppermute | solution.py:289
  46.3 20.2 %collective-permute-start.17 = (bf16[1344,128]{1,0:T(8,128)(2,1)S(1)}, bf16[1344,128]{1,0:T(8,128)(2,1)S(1)}, u32[]{:S(2)}, u32[]{:S(2)}) collective-permute-start(bf16[1344,128]{1,0:T(8,128)(2,1)S(1)} %get-tuple-element.27), channel_id=1, source_target_pairs={{0,2},{2,0},{4,6},{6,4},{8,10},{10,8},{12,14},{14,12},{1,3},{3,1},... | collective-permute-start | bytes 1032200 | tf_op jit(solution)/shard_map/ppermute | solution.py:289
  47.1 18.7 %collective-permute-start.19 = (bf16[864,128]{1,0:T(8,128)(2,1)S(1)}, bf16[864,128]{1,0:T(8,128)(2,1)S(1)}, u32[]{:S(2)}, u32[]{:S(2)}) collective-permute-start(bf16[864,128]{1,0:T(8,128)(2,1)S(1)} %multiply_convert_fusion.hidden.refs_0_), channel_id=1, source_target_pairs={{0,8},{2,10},{4,12},{6,14},{8,0},{10,2},{12,4},{14,6},{1,9},{3,11}... | collective-permute-start | bytes 663560 | tf_op jit(solution)/shard_map/ppermute | solution.py:289
  54.8 11.1 %collective-permute-start.20 = (bf16[864,128]{1,0:T(8,128)(2,1)S(1)}, bf16[864,128]{1,0:T(8,128)(2,1)S(1)}, u32[]{:S(2)}, u32[]{:S(2)}) collective-permute-start(bf16[864,128]{1,0:T(8,128)(2,1)S(1)} %multiply_convert_fusion.hidden.refs_0_), channel_id=1, source_target_pairs={{0,12},{2,14},{4,8},{6,10},{8,4},{10,6},{12,0},{14,2},{1,13},{3,15... | collective-permute-start | bytes 663560 | tf_op jit(solution)/shard_map/ppermute | solution.py:289
  56.9 9.5 %collective-permute-start.34 = (bf16[864,128]{1,0:T(8,128)(2,1)S(1)}, bf16[864,128]{1,0:T(8,128)(2,1)S(1)}, u32[]{:S(2)}, u32[]{:S(2)}) collective-permute-start(bf16[864,128]{1,0:T(8,128)(2,1)S(1)} %collective-permute-done.18.refs_0_.refs_4_), channel_id=1, source_target_pairs={{0,2},{2,0},{4,6},{6,4},{8,10},{10,8},{12,14},{14,12},{1,3},{3,1},... | collective-permute-start | bytes 663560 | tf_op jit(solution)/shard_map/ppermute | solution.py:289
  65.9 3.4 %collective-permute-start.30 = (bf16[864,128]{1,0:T(8,128)(2,1)S(1)}, bf16[864,128]{1,0:T(8,128)(2,1)S(1)}, u32[]{:S(2)}, u32[]{:S(2)}) collective-permute-start(bf16[864,128]{1,0:T(8,128)(2,1)S(1)} %multiply_convert_fusion.hidden.refs_0_), channel_id=1, source_target_pairs={{0,1},{1,0},{2,3},{3,2},{4,5},{5,4},{6,7},{7,6},{8,9},{9,8},{10,11... | collective-permute-start | bytes 663560 | tf_op jit(solution)/shard_map/ppermute | solution.py:292
  65.9 4.4 %collective-permute-start.32 = (bf16[864,128]{1,0:T(8,128)(2,1)S(1)}, bf16[864,128]{1,0:T(8,128)(2,1)S(1)}, u32[]{:S(2)}, u32[]{:S(2)}) collective-permute-start(bf16[864,128]{1,0:T(8,128)(2,1)S(1)} %collective-permute-done.31.refs_2_), channel_id=1, source_target_pairs={{0,1},{1,0},{2,3},{3,2},{4,5},{5,4},{6,7},{7,6},{8,9},{9,8},{10,11... | collective-permute-start | bytes 663560 | tf_op jit(solution)/shard_map/ppermute | solution.py:292
  66.4 7.5 %collective-permute-start.33 = (bf16[864,128]{1,0:T(8,128)(2,1)S(1)}, bf16[864,128]{1,0:T(8,128)(2,1)S(1)}, u32[]{:S(2)}, u32[]{:S(2)}) collective-permute-start(bf16[864,128]{1,0:T(8,128)(2,1)S(1)} %collective-permute-done.18.refs_0_.refs_4_), channel_id=1, source_target_pairs={{0,1},{1,0},{2,3},{3,2},{4,5},{5,4},{6,7},{7,6},{8,9},{9,8},{10,11... | collective-permute-start | bytes 663560 | tf_op jit(solution)/shard_map/ppermute | solution.py:292
  66.5 7.5 %collective-permute-start.35 = (bf16[864,128]{1,0:T(8,128)(2,1)S(1)}, bf16[864,128]{1,0:T(8,128)(2,1)S(1)}, u32[]{:S(2)}, u32[]{:S(2)}) collective-permute-start(bf16[864,128]{1,0:T(8,128)(2,1)S(1)} %collective-permute-done.34.refs_6_), channel_id=1, source_target_pairs={{0,1},{1,0},{2,3},{3,2},{4,5},{5,4},{6,7},{7,6},{8,9},{9,8},{10,11... | collective-permute-start | bytes 663560 | tf_op jit(solution)/shard_map/ppermute | solution.py:292
  67.5 10.9 %collective-permute-start.25 = (bf16[864,128]{1,0:T(8,128)(2,1)S(1)}, bf16[864,128]{1,0:T(8,128)(2,1)S(1)}, u32[]{:S(2)}, u32[]{:S(2)}) collective-permute-start(bf16[864,128]{1,0:T(8,128)(2,1)S(1)} %collective-permute-done.19.refs_1_.refs_0_), channel_id=1, source_target_pairs={{0,2},{2,0},{4,6},{6,4},{8,10},{10,8},{12,14},{14,12},{1,3},{3,1},... | collective-permute-start | bytes 663560 | tf_op jit(solution)/shard_map/ppermute | solution.py:289
  69.3 10.4 %collective-permute-start.28 = (bf16[864,128]{1,0:T(8,128)(2,1)S(1)}, bf16[864,128]{1,0:T(8,128)(2,1)S(1)}, u32[]{:S(2)}, u32[]{:S(2)}) collective-permute-start(bf16[864,128]{1,0:T(8,128)(2,1)S(1)} %collective-permute-done.20.refs_2_.refs_4_), channel_id=1, source_target_pairs={{0,2},{2,0},{4,6},{6,4},{8,10},{10,8},{12,14},{14,12},{1,3},{3,1},... | collective-permute-start | bytes 663560 | tf_op jit(solution)/shard_map/ppermute | solution.py:289
  70.3 9.5 %collective-permute-start.21 = (bf16[384,128]{1,0:T(8,128)(2,1)S(1)}, bf16[384,128]{1,0:T(8,128)(2,1)S(1)}, u32[]{:S(2)}, u32[]{:S(2)}) collective-permute-start(bf16[384,128]{1,0:T(8,128)(2,1)S(1)} %get-tuple-element.29), channel_id=1, source_target_pairs={{0,4},{2,6},{4,0},{6,2},{8,12},{10,14},{12,8},{14,10},{1,5},{3,7},... | collective-permute-start | bytes 294920 | tf_op jit(solution)/shard_map/ppermute | solution.py:289
  73.9 10.0 %collective-permute-start.22 = (bf16[384,128]{1,0:T(8,128)(2,1)S(1)}, bf16[384,128]{1,0:T(8,128)(2,1)S(1)}, u32[]{:S(2)}, u32[]{:S(2)}) collective-permute-start(bf16[384,128]{1,0:T(8,128)(2,1)S(1)} %get-tuple-element.30), channel_id=1, source_target_pairs={{0,8},{2,10},{4,12},{6,14},{8,0},{10,2},{12,4},{14,6},{1,9},{3,11}... | collective-permute-start | bytes 294920 | tf_op jit(solution)/shard_map/ppermute | solution.py:289
  73.9 10.0 %copy-start.5 = (bf16[2,64,320]{2,1,0:T(8,128)(2,1)S(1)}, bf16[2,64,320]{2,1,0:T(8,128)(2,1)}, u32[]{:S(2)}) copy-start(bf16[2,64,320]{2,1,0:T(8,128)(2,1)} %get-tuple-element.20.out_blocks) | copy-start | bytes 245764
  73.9 10.0 %collective-permute-start.23 = (bf16[384,128]{1,0:T(8,128)(2,1)S(1)}, bf16[384,128]{1,0:T(8,128)(2,1)S(1)}, u32[]{:S(2)}, u32[]{:S(2)}) collective-permute-start(bf16[384,128]{1,0:T(8,128)(2,1)S(1)} %get-tuple-element.31), channel_id=1, source_target_pairs={{0,12},{2,14},{4,8},{6,10},{8,4},{10,6},{12,0},{14,2},{1,13},{3,15... | collective-permute-start | bytes 294920 | tf_op jit(solution)/shard_map/ppermute | solution.py:289
  78.4 7.6 %collective-permute-start.24 = (bf16[864,128]{1,0:T(8,128)(2,1)S(1)}, bf16[864,128]{1,0:T(8,128)(2,1)S(1)}, u32[]{:S(2)}, u32[]{:S(2)}) collective-permute-start(bf16[864,128]{1,0:T(8,128)(2,1)S(1)} %collective-permute-done.19.refs_1_.refs_0_), channel_id=1, source_target_pairs={{0,1},{1,0},{2,3},{3,2},{4,5},{5,4},{6,7},{7,6},{8,9},{9,8},{10,11... | collective-permute-start | bytes 663560 | tf_op jit(solution)/shard_map/ppermute | solution.py:292
  79.8 6.3 %collective-permute-start.27 = (bf16[864,128]{1,0:T(8,128)(2,1)S(1)}, bf16[864,128]{1,0:T(8,128)(2,1)S(1)}, u32[]{:S(2)}, u32[]{:S(2)}) collective-permute-start(bf16[864,128]{1,0:T(8,128)(2,1)S(1)} %collective-permute-done.20.refs_2_.refs_4_), channel_id=1, source_target_pairs={{0,1},{1,0},{2,3},{3,2},{4,5},{5,4},{6,7},{7,6},{8,9},{9,8},{10,11... | collective-permute-start | bytes 663560 | tf_op jit(solution)/shard_map/ppermute | solution.py:292
  79.8 6.3 %collective-permute-start.26 = (bf16[864,128]{1,0:T(8,128)(2,1)S(1)}, bf16[864,128]{1,0:T(8,128)(2,1)S(1)}, u32[]{:S(2)}, u32[]{:S(2)}) collective-permute-start(bf16[864,128]{1,0:T(8,128)(2,1)S(1)} %collective-permute-done.25.refs_2_), channel_id=1, source_target_pairs={{0,1},{1,0},{2,3},{3,2},{4,5},{5,4},{6,7},{7,6},{8,9},{9,8},{10,11... | collective-permute-start | bytes 663560 | tf_op jit(solution)/shard_map/ppermute | solution.py:292
  83.9 2.1 %collective-permute-start.29 = (bf16[864,128]{1,0:T(8,128)(2,1)S(1)}, bf16[864,128]{1,0:T(8,128)(2,1)S(1)}, u32[]{:S(2)}, u32[]{:S(2)}) collective-permute-start(bf16[864,128]{1,0:T(8,128)(2,1)S(1)} %collective-permute-done.28.refs_6_), channel_id=1, source_target_pairs={{0,1},{1,0},{2,3},{3,2},{4,5},{5,4},{6,7},{7,6},{8,9},{9,8},{10,11... | collective-permute-start | bytes 663560 | tf_op jit(solution)/shard_map/ppermute | solution.py:292

commit v4 on v3

--- a/solution.py
+++ b/solution.py
@@ -12,7 +12,7 @@
 ROWS_BY_ROWS = (((1,), (1,)), ((), ()))
 ASSEMBLE_FLOPS = 0
 GRAD_FLOPS = 20000000000
-FINAL_FLOPS = 20000000000
+FINAL_FLOPS = 8000000000
 ADD_FLOPS = 0
 PAIR_FLOPS = 0
 SPLIT_FLOPS = 0
@@ -119,13 +119,14 @@
         copy.wait()
 
 
-def assemble_body(facts, *refs):
-    facts, pieces, out = Facts(facts), refs[:-1], refs[-1]
+def assemble_body(*refs):
+    pieces, out = refs[:-1], refs[-1]
+    batch, own_core = lax.axis_index("batch"), lax.axis_index("tensor")
     count = len(pieces) // 2
     rows, half = pieces[0].shape
     for i, piece in enumerate(pieces):
-        row = pl.multiple_of((facts.batch ^ (i % count)) * rows, rows)
-        core = facts.core if i < count else 1 - facts.core
+        row = pl.multiple_of((batch ^ (i % count)) * rows, rows)
+        core = own_core if i < count else 1 - own_core
         out[pl.ds(row, rows), pl.ds(pl.multiple_of(core * half, 128), half)] = piece[...]
 
 
@@ -224,6 +225,10 @@
     grad[0] = (facts.coefficient() * total).astype(grad.dtype)
 
 
+def copy_body(source, _, target):
+    target[...] = source[...]
+
+
 def pass_body(*refs):
     pass
 
@@ -298,6 +303,7 @@
         return [line[k] if k in line else flip(line[k ^ 1], 1) for k in range(8)]
 
     line = along_z(tokens)
+    arrived = line[2]
     facts, cot_and_back, out_blocks, in_blocks, line[2] = kernel_call(
         prepare_body,
         [
@@ -320,9 +326,9 @@
     rows = kernel_call(
         assemble_body,
         array(token_count, model_width),
-        [IN_SMEM] + [IN_VMEM] * 16,
+        [IN_VMEM] * 16,
         flops=ASSEMBLE_FLOPS,
-    )(facts, *own, *other)
+    )(*own[:2], arrived, *own[3:], *other)
     gate_value = lax.dot_general(gate_weight.T, rows, ROWS_BY_ROWS, preferred_element_type=f32)
     up_value = lax.dot_general(up_weight.T, rows, ROWS_BY_ROWS, preferred_element_type=f32)
     hidden = (jax.nn.silu(gate_value) * up_value).astype(bf16)
@@ -342,6 +348,9 @@
         flops=ADD_FLOPS,
     )(facts, kept, to_other_core(leaving))
     line = along_z(hidden)
+    line[0] = kernel_call(copy_body, array(width, token_count), [IN_VMEM, IN_HBM])(
+        hidden, line[2]
+    )
     gathered = kernel_call(
         pass_body,
         array(8, columns + rank, token_count),
@@ -357,7 +366,7 @@
         [array(columns + rank, token_count)] * 4,
         [IN_SMEM] + [IN_VMEM] * 2 + [IN_HBM] * 3,
         flops=PAIR_FLOPS,
-    )(facts, stays, flip(leaving, 1), *[line[k] for k in (2, 4, 6)])
+    )(facts, stays, flip(leaving, 1), line[2], line[2], line[2])
     shares = [shares[0]] + [flip(shares[z], 2 * z) for z in (1, 2, 3)]
     mixed, grad_out, low_chosen = kernel_call(
         final_body,

time: 89.9 us -> 88.9 us (0.989)
  waiting for transfers between devices: 28.8 us -> 31.3 us
  starting transfers between devices: 32 us -> 29.9 us
    ppermute x18, starting transfers between devices: 24.3 us -> 22.3 us  [flip(): return lax.ppermute(piece, 'batch', [(i, i ^ k) for i in range(8)])]
    all_to_all x1, waiting for transfers between devices: 2.75 us -> 4.48 us  [on_chips(): lax.all_to_all(cot_and_back, 'batch', split_axis=0, concat_axis=0, tiled=...]
    ppermute x18, waiting for transfers between devices: 23.9 us -> 24.9 us  [flip(): return lax.ppermute(piece, 'batch', [(i, i ^ k) for i in range(8)])]
    unnamed x26 -> x24, local copies, waits for them, and re-layouts: 2.19 us -> 1.57 us
  transfers between devices with their start and end apart: 37 -> 37, of which waited for: 10 -> 11; matrix products, arithmetic and copies ran while one was open for 12% -> 12% of each run, Pallas kernels for 13% -> 13%
where the time goes in v4:
time: 88.9 us; the launch traced here: 87.2 us
  waiting for transfers between devices  31.3 us (35%)
  starting transfers between devices  29.9 us (34%)
  Pallas kernels  13.3 us (15%)
  matrix products  10.1 us (11%)
  local copies, waits for them, and re-layouts  1.57 us (2%)
  between operations  0.97 us (1%)
    ppermute x18, waiting for transfers between devices, flip(): return lax.ppermute(piece, 'batch', [(i, i ^ k) for i in range(8)])  24.9 us
    ppermute x18, starting transfers between devices, flip(): return lax.ppermute(piece, 'batch', [(i, i ^ k) for i in range(8)])  22.3 us
    dot_general x1, matrix products, on_chips(): lax.dot_general(gate_weight.T, rows, ROWS_BY_ROWS, preferred_element_type...  6.11 us
    all_to_all x1, starting transfers between devices, on_chips(): lax.all_to_all(cot_and_back, 'batch', split_axis=0, concat_axis=0, tiled=...  4.97 us
    all_to_all x1, waiting for transfers between devices, on_chips(): lax.all_to_all(cot_and_back, 'batch', split_axis=0, concat_axis=0, tiled=...  4.48 us
    pallas_call x2, Pallas kernels, on_chips(): kernel_call(functools.partial(in_grad_body, flips=flips), array(1, rank,...  4.19 us
    pallas_call x1, Pallas kernels, on_chips(): kernel_call(prepare_body, [jax.ShapeDtypeStruct((3 + 2 * block_count,), j...  3.07 us
    ppermute x18, starting transfers between devices, to_other_core(): return lax.ppermute(piece, 'tensor', [(0, 1), (1, 0)])  2.59 us
  transfers between devices with their start and end apart: 37, of which 11 were waited for; matrix products, arithmetic and copies ran while one was open for 12% of the time, Pallas kernels for 13%

profile of v4, /device:TPU:2, one launch (start us, length us, event | category | flops | bytes accessed | tf_op | source)
XLA Modules:
  0.0 87.2 jit_solution(12841564211928876253)
XLA Ops:
  0.6 1.6 %collective-permute-start = (bf16[16,2560]{1,0:T(8,128)(2,1)}, bf16[16,2560]{1,0:T(8,128)(2,1)S(1)}, u32[]{:S(2)}, u32[]{:S(2)}) collective-permute-start(bf16[16,2560]{1,0:T(8,128)(2,1)} %refs_0_.1), channel_id=1, source_target_pairs={{0,4},{2,6},{4,0},{6,2},{8,12},{10,14},{12,8},{14,10},{1,5},{3,7},... | collective-permute-start | bytes 245768 | tf_op jit(solution)/shard_map/ppermute | solution.py:294
  2.3 2.6 %collective-permute-start.3 = (bf16[16,2560]{1,0:T(8,128)(2,1)}, bf16[16,2560]{1,0:T(8,128)(2,1)S(1)}, u32[]{:S(2)}, u32[]{:S(2)}) collective-permute-start(bf16[16,2560]{1,0:T(8,128)(2,1)} %refs_0_.1), channel_id=1, source_target_pairs={{0,8},{2,10},{4,12},{6,14},{8,0},{10,2},{12,4},{14,6},{1,9},{3,11}... | collective-permute-start | bytes 245768 | tf_op jit(solution)/shard_map/ppermute | solution.py:294
  4.9 0.2 collective-permute-start.5
  5.1 1.5 %collective-permute-start.1 = (bf16[16,2560]{1,0:T(8,128)(2,1)}, bf16[16,2560]{1,0:T(8,128)(2,1)S(1)}, u32[]{:S(2)}, u32[]{:S(2)}) collective-permute-start(bf16[16,2560]{1,0:T(8,128)(2,1)} %refs_0_.1), channel_id=1, source_target_pairs={{0,2},{2,0},{4,6},{6,4},{8,10},{10,8},{12,14},{14,12},{1,3},{3,1},... | collective-permute-start | bytes 245768 | tf_op jit(solution)/shard_map/ppermute | solution.py:294
  6.6 0.0 collective-permute-start.7
  6.6 0.0 collective-permute-done.piece.refs_2_
  6.6 0.6 copy-done
  7.3 3.1 %shard_map.121 = (s32[7]{0:T(128)}, bf16[8,384,128]{2,1,0:T(8,128)(2,1)}, bf16[2,64,320]{2,1,0:T(8,128)(2,1)}, bf16[2,64,864]{2,1,0:T(8,128)(2,1)}, bf16[16,2560]{1,0:T(8,128)(2,1)}) custom-call(s32[2]{0:T(128)} %owner.1, s32[2]{0:T(128)} %length.1, s32[16]{0:T(128)} %placement.1, bf16[16,64,320]{2,1,0:T(8,128)(2,1)} %adapter_out.1, ...), custom_call_target="tpu_custom_call" | custom-call | tf_op jit(solution)/shard_map/pallas_call | solution.py:307
  10.3 0.6 collective-permute-start.2
  10.9 0.8 collective-permute-done.3.refs_4_
  11.7 1.5 %collective-permute-start.4 = (bf16[16,2560]{1,0:T(8,128)(2,1)S(1)}, bf16[16,2560]{1,0:T(8,128)(2,1)S(1)}, u32[]{:S(2)}, u32[]{:S(2)}) collective-permute-start(bf16[16,2560]{1,0:T(8,128)(2,1)S(1)} %collective-permute-done.3.refs_4_), channel_id=1, source_target_pairs={{0,2},{2,0},{4,6},{6,4},{8,10},{10,8},{12,14},{14,12},{1,3},{3,1},... | collective-permute-start | bytes 245768 | tf_op jit(solution)/shard_map/ppermute | solution.py:294
  13.2 0.5 collective-permute-start.6
  13.7 0.5 collective-permute-start.9
  14.3 1.6 %collective-permute-done.2.refs_3_ = bf16[16,2560]{1,0:T(8,128)(2,1)S(1)} collective-permute-done((bf16[16,2560]{1,0:T(8,128)(2,1)}, bf16[16,2560]{1,0:T(8,128)(2,1)S(1)}, u32[]{:S(2)}, u32[]{:S(2)}) %collective-permute-start.2) | collective-permute-done | bytes 81952 | tf_op jit(solution)/shard_map/ppermute | solution.py:294
  15.9 1.8 %collective-permute-done.4.refs_5_ = bf16[16,2560]{1,0:T(8,128)(2,1)S(1)} collective-permute-done((bf16[16,2560]{1,0:T(8,128)(2,1)S(1)}, bf16[16,2560]{1,0:T(8,128)(2,1)S(1)}, u32[]{:S(2)}, u32[]{:S(2)}) %collective-permute-start.4) | collective-permute-done | bytes 81952 | tf_op jit(solution)/shard_map/ppermute | solution.py:294
  17.6 0.0 collective-permute-start.13
  17.6 1.4 %collective-permute-done.6.refs_7_ = bf16[16,2560]{1,0:T(8,128)(2,1)S(1)} collective-permute-done((bf16[16,2560]{1,0:T(8,128)(2,1)S(1)}, bf16[16,2560]{1,0:T(8,128)(2,1)S(1)}, u32[]{:S(2)}, u32[]{:S(2)}) %collective-permute-start.6) | collective-permute-done | bytes 81952 | tf_op jit(solution)/shard_map/ppermute | solution.py:294
  19.0 0.5 collective-permute-start.12
  19.5 0.1 collective-permute-start.14
  19.6 5.0 %all-to-all-start = ((bf16[8,384,128]{2,1,0:T(8,128)(2,1)}), bf16[8,384,128]{2,1,0:T(8,128)(2,1)S(1)}, u32[]{:S(2)}, u32[]{:S(2)}) async-start(bf16[8,384,128]{2,1,0:T(8,128)(2,1)} %get-tuple-element.21), calls=%async_computation | async-start | bytes 1572864 | tf_op jit(solution)/shard_map/all_to_all | solution.py:323
  24.5 0.0 collective-permute-done.11.refs_12_
  24.6 0.0 collective-permute-done.10.refs_11_
  24.6 0.0 copy-start.1
  24.6 0.9 %copy-done.1 = bf16[16,2560]{1,0:T(8,128)(2,1)S(1)} copy-done((bf16[16,2560]{1,0:T(8,128)(2,1)S(1)}, bf16[16,2560]{1,0:T(8,128)(2,1)}, u32[]{:S(2)}) %copy-start.1) | copy-done | bytes 81944
  25.5 0.1 shard_map.122
  25.6 0.0 slice-start.1
  25.6 0.0 slice-start.3
  25.6 0.0 slice-start.4
  25.7 6.1 %convolution_bitcast_fusion.1 = f32[864,128]{1,0:T(8,128)S(1)} fusion(bf16[128,5120]{1,0:T(8,128)(2,1)S(1)} %shard_map.122, bf16[5120,864]{0,1:T(8,128)(2,1)} %param.11), kind=kOutput, calls=%fused_computation.2 | convolution fusion | flops 1132462080 | bytes 10600448 | tf_op jit(solution)/shard_map/dot_general | solution.py:332
  31.8 0.0 slice-start.5
  31.8 2.5 %multiply_convert_fusion.hidden.source = bf16[864,128]{1,0:T(8,128)(2,1)S(1)} fusion(f32[864,128]{1,0:T(8,128)S(1)} %convolution_bitcast_fusion.1, bf16[128,5120]{1,0:T(8,128)(2,1)S(1)} %shard_map.122, bf16[5120,864]{0,1:T(8,128)(2,1)S(1)} %bitcast.13), kind=kOutput, calls=%fused_computation.3 | convolution fusion | flops 1133125632 | bytes 10821632 | tf_op jit(solution)/shard_map/dot_general | solution.py:333
  34.3 0.0 copy-start.2
  34.3 1.6 %convolution_convert_fusion.base = bf16[128,5120]{1,0:T(8,128)(2,1)S(1)} fusion(bf16[864,128]{1,0:T(8,128)(2,1)S(1)} %multiply_convert_fusion.hidden.source, bf16[864,5120]{1,0:T(8,128)(2,1)S(1)} %bitcast.15), kind=kOutput, calls=%fused_computation | convolution fusion | flops 1133117440 | bytes 10379264 | tf_op jit(solution)/shard_map/dot_general | solution.py:335
  35.9 2.0 %shard_map.123 = (bf16[2624,128]{1,0:T(8,128)(2,1)S(1)}, bf16[2624,128]{1,0:T(8,128)(2,1)S(1)}) custom-call(s32[7]{0:T(128)S(1)} %copy-done.4, bf16[128,5120]{1,0:T(8,128)(2,1)S(1)} %convolution_convert_fusion.base, bf16[864,128]{1,0:T(8,128)(2,1)S(1)} %multiply_convert_fusion.hidden.source, bf16[2,64,864]{2,1,0:T(8,128)(2,1)S(1)} %copy-done.2), custom_call_target="tpu_custom_call" | custom-call | tf_op jit(solution)/shard_map/pallas_call | solution.py:338
  37.9 0.3 collective-permute-start.15
  38.2 1.9 %collective-permute-done.15.arrived = bf16[2624,128]{1,0:T(8,128)(2,1)S(1)} collective-permute-done((bf16[2624,128]{1,0:T(8,128)(2,1)S(1)}, bf16[2624,128]{1,0:T(8,128)(2,1)S(1)}, u32[]{:S(2)}, u32[]{:S(2)}) %collective-permute-start.15) | collective-permute-done | bytes 671776 | tf_op jit(solution)/shard_map/ppermute | solution.py:297
  40.1 0.7 shard_map.124
  40.8 4.5 %all-to-all-done.refs_0_ = bf16[8,384,128]{2,1,0:T(8,128)(2,1)S(1)} async-done(((bf16[8,384,128]{2,1,0:T(8,128)(2,1)}), bf16[8,384,128]{2,1,0:T(8,128)(2,1)S(1)}, u32[]{:S(2)}, u32[]{:S(2)}) %all-to-all-start) | async-done | bytes 786464 | tf_op jit(solution)/shard_map/all_to_all | solution.py:323
  45.3 0.1 collective-permute-start.18
  45.4 1.4 %collective-permute-start.17 = (bf16[1344,128]{1,0:T(8,128)(2,1)S(1)}, bf16[1344,128]{1,0:T(8,128)(2,1)S(1)}, u32[]{:S(2)}, u32[]{:S(2)}) collective-permute-start(bf16[1344,128]{1,0:T(8,128)(2,1)S(1)} %get-tuple-element.27), channel_id=1, source_target_pairs={{0,2},{2,0},{4,6},{6,4},{8,10},{10,8},{12,14},{14,12},{1,3},{3,1},... | collective-permute-start | bytes 1032200 | tf_op jit(solution)/shard_map/ppermute | solution.py:294
  46.8 2.0 %collective-permute-start.22 = (bf16[864,128]{1,0:T(8,128)(2,1)S(1)}, bf16[864,128]{1,0:T(8,128)(2,1)S(1)}, u32[]{:S(2)}, u32[]{:S(2)}) collective-permute-start(bf16[864,128]{1,0:T(8,128)(2,1)S(1)} %multiply_convert_fusion.hidden.source), channel_id=1, source_target_pairs={{0,8},{2,10},{4,12},{6,14},{8,0},{10,2},{12,4},{14,6},{1,9},{3,11}... | collective-permute-start | bytes 663560 | tf_op jit(solution)/shard_map/ppermute | solution.py:294
  48.8 7.0 %collective-permute-done.18.refs_0_.refs_1_.refs_2_._.refs_4_ = bf16[864,128]{1,0:T(8,128)(2,1)S(1)} collective-permute-done((bf16[864,128]{1,0:T(8,128)(2,1)S(1)}, bf16[864,128]{1,0:T(8,128)(2,1)S(1)}, u32[]{:S(2)}, u32[]{:S(2)}) %collective-permute-start.18) | collective-permute-done | bytes 221216 | tf_op jit(solution)/shard_map/ppermute | solution.py:294
  55.8 2.1 %collective-permute-start.31 = (bf16[864,128]{1,0:T(8,128)(2,1)S(1)}, bf16[864,128]{1,0:T(8,128)(2,1)S(1)}, u32[]{:S(2)}, u32[]{:S(2)}) collective-permute-start(bf16[864,128]{1,0:T(8,128)(2,1)S(1)} %shard_map.129.refs_0_), channel_id=1, source_target_pairs={{0,2},{2,0},{4,6},{6,4},{8,10},{10,8},{12,14},{14,12},{1,3},{3,1},... | collective-permute-start | bytes 663560 | tf_op jit(solution)/shard_map/ppermute | solution.py:294
  58.0 0.1 collective-permute-start.34
  58.0 1.9 %collective-permute-done.22.refs_0_ = bf16[864,128]{1,0:T(8,128)(2,1)S(1)} collective-permute-done((bf16[864,128]{1,0:T(8,128)(2,1)S(1)}, bf16[864,128]{1,0:T(8,128)(2,1)S(1)}, u32[]{:S(2)}, u32[]{:S(2)}) %collective-permute-start.22) | collective-permute-done | bytes 221216 | tf_op jit(solution)/shard_map/ppermute | solution.py:294
  60.0 1.5 %collective-permute-start.26 = (bf16[864,128]{1,0:T(8,128)(2,1)S(1)}, bf16[864,128]{1,0:T(8,128)(2,1)S(1)}, u32[]{:S(2)}, u32[]{:S(2)}) collective-permute-start(bf16[864,128]{1,0:T(8,128)(2,1)S(1)} %multiply_convert_fusion.hidden.source), channel_id=1, source_target_pairs={{0,12},{2,14},{4,8},{6,10},{8,4},{10,6},{12,0},{14,2},{1,13},{3,15... | collective-permute-start | bytes 663560 | tf_op jit(solution)/shard_map/ppermute | solution.py:294
  61.5 2.8 %collective-permute-done.31.refs_2_ = bf16[864,128]{1,0:T(8,128)(2,1)S(1)} collective-permute-done((bf16[864,128]{1,0:T(8,128)(2,1)S(1)}, bf16[864,128]{1,0:T(8,128)(2,1)S(1)}, u32[]{:S(2)}, u32[]{:S(2)}) %collective-permute-start.31) | collective-permute-done | bytes 221216 | tf_op jit(solution)/shard_map/ppermute | solution.py:294
  64.2 3.8 %collective-permute-done.34.refs_6_ = bf16[864,128]{1,0:T(8,128)(2,1)S(1)} collective-permute-done((bf16[864,128]{1,0:T(8,128)(2,1)S(1)}, bf16[864,128]{1,0:T(8,128)(2,1)S(1)}, u32[]{:S(2)}, u32[]{:S(2)}) %collective-permute-start.34) | collective-permute-done | bytes 221216 | tf_op jit(solution)/shard_map/ppermute | solution.py:294
  68.0 0.5 collective-permute-start.32
  68.5 0.1 collective-permute-start.35
  68.6 0.6 shard_map.126
  69.2 0.6 shard_map.128.ranked
  69.8 1.8 %collective-permute-start.24 = (bf16[864,128]{1,0:T(8,128)(2,1)S(1)}, bf16[864,128]{1,0:T(8,128)(2,1)S(1)}, u32[]{:S(2)}, u32[]{:S(2)}) collective-permute-start(bf16[864,128]{1,0:T(8,128)(2,1)S(1)} %collective-permute-done.22.refs_0_), channel_id=1, source_target_pairs={{0,2},{2,0},{4,6},{6,4},{8,10},{10,8},{12,14},{14,12},{1,3},{3,1},... | collective-permute-start | bytes 663560 | tf_op jit(solution)/shard_map/ppermute | solution.py:294
  71.6 0.3 collective-permute-start.28
  71.9 0.5 collective-permute-start.19
  72.4 2.3 %collective-permute-start.20 = (bf16[384,128]{1,0:T(8,128)(2,1)S(1)}, bf16[384,128]{1,0:T(8,128)(2,1)S(1)}, u32[]{:S(2)}, u32[]{:S(2)}) collective-permute-start(bf16[384,128]{1,0:T(8,128)(2,1)S(1)} %get-tuple-element.30), channel_id=1, source_target_pairs={{0,8},{2,10},{4,12},{6,14},{8,0},{10,2},{12,4},{14,6},{1,9},{3,11}... | collective-permute-start | bytes 294920 | tf_op jit(solution)/shard_map/ppermute | solution.py:294
  74.7 1.7 %collective-permute-start.21 = (bf16[384,128]{1,0:T(8,128)(2,1)S(1)}, bf16[384,128]{1,0:T(8,128)(2,1)S(1)}, u32[]{:S(2)}, u32[]{:S(2)}) collective-permute-start(bf16[384,128]{1,0:T(8,128)(2,1)S(1)} %get-tuple-element.31), channel_id=1, source_target_pairs={{0,12},{2,14},{4,8},{6,10},{8,4},{10,6},{12,0},{14,2},{1,13},{3,15... | collective-permute-start | bytes 294920 | tf_op jit(solution)/shard_map/ppermute | solution.py:294
  76.3 2.1 %shard_map.130.refs_8_ = bf16[1,64,13824]{2,1,0:T(8,128)(2,1)} custom-call(s32[7]{0:T(128)S(1)} %copy-done.4, bf16[64,128]{1,0:T(8,128)(2,1)S(1)} %shard_map.128.ranked, bf16[864,128]{1,0:T(8,128)(2,1)S(1)} %shard_map.129.refs_0_, bf16[864,128]{1,0:T(8,128)(2,1)S(1)} %collective-permute-done.30.refs_1_, ...), custom_call_target="tpu_custom_call" | custom-call | flops 20000000000 | tf_op jit(solution)/shard_map/pallas_call | solution.py:389
  78.4 0.1 collective-permute-start.23
  78.5 3.9 %collective-permute-done.28.refs_6_ = bf16[864,128]{1,0:T(8,128)(2,1)S(1)} collective-permute-done((bf16[864,128]{1,0:T(8,128)(2,1)S(1)}, bf16[864,128]{1,0:T(8,128)(2,1)S(1)}, u32[]{:S(2)}, u32[]{:S(2)}) %collective-permute-start.28) | collective-permute-done | bytes 221216 | tf_op jit(solution)/shard_map/ppermute | solution.py:294
  82.4 0.5 collective-permute-start.25
  82.9 0.1 collective-permute-start.29
  83.0 2.1 %shard_map.127 = (bf16[320,128]{1,0:T(8,128)(2,1)}, bf16[1,64,5120]{2,1,0:T(8,128)(2,1)}, bf16[64,128]{1,0:T(8,128)(2,1)S(1)}) custom-call(s32[7]{0:T(128)S(1)} %copy-done.4, bf16[2,64,320]{2,1,0:T(8,128)(2,1)S(1)} %copy-done.5, bf16[8,384,128]{2,1,0:T(8,128)(2,1)S(1)} %shard_map.125.gathered, ...), custom_call_target="tpu_custom_call" | custom-call | flops 8000000000 | tf_op jit(solution)/shard_map/pallas_call | solution.py:371
  85.1 2.1 %shard_map.131 = bf16[1,64,13824]{2,1,0:T(8,128)(2,1)} custom-call(s32[7]{0:T(128)S(1)} %copy-done.4, bf16[64,128]{1,0:T(8,128)(2,1)S(1)} %shard_map.128.ranked, bf16[864,128]{1,0:T(8,128)(2,1)S(1)} %collective-permute-done.22.refs_0_, bf16[864,128]{1,0:T(8,128)(2,1)S(1)} %collective-permute-done.23.refs_1_, ...), custom_call_target="tpu_custom_call", output_to_operand_aliasing={{}: (10, {})} | custom-call | flops 20000000000 | tf_op jit(solution)/shard_map/pallas_call | solution.py:389
  (50 shorter events, 0.1 us)
Async XLA Ops:
  0.6 24.0 %copy-start.3 = (bf16[16,2560]{1,0:T(8,128)(2,1)S(1)}, bf16[16,2560]{1,0:T(8,128)(2,1)}, u32[]{:S(2)}) copy-start(bf16[16,2560]{1,0:T(8,128)(2,1)} %refs_0_.1) | copy-start | bytes 245764
  0.6 6.0 %collective-permute-start = (bf16[16,2560]{1,0:T(8,128)(2,1)}, bf16[16,2560]{1,0:T(8,128)(2,1)S(1)}, u32[]{:S(2)}, u32[]{:S(2)}) collective-permute-start(bf16[16,2560]{1,0:T(8,128)(2,1)} %refs_0_.1), channel_id=1, source_target_pairs={{0,4},{2,6},{4,0},{6,2},{8,12},{10,14},{12,8},{14,10},{1,5},{3,7},... | collective-permute-start | bytes 245768 | tf_op jit(solution)/shard_map/ppermute | solution.py:294
  2.3 9.4 %collective-permute-start.3 = (bf16[16,2560]{1,0:T(8,128)(2,1)}, bf16[16,2560]{1,0:T(8,128)(2,1)S(1)}, u32[]{:S(2)}, u32[]{:S(2)}) collective-permute-start(bf16[16,2560]{1,0:T(8,128)(2,1)} %refs_0_.1), channel_id=1, source_target_pairs={{0,8},{2,10},{4,12},{6,14},{8,0},{10,2},{12,4},{14,6},{1,9},{3,11}... | collective-permute-start | bytes 245768 | tf_op jit(solution)/shard_map/ppermute | solution.py:294
  4.9 8.4 %collective-permute-start.5 = (bf16[16,2560]{1,0:T(8,128)(2,1)}, bf16[16,2560]{1,0:T(8,128)(2,1)S(1)}, u32[]{:S(2)}, u32[]{:S(2)}) collective-permute-start(bf16[16,2560]{1,0:T(8,128)(2,1)} %refs_0_.1), channel_id=1, source_target_pairs={{0,12},{2,14},{4,8},{6,10},{8,4},{10,6},{12,0},{14,2},{1,13},{3,15... | collective-permute-start | bytes 245768 | tf_op jit(solution)/shard_map/ppermute | solution.py:294
  5.1 8.6 %collective-permute-start.1 = (bf16[16,2560]{1,0:T(8,128)(2,1)}, bf16[16,2560]{1,0:T(8,128)(2,1)S(1)}, u32[]{:S(2)}, u32[]{:S(2)}) collective-permute-start(bf16[16,2560]{1,0:T(8,128)(2,1)} %refs_0_.1), channel_id=1, source_target_pairs={{0,2},{2,0},{4,6},{6,4},{8,10},{10,8},{12,14},{14,12},{1,3},{3,1},... | collective-permute-start | bytes 245768 | tf_op jit(solution)/shard_map/ppermute | solution.py:294
  6.6 7.1 %collective-permute-start.7 = (bf16[16,2560]{1,0:T(8,128)(2,1)}, bf16[16,2560]{1,0:T(8,128)(2,1)S(1)}, u32[]{:S(2)}, u32[]{:S(2)}) collective-permute-start(bf16[16,2560]{1,0:T(8,128)(2,1)} %refs_0_.1), channel_id=1, source_target_pairs={{0,1},{1,0},{2,3},{3,2},{4,5},{5,4},{6,7},{7,6},{8,9},{9,8},{10,11... | collective-permute-start | bytes 245768 | tf_op jit(solution)/shard_map/ppermute | solution.py:297
  6.6 0.6 copy-start
  10.3 5.5 %collective-permute-start.2 = (bf16[16,2560]{1,0:T(8,128)(2,1)}, bf16[16,2560]{1,0:T(8,128)(2,1)S(1)}, u32[]{:S(2)}, u32[]{:S(2)}) collective-permute-start(bf16[16,2560]{1,0:T(8,128)(2,1)} %get-tuple-element.22), channel_id=1, source_target_pairs={{0,2},{2,0},{4,6},{6,4},{8,10},{10,8},{12,14},{14,12},{1,3},{3,1},... | collective-permute-start | bytes 245768 | tf_op jit(solution)/shard_map/ppermute | solution.py:294
  11.7 5.9 %collective-permute-start.4 = (bf16[16,2560]{1,0:T(8,128)(2,1)S(1)}, bf16[16,2560]{1,0:T(8,128)(2,1)S(1)}, u32[]{:S(2)}, u32[]{:S(2)}) collective-permute-start(bf16[16,2560]{1,0:T(8,128)(2,1)S(1)} %collective-permute-done.3.refs_4_), channel_id=1, source_target_pairs={{0,2},{2,0},{4,6},{6,4},{8,10},{10,8},{12,14},{14,12},{1,3},{3,1},... | collective-permute-start | bytes 245768 | tf_op jit(solution)/shard_map/ppermute | solution.py:294
  13.2 5.8 %collective-permute-start.6 = (bf16[16,2560]{1,0:T(8,128)(2,1)S(1)}, bf16[16,2560]{1,0:T(8,128)(2,1)S(1)}, u32[]{:S(2)}, u32[]{:S(2)}) collective-permute-start(bf16[16,2560]{1,0:T(8,128)(2,1)S(1)} %collective-permute-done.5.refs_6_), channel_id=1, source_target_pairs={{0,2},{2,0},{4,6},{6,4},{8,10},{10,8},{12,14},{14,12},{1,3},{3,1},... | collective-permute-start | bytes 245768 | tf_op jit(solution)/shard_map/ppermute | solution.py:294
  13.7 5.2 %collective-permute-start.8 = (bf16[16,2560]{1,0:T(8,128)(2,1)S(1)}, bf16[16,2560]{1,0:T(8,128)(2,1)S(1)}, u32[]{:S(2)}, u32[]{:S(2)}) collective-permute-start(bf16[16,2560]{1,0:T(8,128)(2,1)S(1)} %collective-permute-done.1.refs_1_), channel_id=1, source_target_pairs={{0,1},{1,0},{2,3},{3,2},{4,5},{5,4},{6,7},{7,6},{8,9},{9,8},{10,11... | collective-permute-start | bytes 245768 | tf_op jit(solution)/shard_map/ppermute | solution.py:297
  13.7 5.7 %collective-permute-start.9 = (bf16[16,2560]{1,0:T(8,128)(2,1)}, bf16[16,2560]{1,0:T(8,128)(2,1)S(1)}, u32[]{:S(2)}, u32[]{:S(2)}) collective-permute-start(bf16[16,2560]{1,0:T(8,128)(2,1)} %get-tuple-element.22), channel_id=1, source_target_pairs={{0,1},{1,0},{2,3},{3,2},{4,5},{5,4},{6,7},{7,6},{8,9},{9,8},{10,11... | collective-permute-start | bytes 245768 | tf_op jit(solution)/shard_map/ppermute | solution.py:297
  15.9 8.7 %collective-permute-start.11 = (bf16[16,2560]{1,0:T(8,128)(2,1)S(1)}, bf16[16,2560]{1,0:T(8,128)(2,1)S(1)}, u32[]{:S(2)}, u32[]{:S(2)}) collective-permute-start(bf16[16,2560]{1,0:T(8,128)(2,1)S(1)} %collective-permute-done.3.refs_4_), channel_id=1, source_target_pairs={{0,1},{1,0},{2,3},{3,2},{4,5},{5,4},{6,7},{7,6},{8,9},{9,8},{10,11... | collective-permute-start | bytes 245768 | tf_op jit(solution)/shard_map/ppermute | solution.py:297
  17.6 6.9 %collective-permute-start.13 = (bf16[16,2560]{1,0:T(8,128)(2,1)S(1)}, bf16[16,2560]{1,0:T(8,128)(2,1)S(1)}, u32[]{:S(2)}, u32[]{:S(2)}) collective-permute-start(bf16[16,2560]{1,0:T(8,128)(2,1)S(1)} %collective-permute-done.5.refs_6_), channel_id=1, source_target_pairs={{0,1},{1,0},{2,3},{3,2},{4,5},{5,4},{6,7},{7,6},{8,9},{9,8},{10,11... | collective-permute-start | bytes 245768 | tf_op jit(solution)/shard_map/ppermute | solution.py:297
  19.0 5.6 %collective-permute-start.10 = (bf16[16,2560]{1,0:T(8,128)(2,1)S(1)}, bf16[16,2560]{1,0:T(8,128)(2,1)S(1)}, u32[]{:S(2)}, u32[]{:S(2)}) collective-permute-start(bf16[16,2560]{1,0:T(8,128)(2,1)S(1)} %collective-permute-done.2.refs_3_), channel_id=1, source_target_pairs={{0,1},{1,0},{2,3},{3,2},{4,5},{5,4},{6,7},{7,6},{8,9},{9,8},{10,11... | collective-permute-start | bytes 245768 | tf_op jit(solution)/shard_map/ppermute | solution.py:297
  19.0 5.6 %collective-permute-start.12 = (bf16[16,2560]{1,0:T(8,128)(2,1)S(1)}, bf16[16,2560]{1,0:T(8,128)(2,1)S(1)}, u32[]{:S(2)}, u32[]{:S(2)}) collective-permute-start(bf16[16,2560]{1,0:T(8,128)(2,1)S(1)} %collective-permute-done.4.refs_5_), channel_id=1, source_target_pairs={{0,1},{1,0},{2,3},{3,2},{4,5},{5,4},{6,7},{7,6},{8,9},{9,8},{10,11... | collective-permute-start | bytes 245768 | tf_op jit(solution)/shard_map/ppermute | solution.py:297
  19.5 5.1 %collective-permute-start.14 = (bf16[16,2560]{1,0:T(8,128)(2,1)S(1)}, bf16[16,2560]{1,0:T(8,128)(2,1)S(1)}, u32[]{:S(2)}, u32[]{:S(2)}) collective-permute-start(bf16[16,2560]{1,0:T(8,128)(2,1)S(1)} %collective-permute-done.6.refs_7_), channel_id=1, source_target_pairs={{0,1},{1,0},{2,3},{3,2},{4,5},{5,4},{6,7},{7,6},{8,9},{9,8},{10,11... | collective-permute-start | bytes 245768 | tf_op jit(solution)/shard_map/ppermute | solution.py:297
  19.6 25.7 %all-to-all-start = ((bf16[8,384,128]{2,1,0:T(8,128)(2,1)}), bf16[8,384,128]{2,1,0:T(8,128)(2,1)S(1)}, u32[]{:S(2)}, u32[]{:S(2)}) async-start(bf16[8,384,128]{2,1,0:T(8,128)(2,1)} %get-tuple-element.21), calls=%async_computation | async-start | bytes 1572864 | tf_op jit(solution)/shard_map/all_to_all | solution.py:323
  24.6 0.9 %copy-start.1 = (bf16[16,2560]{1,0:T(8,128)(2,1)S(1)}, bf16[16,2560]{1,0:T(8,128)(2,1)}, u32[]{:S(2)}) copy-start(bf16[16,2560]{1,0:T(8,128)(2,1)} %copy-done) | copy-start | bytes 245764
  25.5 6.3 %slice-start = ((s8[8847360]{0:T(1024)(128)(4,1)}), s8[4194304]{0:T(1024)(128)(4,1)S(1)}, s32[]{:S(2)}) async-start(s8[8847360]{0:T(1024)(128)(4,1)} %bitcast.12), calls=%async_computation.1 | async-start | bytes 8388608
  25.6 6.2 %slice-start.1 = ((s8[8847360]{0:T(1024)(128)(4,1)}), s8[4194304]{0:T(1024)(128)(4,1)S(1)}, s32[]{:S(2)}) async-start(s8[8847360]{0:T(1024)(128)(4,1)} %bitcast.12), calls=%async_computation.2 | async-start | bytes 8388608
  25.6 6.2 %slice-start.2 = ((s8[8847360]{0:T(1024)(128)(4,1)}), s8[458752]{0:T(1024)(128)(4,1)S(1)}, s32[]{:S(2)}) async-start(s8[8847360]{0:T(1024)(128)(4,1)} %bitcast.12), calls=%async_computation.3 | async-start | bytes 917504
  25.6 8.6 %slice-start.3 = ((s8[8847360]{0:T(1024)(128)(4,1)}), s8[4194304]{0:T(1024)(128)(4,1)S(1)}, s32[]{:S(2)}) async-start(s8[8847360]{0:T(1024)(128)(4,1)} %bitcast.14), calls=%async_computation.4 | async-start | bytes 8388608
  25.6 8.6 %slice-start.4 = ((s8[8847360]{0:T(1024)(128)(4,1)}), s8[4194304]{0:T(1024)(128)(4,1)S(1)}, s32[]{:S(2)}) async-start(s8[8847360]{0:T(1024)(128)(4,1)} %bitcast.14), calls=%async_computation.5 | async-start | bytes 8388608
  31.8 2.5 %slice-start.5 = ((s8[8847360]{0:T(1024)(128)(4,1)}), s8[458752]{0:T(1024)(128)(4,1)S(1)}, s32[]{:S(2)}) async-start(s8[8847360]{0:T(1024)(128)(4,1)} %bitcast.14), calls=%async_computation.6 | async-start | bytes 917504
  34.3 1.6 %copy-start.2 = (bf16[2,64,864]{2,1,0:T(8,128)(2,1)S(1)}, bf16[2,64,864]{2,1,0:T(8,128)(2,1)}, u32[]{:S(2)}) copy-start(bf16[2,64,864]{2,1,0:T(8,128)(2,1)} %get-tuple-element.23.in_blocks) | copy-start | bytes 663556
  34.3 1.6 %copy-start.4 = (s32[7]{0:T(128)S(1)}, s32[7]{0:T(128)}, u32[]{:S(2)}) copy-start(s32[7]{0:T(128)} %get-tuple-element.19.facts) | copy-start | bytes 88
  37.9 2.2 %collective-permute-start.15 = (bf16[2624,128]{1,0:T(8,128)(2,1)S(1)}, bf16[2624,128]{1,0:T(8,128)(2,1)S(1)}, u32[]{:S(2)}, u32[]{:S(2)}) collective-permute-start(bf16[2624,128]{1,0:T(8,128)(2,1)S(1)} %get-tuple-element.25), channel_id=1, source_target_pairs={{0,1},{1,0},{2,3},{3,2},{4,5},{5,4},{6,7},{7,6},{8,9},{9,8},{10,11... | collective-permute-start | bytes 2015240 | tf_op jit(solution)/shard_map/ppermute | solution.py:297
  45.3 23.2 %collective-permute-start.16 = (bf16[8,384,128]{2,1,0:T(8,128)(2,1)S(1)}, bf16[8,384,128]{2,1,0:T(8,128)(2,1)S(1)}, u32[]{:S(2)}, u32[]{:S(2)}) collective-permute-start(bf16[8,384,128]{2,1,0:T(8,128)(2,1)S(1)} %shard_map.125.gathered), channel_id=1, source_target_pairs={{0,1},{1,0},{2,3},{3,2},{4,5},{5,4},{6,7},{7,6},{8,9},{9,8},{10,11... | collective-permute-start | bytes 2359304 | tf_op jit(solution)/shard_map/ppermute | solution.py:297
  45.3 10.5 %collective-permute-start.18 = (bf16[864,128]{1,0:T(8,128)(2,1)S(1)}, bf16[864,128]{1,0:T(8,128)(2,1)S(1)}, u32[]{:S(2)}, u32[]{:S(2)}) collective-permute-start(bf16[864,128]{1,0:T(8,128)(2,1)S(1)} %multiply_convert_fusion.hidden.source), channel_id=1, source_target_pairs={{0,4},{2,6},{4,0},{6,2},{8,12},{10,14},{12,8},{14,10},{1,5},{3,7},... | collective-permute-start | bytes 663560 | tf_op jit(solution)/shard_map/ppermute | solution.py:294
  45.4 22.6 %collective-permute-start.17 = (bf16[1344,128]{1,0:T(8,128)(2,1)S(1)}, bf16[1344,128]{1,0:T(8,128)(2,1)S(1)}, u32[]{:S(2)}, u32[]{:S(2)}) collective-permute-start(bf16[1344,128]{1,0:T(8,128)(2,1)S(1)} %get-tuple-element.27), channel_id=1, source_target_pairs={{0,2},{2,0},{4,6},{6,4},{8,10},{10,8},{12,14},{14,12},{1,3},{3,1},... | collective-permute-start | bytes 1032200 | tf_op jit(solution)/shard_map/ppermute | solution.py:294
  46.8 13.2 %collective-permute-start.22 = (bf16[864,128]{1,0:T(8,128)(2,1)S(1)}, bf16[864,128]{1,0:T(8,128)(2,1)S(1)}, u32[]{:S(2)}, u32[]{:S(2)}) collective-permute-start(bf16[864,128]{1,0:T(8,128)(2,1)S(1)} %multiply_convert_fusion.hidden.source), channel_id=1, source_target_pairs={{0,8},{2,10},{4,12},{6,14},{8,0},{10,2},{12,4},{14,6},{1,9},{3,11}... | collective-permute-start | bytes 663560 | tf_op jit(solution)/shard_map/ppermute | solution.py:294
  55.8 8.4 %collective-permute-start.31 = (bf16[864,128]{1,0:T(8,128)(2,1)S(1)}, bf16[864,128]{1,0:T(8,128)(2,1)S(1)}, u32[]{:S(2)}, u32[]{:S(2)}) collective-permute-start(bf16[864,128]{1,0:T(8,128)(2,1)S(1)} %shard_map.129.refs_0_), channel_id=1, source_target_pairs={{0,2},{2,0},{4,6},{6,4},{8,10},{10,8},{12,14},{14,12},{1,3},{3,1},... | collective-permute-start | bytes 663560 | tf_op jit(solution)/shard_map/ppermute | solution.py:294
  58.0 10.1 %collective-permute-start.34 = (bf16[864,128]{1,0:T(8,128)(2,1)S(1)}, bf16[864,128]{1,0:T(8,128)(2,1)S(1)}, u32[]{:S(2)}, u32[]{:S(2)}) collective-permute-start(bf16[864,128]{1,0:T(8,128)(2,1)S(1)} %collective-permute-done.18.refs_0_.refs_1_.refs_2_._.refs_4_), channel_id=1, source_target_pairs={{0,2},{2,0},{4,6},{6,4},{8,10},{10,8},{12,14},{14,12},{1,3},{3,1},... | collective-permute-start | bytes 663560 | tf_op jit(solution)/shard_map/ppermute | solution.py:294
  60.0 9.9 %collective-permute-start.26 = (bf16[864,128]{1,0:T(8,128)(2,1)S(1)}, bf16[864,128]{1,0:T(8,128)(2,1)S(1)}, u32[]{:S(2)}, u32[]{:S(2)}) collective-permute-start(bf16[864,128]{1,0:T(8,128)(2,1)S(1)} %multiply_convert_fusion.hidden.source), channel_id=1, source_target_pairs={{0,12},{2,14},{4,8},{6,10},{8,4},{10,6},{12,0},{14,2},{1,13},{3,15... | collective-permute-start | bytes 663560 | tf_op jit(solution)/shard_map/ppermute | solution.py:294
  64.2 7.4 %collective-permute-start.30 = (bf16[864,128]{1,0:T(8,128)(2,1)S(1)}, bf16[864,128]{1,0:T(8,128)(2,1)S(1)}, u32[]{:S(2)}, u32[]{:S(2)}) collective-permute-start(bf16[864,128]{1,0:T(8,128)(2,1)S(1)} %shard_map.129.refs_0_), channel_id=1, source_target_pairs={{0,1},{1,0},{2,3},{3,2},{4,5},{5,4},{6,7},{7,6},{8,9},{9,8},{10,11... | collective-permute-start | bytes 663560 | tf_op jit(solution)/shard_map/ppermute | solution.py:297
  68.0 3.9 %collective-permute-start.33 = (bf16[864,128]{1,0:T(8,128)(2,1)S(1)}, bf16[864,128]{1,0:T(8,128)(2,1)S(1)}, u32[]{:S(2)}, u32[]{:S(2)}) collective-permute-start(bf16[864,128]{1,0:T(8,128)(2,1)S(1)} %collective-permute-done.18.refs_0_.refs_1_.refs_2_._.refs_4_), channel_id=1, source_target_pairs={{0,1},{1,0},{2,3},{3,2},{4,5},{5,4},{6,7},{7,6},{8,9},{9,8},{10,11... | collective-permute-start | bytes 663560 | tf_op jit(solution)/shard_map/ppermute | solution.py:297
  68.0 4.4 %collective-permute-start.32 = (bf16[864,128]{1,0:T(8,128)(2,1)S(1)}, bf16[864,128]{1,0:T(8,128)(2,1)S(1)}, u32[]{:S(2)}, u32[]{:S(2)}) collective-permute-start(bf16[864,128]{1,0:T(8,128)(2,1)S(1)} %collective-permute-done.31.refs_2_), channel_id=1, source_target_pairs={{0,1},{1,0},{2,3},{3,2},{4,5},{5,4},{6,7},{7,6},{8,9},{9,8},{10,11... | collective-permute-start | bytes 663560 | tf_op jit(solution)/shard_map/ppermute | solution.py:297
  68.5 6.1 %collective-permute-start.35 = (bf16[864,128]{1,0:T(8,128)(2,1)S(1)}, bf16[864,128]{1,0:T(8,128)(2,1)S(1)}, u32[]{:S(2)}, u32[]{:S(2)}) collective-permute-start(bf16[864,128]{1,0:T(8,128)(2,1)S(1)} %collective-permute-done.34.refs_6_), channel_id=1, source_target_pairs={{0,1},{1,0},{2,3},{3,2},{4,5},{5,4},{6,7},{7,6},{8,9},{9,8},{10,11... | collective-permute-start | bytes 663560 | tf_op jit(solution)/shard_map/ppermute | solution.py:297
  69.8 8.6 %collective-permute-start.24 = (bf16[864,128]{1,0:T(8,128)(2,1)S(1)}, bf16[864,128]{1,0:T(8,128)(2,1)S(1)}, u32[]{:S(2)}, u32[]{:S(2)}) collective-permute-start(bf16[864,128]{1,0:T(8,128)(2,1)S(1)} %collective-permute-done.22.refs_0_), channel_id=1, source_target_pairs={{0,2},{2,0},{4,6},{6,4},{8,10},{10,8},{12,14},{14,12},{1,3},{3,1},... | collective-permute-start | bytes 663560 | tf_op jit(solution)/shard_map/ppermute | solution.py:294
  71.6 10.8 %collective-permute-start.28 = (bf16[864,128]{1,0:T(8,128)(2,1)S(1)}, bf16[864,128]{1,0:T(8,128)(2,1)S(1)}, u32[]{:S(2)}, u32[]{:S(2)}) collective-permute-start(bf16[864,128]{1,0:T(8,128)(2,1)S(1)} %collective-permute-done.26.refs_4_), channel_id=1, source_target_pairs={{0,2},{2,0},{4,6},{6,4},{8,10},{10,8},{12,14},{14,12},{1,3},{3,1},... | collective-permute-start | bytes 663560 | tf_op jit(solution)/shard_map/ppermute | solution.py:294
  71.9 10.5 %collective-permute-start.19 = (bf16[384,128]{1,0:T(8,128)(2,1)S(1)}, bf16[384,128]{1,0:T(8,128)(2,1)S(1)}, u32[]{:S(2)}, u32[]{:S(2)}) collective-permute-start(bf16[384,128]{1,0:T(8,128)(2,1)S(1)} %get-tuple-element.29), channel_id=1, source_target_pairs={{0,4},{2,6},{4,0},{6,2},{8,12},{10,14},{12,8},{14,10},{1,5},{3,7},... | collective-permute-start | bytes 294920 | tf_op jit(solution)/shard_map/ppermute | solution.py:294
  72.4 10.5 %collective-permute-start.20 = (bf16[384,128]{1,0:T(8,128)(2,1)S(1)}, bf16[384,128]{1,0:T(8,128)(2,1)S(1)}, u32[]{:S(2)}, u32[]{:S(2)}) collective-permute-start(bf16[384,128]{1,0:T(8,128)(2,1)S(1)} %get-tuple-element.30), channel_id=1, source_target_pairs={{0,8},{2,10},{4,12},{6,14},{8,0},{10,2},{12,4},{14,6},{1,9},{3,11}... | collective-permute-start | bytes 294920 | tf_op jit(solution)/shard_map/ppermute | solution.py:294
  74.7 8.3 %copy-start.5 = (bf16[2,64,320]{2,1,0:T(8,128)(2,1)S(1)}, bf16[2,64,320]{2,1,0:T(8,128)(2,1)}, u32[]{:S(2)}) copy-start(bf16[2,64,320]{2,1,0:T(8,128)(2,1)} %get-tuple-element.20.out_blocks) | copy-start | bytes 245764
  74.7 8.3 %collective-permute-start.21 = (bf16[384,128]{1,0:T(8,128)(2,1)S(1)}, bf16[384,128]{1,0:T(8,128)(2,1)S(1)}, u32[]{:S(2)}, u32[]{:S(2)}) collective-permute-start(bf16[384,128]{1,0:T(8,128)(2,1)S(1)} %get-tuple-element.31), channel_id=1, source_target_pairs={{0,12},{2,14},{4,8},{6,10},{8,4},{10,6},{12,0},{14,2},{1,13},{3,15... | collective-permute-start | bytes 294920 | tf_op jit(solution)/shard_map/ppermute | solution.py:294
  78.4 6.6 %collective-permute-start.23 = (bf16[864,128]{1,0:T(8,128)(2,1)S(1)}, bf16[864,128]{1,0:T(8,128)(2,1)S(1)}, u32[]{:S(2)}, u32[]{:S(2)}) collective-permute-start(bf16[864,128]{1,0:T(8,128)(2,1)S(1)} %collective-permute-done.22.refs_0_), channel_id=1, source_target_pairs={{0,1},{1,0},{2,3},{3,2},{4,5},{5,4},{6,7},{7,6},{8,9},{9,8},{10,11... | collective-permute-start | bytes 663560 | tf_op jit(solution)/shard_map/ppermute | solution.py:297
  82.4 2.7 %collective-permute-start.27 = (bf16[864,128]{1,0:T(8,128)(2,1)S(1)}, bf16[864,128]{1,0:T(8,128)(2,1)S(1)}, u32[]{:S(2)}, u32[]{:S(2)}) collective-permute-start(bf16[864,128]{1,0:T(8,128)(2,1)S(1)} %collective-permute-done.26.refs_4_), channel_id=1, source_target_pairs={{0,1},{1,0},{2,3},{3,2},{4,5},{5,4},{6,7},{7,6},{8,9},{9,8},{10,11... | collective-permute-start | bytes 663560 | tf_op jit(solution)/shard_map/ppermute | solution.py:297
  82.4 2.7 %collective-permute-start.25 = (bf16[864,128]{1,0:T(8,128)(2,1)S(1)}, bf16[864,128]{1,0:T(8,128)(2,1)S(1)}, u32[]{:S(2)}, u32[]{:S(2)}) collective-permute-start(bf16[864,128]{1,0:T(8,128)(2,1)S(1)} %collective-permute-done.24.refs_2_), channel_id=1, source_target_pairs={{0,1},{1,0},{2,3},{3,2},{4,5},{5,4},{6,7},{7,6},{8,9},{9,8},{10,11... | collective-permute-start | bytes 663560 | tf_op jit(solution)/shard_map/ppermute | solution.py:297
  82.9 2.2 %collective-permute-start.29 = (bf16[864,128]{1,0:T(8,128)(2,1)S(1)}, bf16[864,128]{1,0:T(8,128)(2,1)S(1)}, u32[]{:S(2)}, u32[]{:S(2)}) collective-permute-start(bf16[864,128]{1,0:T(8,128)(2,1)S(1)} %collective-permute-done.28.refs_6_), channel_id=1, source_target_pairs={{0,1},{1,0},{2,3},{3,2},{4,5},{5,4},{6,7},{7,6},{8,9},{9,8},{10,11... | collective-permute-start | bytes 663560 | tf_op jit(solution)/shard_map/ppermute | solution.py:297

commit v5 on v4

--- a/solution.py
+++ b/solution.py
@@ -11,7 +11,8 @@
 
 ROWS_BY_ROWS = (((1,), (1,)), ((), ()))
 ASSEMBLE_FLOPS = 0
-GRAD_FLOPS = 20000000000
+FIRST_FLOPS = 20000000000
+LAST_FLOPS = 20000000000
 FINAL_FLOPS = 8000000000
 ADD_FLOPS = 0
 PAIR_FLOPS = 0
@@ -195,8 +196,8 @@
         out[columns:] = low
 
 
-def final_body(facts, out_blocks, gathered, gathered_other, *refs):
-    facts, arrived, (mixed, grad, ranked, features) = Facts(facts), refs[:-4], refs[-4:]
+def final_body(facts, out_blocks, features, *refs):
+    facts, arrived, (mixed, grad, ranked) = Facts(facts), refs[:-3], refs[-3:]
     columns, token_count = mixed.shape
     total = arrived[0][...].astype(jnp.float32)
     for share in arrived[1:]:
@@ -215,10 +216,6 @@
     mixed[...] = (total[:columns] + lowrank_adapter_scale * contribution).astype(mixed.dtype)
     chosen = facts.chosen(token_count) & facts.live(token_count)
     ranked[...] = jnp.where(chosen, low, 0.0).astype(ranked.dtype)
-    for half, pieces in ((facts.core, gathered), (1 - facts.core, gathered_other)):
-        for b in range(pieces.shape[0]):
-            here = pl.ds(pl.multiple_of((2 * b + half) * columns, 16), columns)
-            features[here] = pieces[b, :columns]
     total = lax.dot_general(
         ranked[...], features[...], ROWS_BY_ROWS, preferred_element_type=jnp.float32
     )
@@ -233,14 +230,19 @@
     pass
 
 
-def back_body(facts, gathered, gathered_other, ranked):
+def back_body(facts, gathered, gathered_other, features, ranked):
     back = jnp.zeros(ranked.shape, jnp.float32)
     first = gathered.shape[1] - ranked.shape[0]
     for pieces in (gathered, gathered_other):
         for b in range(pieces.shape[0]):
             back = back + pieces[b, first:].astype(jnp.float32)
-    chosen = Facts(facts).chosen(ranked.shape[1])
+    facts = Facts(facts)
+    chosen = facts.chosen(ranked.shape[1])
     ranked[...] = jnp.where(chosen, back, 0.0).astype(ranked.dtype)
+    for half, pieces in ((facts.core, gathered), (1 - facts.core, gathered_other)):
+        for b in range(pieces.shape[0]):
+            here = pl.ds(pl.multiple_of((2 * b + half) * first, 16), first)
+            features[here] = pieces[b, :first]
 
 
 def in_grad_body(facts, ranked, *refs, flips):
@@ -368,16 +370,17 @@
         flops=PAIR_FLOPS,
     )(facts, stays, flip(leaving, 1), line[2], line[2], line[2])
     shares = [shares[0]] + [flip(shares[z], 2 * z) for z in (1, 2, 3)]
+    cot_all, back_chosen = kernel_call(
+        back_body,
+        [array(model_width, token_count), array(rank, token_count)],
+        [IN_SMEM] + [IN_VMEM] * 2,
+    )(facts, gathered, gathered_other)
     mixed, grad_out, low_chosen = kernel_call(
         final_body,
         [array(columns, token_count), array(1, rank, model_width), array(rank, token_count)],
-        [IN_SMEM] + [IN_VMEM] * 7,
-        scratch=[pltpu.VMEM((model_width, token_count), bf16)],
+        [IN_SMEM] + [IN_VMEM] * 6,
         flops=FINAL_FLOPS,
-    )(facts, out_blocks, gathered, gathered_other, *shares)
-    back_chosen = kernel_call(back_body, array(rank, token_count), [IN_SMEM] + [IN_VMEM] * 2)(
-        facts, gathered, gathered_other
-    )
+    )(facts, out_blocks, cot_all, *shares)
     grad_in = None
     for flips in ((0, 2), (4, 6)):
         order = [p for k in flips for p in (k, k ^ 1)]
@@ -397,7 +400,7 @@
             ],
             out_specs=IN_HBM,
             aliases=aliases,
-            flops=GRAD_FLOPS,
+            flops=LAST_FLOPS if last else FIRST_FLOPS,
         )(facts, back_chosen, *pieces, *last)
     return mixed.T, grad_in, grad_out
 

time: 88.9 us -> 88.4 us (level)
  no operation moved by 1% of the time
where the time goes in v5:
time: 88.4 us; the launch traced here: 86.6 us
  waiting for transfers between devices  30.8 us (35%)
  starting transfers between devices  29.8 us (34%)
  Pallas kernels  13.4 us (15%)
  matrix products  10.1 us (11%)
  local copies, waits for them, and re-layouts  1.57 us (2%)
  between operations  0.98 us (1%)
    ppermute x18, waiting for transfers between devices, flip(): return lax.ppermute(piece, 'batch', [(i, i ^ k) for i in range(8)])  24.6 us
    ppermute x18, starting transfers between devices, flip(): return lax.ppermute(piece, 'batch', [(i, i ^ k) for i in range(8)])  22.5 us
    dot_general x1, matrix products, on_chips(): lax.dot_general(gate_weight.T, rows, ROWS_BY_ROWS, preferred_element_type...  6.1 us
    all_to_all x1, starting transfers between devices, on_chips(): lax.all_to_all(cot_and_back, 'batch', split_axis=0, concat_axis=0, tiled=...  4.97 us
    pallas_call x2, Pallas kernels, on_chips(): kernel_call(functools.partial(in_grad_body, flips=flips), array(1, rank,...  4.19 us
    all_to_all x1, waiting for transfers between devices, on_chips(): lax.all_to_all(cot_and_back, 'batch', split_axis=0, concat_axis=0, tiled=...  4.11 us
    pallas_call x1, Pallas kernels, on_chips(): kernel_call(prepare_body, [jax.ShapeDtypeStruct((3 + 2 * block_count,), j...  3.06 us
    dot_general x1, matrix products, on_chips(): lax.dot_general(up_weight.T, rows, ROWS_BY_ROWS, preferred_element_type=f32)  2.45 us
  transfers between devices with their start and end apart: 37, of which 11 were waited for; matrix products, arithmetic and copies ran while one was open for 12% of the time, Pallas kernels for 13%

profile of v5, /device:TPU:2, one launch (start us, length us, event | category | flops | bytes accessed | tf_op | source)
XLA Modules:
  0.0 86.6 jit_solution(4632395978001235820)
XLA Ops:
  0.6 1.6 %collective-permute-start = (bf16[16,2560]{1,0:T(8,128)(2,1)}, bf16[16,2560]{1,0:T(8,128)(2,1)S(1)}, u32[]{:S(2)}, u32[]{:S(2)}) collective-permute-start(bf16[16,2560]{1,0:T(8,128)(2,1)} %refs_0_.1), channel_id=1, source_target_pairs={{0,4},{2,6},{4,0},{6,2},{8,12},{10,14},{12,8},{14,10},{1,5},{3,7},... | collective-permute-start | bytes 245768 | tf_op jit(solution)/shard_map/ppermute | solution.py:296
  2.3 2.6 %collective-permute-start.3 = (bf16[16,2560]{1,0:T(8,128)(2,1)}, bf16[16,2560]{1,0:T(8,128)(2,1)S(1)}, u32[]{:S(2)}, u32[]{:S(2)}) collective-permute-start(bf16[16,2560]{1,0:T(8,128)(2,1)} %refs_0_.1), channel_id=1, source_target_pairs={{0,8},{2,10},{4,12},{6,14},{8,0},{10,2},{12,4},{14,6},{1,9},{3,11}... | collective-permute-start | bytes 245768 | tf_op jit(solution)/shard_map/ppermute | solution.py:296
  4.9 0.2 collective-permute-start.5
  5.1 1.5 %collective-permute-start.1 = (bf16[16,2560]{1,0:T(8,128)(2,1)}, bf16[16,2560]{1,0:T(8,128)(2,1)S(1)}, u32[]{:S(2)}, u32[]{:S(2)}) collective-permute-start(bf16[16,2560]{1,0:T(8,128)(2,1)} %refs_0_.1), channel_id=1, source_target_pairs={{0,2},{2,0},{4,6},{6,4},{8,10},{10,8},{12,14},{14,12},{1,3},{3,1},... | collective-permute-start | bytes 245768 | tf_op jit(solution)/shard_map/ppermute | solution.py:296
  6.6 0.0 collective-permute-start.7
  6.6 0.0 collective-permute-done.piece.refs_2_
  6.6 0.6 copy-done
  7.3 3.1 %shard_map.121 = (s32[7]{0:T(128)}, bf16[8,384,128]{2,1,0:T(8,128)(2,1)}, bf16[2,64,320]{2,1,0:T(8,128)(2,1)}, bf16[2,64,864]{2,1,0:T(8,128)(2,1)}, bf16[16,2560]{1,0:T(8,128)(2,1)}) custom-call(s32[2]{0:T(128)} %owner.1, s32[2]{0:T(128)} %length.1, s32[16]{0:T(128)} %placement.1, bf16[16,64,320]{2,1,0:T(8,128)(2,1)} %adapter_out.1, ...), custom_call_target="tpu_custom_call" | custom-call | tf_op jit(solution)/shard_map/pallas_call | solution.py:309
  10.3 0.6 collective-permute-start.2
  10.9 0.8 collective-permute-done.3.refs_4_
  11.7 0.0 collective-permute-done.5.refs_6_
  11.7 1.5 %collective-permute-start.4 = (bf16[16,2560]{1,0:T(8,128)(2,1)S(1)}, bf16[16,2560]{1,0:T(8,128)(2,1)S(1)}, u32[]{:S(2)}, u32[]{:S(2)}) collective-permute-start(bf16[16,2560]{1,0:T(8,128)(2,1)S(1)} %collective-permute-done.3.refs_4_), channel_id=1, source_target_pairs={{0,2},{2,0},{4,6},{6,4},{8,10},{10,8},{12,14},{14,12},{1,3},{3,1},... | collective-permute-start | bytes 245768 | tf_op jit(solution)/shard_map/ppermute | solution.py:296
  13.2 0.0 collective-permute-done.1.refs_1_
  13.2 0.5 collective-permute-start.6
  13.7 2.1 %collective-permute-done.2.refs_3_ = bf16[16,2560]{1,0:T(8,128)(2,1)S(1)} collective-permute-done((bf16[16,2560]{1,0:T(8,128)(2,1)}, bf16[16,2560]{1,0:T(8,128)(2,1)S(1)}, u32[]{:S(2)}, u32[]{:S(2)}) %collective-permute-start.2) | collective-permute-done | bytes 81952 | tf_op jit(solution)/shard_map/ppermute | solution.py:296
  15.8 0.0 collective-permute-start.13
  15.9 0.0 collective-permute-done.9.refs_10_
  15.9 0.5 collective-permute-start.8
  16.4 1.2 %collective-permute-done.4.refs_5_ = bf16[16,2560]{1,0:T(8,128)(2,1)S(1)} collective-permute-done((bf16[16,2560]{1,0:T(8,128)(2,1)S(1)}, bf16[16,2560]{1,0:T(8,128)(2,1)S(1)}, u32[]{:S(2)}, u32[]{:S(2)}) %collective-permute-start.4) | collective-permute-done | bytes 81952 | tf_op jit(solution)/shard_map/ppermute | solution.py:296
  17.6 1.4 %collective-permute-done.6.refs_7_ = bf16[16,2560]{1,0:T(8,128)(2,1)S(1)} collective-permute-done((bf16[16,2560]{1,0:T(8,128)(2,1)S(1)}, bf16[16,2560]{1,0:T(8,128)(2,1)S(1)}, u32[]{:S(2)}, u32[]{:S(2)}) %collective-permute-start.6) | collective-permute-done | bytes 81952 | tf_op jit(solution)/shard_map/ppermute | solution.py:296
  19.0 0.5 collective-permute-start.14
  19.5 5.0 %all-to-all-start = ((bf16[8,384,128]{2,1,0:T(8,128)(2,1)}), bf16[8,384,128]{2,1,0:T(8,128)(2,1)S(1)}, u32[]{:S(2)}, u32[]{:S(2)}) async-start(bf16[8,384,128]{2,1,0:T(8,128)(2,1)} %get-tuple-element.23), calls=%async_computation | async-start | bytes 1572864 | tf_op jit(solution)/shard_map/all_to_all | solution.py:325
  24.5 0.0 copy-start.1
  24.5 0.9 %copy-done.1 = bf16[16,2560]{1,0:T(8,128)(2,1)S(1)} copy-done((bf16[16,2560]{1,0:T(8,128)(2,1)S(1)}, bf16[16,2560]{1,0:T(8,128)(2,1)}, u32[]{:S(2)}) %copy-start.1) | copy-done | bytes 81944
  25.4 0.1 shard_map.122
  25.5 0.0 slice-start.1
  25.6 0.0 slice-start.3
  25.6 0.0 slice-start.4
  25.6 6.1 %convolution_bitcast_fusion.1 = f32[864,128]{1,0:T(8,128)S(1)} fusion(bf16[128,5120]{1,0:T(8,128)(2,1)S(1)} %shard_map.122, bf16[5120,864]{0,1:T(8,128)(2,1)} %param.11), kind=kOutput, calls=%fused_computation.2 | convolution fusion | flops 1132462080 | bytes 10600448 | tf_op jit(solution)/shard_map/dot_general | solution.py:334
  31.7 0.0 slice-start.5
  31.7 2.5 %multiply_convert_fusion.hidden.source = bf16[864,128]{1,0:T(8,128)(2,1)S(1)} fusion(f32[864,128]{1,0:T(8,128)S(1)} %convolution_bitcast_fusion.1, bf16[128,5120]{1,0:T(8,128)(2,1)S(1)} %shard_map.122, bf16[5120,864]{0,1:T(8,128)(2,1)S(1)} %bitcast.13), kind=kOutput, calls=%fused_computation.3 | convolution fusion | flops 1133125632 | bytes 10821632 | tf_op jit(solution)/shard_map/dot_general | solution.py:335
  34.2 0.0 copy-start.2
  34.3 1.6 %convolution_convert_fusion.base = bf16[128,5120]{1,0:T(8,128)(2,1)S(1)} fusion(bf16[864,128]{1,0:T(8,128)(2,1)S(1)} %multiply_convert_fusion.hidden.source, bf16[864,5120]{1,0:T(8,128)(2,1)S(1)} %bitcast.15), kind=kOutput, calls=%fused_computation | convolution fusion | flops 1133117440 | bytes 10379264 | tf_op jit(solution)/shard_map/dot_general | solution.py:337
  35.8 2.0 %shard_map.123 = (bf16[2624,128]{1,0:T(8,128)(2,1)S(1)}, bf16[2624,128]{1,0:T(8,128)(2,1)S(1)}) custom-call(s32[7]{0:T(128)S(1)} %copy-done.4, bf16[128,5120]{1,0:T(8,128)(2,1)S(1)} %convolution_convert_fusion.base, bf16[864,128]{1,0:T(8,128)(2,1)S(1)} %multiply_convert_fusion.hidden.source, bf16[2,64,864]{2,1,0:T(8,128)(2,1)S(1)} %copy-done.2), custom_call_target="tpu_custom_call" | custom-call | tf_op jit(solution)/shard_map/pallas_call | solution.py:340
  37.8 0.1 collective-permute-start.15
  37.9 2.1 %collective-permute-done.15.arrived = bf16[2624,128]{1,0:T(8,128)(2,1)S(1)} collective-permute-done((bf16[2624,128]{1,0:T(8,128)(2,1)S(1)}, bf16[2624,128]{1,0:T(8,128)(2,1)S(1)}, u32[]{:S(2)}, u32[]{:S(2)}) %collective-permute-start.15) | collective-permute-done | bytes 671776 | tf_op jit(solution)/shard_map/ppermute | solution.py:299
  40.0 0.7 shard_map.124
  40.7 4.1 %all-to-all-done.refs_0_ = bf16[8,384,128]{2,1,0:T(8,128)(2,1)S(1)} async-done(((bf16[8,384,128]{2,1,0:T(8,128)(2,1)}), bf16[8,384,128]{2,1,0:T(8,128)(2,1)S(1)}, u32[]{:S(2)}, u32[]{:S(2)}) %all-to-all-start) | async-done | bytes 786464 | tf_op jit(solution)/shard_map/all_to_all | solution.py:325
  44.8 0.3 collective-permute-start.18
  45.1 1.1 %collective-permute-start.17 = (bf16[1344,128]{1,0:T(8,128)(2,1)S(1)}, bf16[1344,128]{1,0:T(8,128)(2,1)S(1)}, u32[]{:S(2)}, u32[]{:S(2)}) collective-permute-start(bf16[1344,128]{1,0:T(8,128)(2,1)S(1)} %get-tuple-element.30), channel_id=1, source_target_pairs={{0,2},{2,0},{4,6},{6,4},{8,10},{10,8},{12,14},{14,12},{1,3},{3,1},... | collective-permute-start | bytes 1032200 | tf_op jit(solution)/shard_map/ppermute | solution.py:296
  46.3 2.0 %collective-permute-start.22 = (bf16[864,128]{1,0:T(8,128)(2,1)S(1)}, bf16[864,128]{1,0:T(8,128)(2,1)S(1)}, u32[]{:S(2)}, u32[]{:S(2)}) collective-permute-start(bf16[864,128]{1,0:T(8,128)(2,1)S(1)} %multiply_convert_fusion.hidden.source), channel_id=1, source_target_pairs={{0,8},{2,10},{4,12},{6,14},{8,0},{10,2},{12,4},{14,6},{1,9},{3,11}... | collective-permute-start | bytes 663560 | tf_op jit(solution)/shard_map/ppermute | solution.py:296
  48.2 6.6 %collective-permute-done.18.refs_0_.refs_1_.refs_2_._.refs_4_ = bf16[864,128]{1,0:T(8,128)(2,1)S(1)} collective-permute-done((bf16[864,128]{1,0:T(8,128)(2,1)S(1)}, bf16[864,128]{1,0:T(8,128)(2,1)S(1)}, u32[]{:S(2)}, u32[]{:S(2)}) %collective-permute-start.18) | collective-permute-done | bytes 221216 | tf_op jit(solution)/shard_map/ppermute | solution.py:296
  54.8 2.5 %collective-permute-start.31 = (bf16[864,128]{1,0:T(8,128)(2,1)S(1)}, bf16[864,128]{1,0:T(8,128)(2,1)S(1)}, u32[]{:S(2)}, u32[]{:S(2)}) collective-permute-start(bf16[864,128]{1,0:T(8,128)(2,1)S(1)} %shard_map.129.refs_0_), channel_id=1, source_target_pairs={{0,2},{2,0},{4,6},{6,4},{8,10},{10,8},{12,14},{14,12},{1,3},{3,1},... | collective-permute-start | bytes 663560 | tf_op jit(solution)/shard_map/ppermute | solution.py:296
  57.3 0.1 collective-permute-start.34
  57.4 2.1 %collective-permute-done.22.refs_0_ = bf16[864,128]{1,0:T(8,128)(2,1)S(1)} collective-permute-done((bf16[864,128]{1,0:T(8,128)(2,1)S(1)}, bf16[864,128]{1,0:T(8,128)(2,1)S(1)}, u32[]{:S(2)}, u32[]{:S(2)}) %collective-permute-start.22) | collective-permute-done | bytes 221216 | tf_op jit(solution)/shard_map/ppermute | solution.py:296
  59.5 1.4 %collective-permute-start.26 = (bf16[864,128]{1,0:T(8,128)(2,1)S(1)}, bf16[864,128]{1,0:T(8,128)(2,1)S(1)}, u32[]{:S(2)}, u32[]{:S(2)}) collective-permute-start(bf16[864,128]{1,0:T(8,128)(2,1)S(1)} %multiply_convert_fusion.hidden.source), channel_id=1, source_target_pairs={{0,12},{2,14},{4,8},{6,10},{8,4},{10,6},{12,0},{14,2},{1,13},{3,15... | collective-permute-start | bytes 663560 | tf_op jit(solution)/shard_map/ppermute | solution.py:296
  60.9 2.7 %collective-permute-done.31.refs_2_ = bf16[864,128]{1,0:T(8,128)(2,1)S(1)} collective-permute-done((bf16[864,128]{1,0:T(8,128)(2,1)S(1)}, bf16[864,128]{1,0:T(8,128)(2,1)S(1)}, u32[]{:S(2)}, u32[]{:S(2)}) %collective-permute-start.31) | collective-permute-done | bytes 221216 | tf_op jit(solution)/shard_map/ppermute | solution.py:296
  63.6 3.8 %collective-permute-done.34.refs_6_ = bf16[864,128]{1,0:T(8,128)(2,1)S(1)} collective-permute-done((bf16[864,128]{1,0:T(8,128)(2,1)S(1)}, bf16[864,128]{1,0:T(8,128)(2,1)S(1)}, u32[]{:S(2)}, u32[]{:S(2)}) %collective-permute-start.34) | collective-permute-done | bytes 221216 | tf_op jit(solution)/shard_map/ppermute | solution.py:296
  67.4 0.5 collective-permute-start.32
  67.9 0.1 collective-permute-start.35
  68.0 0.6 shard_map.127
  68.6 0.7 shard_map.126
  69.3 1.8 %collective-permute-start.24 = (bf16[864,128]{1,0:T(8,128)(2,1)S(1)}, bf16[864,128]{1,0:T(8,128)(2,1)S(1)}, u32[]{:S(2)}, u32[]{:S(2)}) collective-permute-start(bf16[864,128]{1,0:T(8,128)(2,1)S(1)} %collective-permute-done.22.refs_0_), channel_id=1, source_target_pairs={{0,2},{2,0},{4,6},{6,4},{8,10},{10,8},{12,14},{14,12},{1,3},{3,1},... | collective-permute-start | bytes 663560 | tf_op jit(solution)/shard_map/ppermute | solution.py:296
  71.1 0.3 collective-permute-start.28
  71.4 0.1 collective-permute-start.19
  71.5 2.8 %collective-permute-start.20 = (bf16[384,128]{1,0:T(8,128)(2,1)S(1)}, bf16[384,128]{1,0:T(8,128)(2,1)S(1)}, u32[]{:S(2)}, u32[]{:S(2)}) collective-permute-start(bf16[384,128]{1,0:T(8,128)(2,1)S(1)} %get-tuple-element.33), channel_id=1, source_target_pairs={{0,8},{2,10},{4,12},{6,14},{8,0},{10,2},{12,4},{14,6},{1,9},{3,11}... | collective-permute-start | bytes 294920 | tf_op jit(solution)/shard_map/ppermute | solution.py:296
  74.4 1.5 %collective-permute-start.21 = (bf16[384,128]{1,0:T(8,128)(2,1)S(1)}, bf16[384,128]{1,0:T(8,128)(2,1)S(1)}, u32[]{:S(2)}, u32[]{:S(2)}) collective-permute-start(bf16[384,128]{1,0:T(8,128)(2,1)S(1)} %get-tuple-element.34), channel_id=1, source_target_pairs={{0,12},{2,14},{4,8},{6,10},{8,4},{10,6},{12,0},{14,2},{1,13},{3,15... | collective-permute-start | bytes 294920 | tf_op jit(solution)/shard_map/ppermute | solution.py:296
  75.8 2.1 %shard_map.130.refs_8_ = bf16[1,64,13824]{2,1,0:T(8,128)(2,1)} custom-call(s32[7]{0:T(128)S(1)} %copy-done.4, bf16[64,128]{1,0:T(8,128)(2,1)S(1)} %get-tuple-element.36.ranked, bf16[864,128]{1,0:T(8,128)(2,1)S(1)} %shard_map.129.refs_0_, bf16[864,128]{1,0:T(8,128)(2,1)S(1)} %collective-permute-done.30.refs_1_, ...), custom_call_target="tpu_custom_call" | custom-call | flops 20000000000 | tf_op jit(solution)/shard_map/pallas_call | solution.py:392
  77.9 0.1 collective-permute-start.23
  78.0 3.9 %collective-permute-done.28.refs_6_ = bf16[864,128]{1,0:T(8,128)(2,1)S(1)} collective-permute-done((bf16[864,128]{1,0:T(8,128)(2,1)S(1)}, bf16[864,128]{1,0:T(8,128)(2,1)S(1)}, u32[]{:S(2)}, u32[]{:S(2)}) %collective-permute-start.28) | collective-permute-done | bytes 221216 | tf_op jit(solution)/shard_map/ppermute | solution.py:296
  81.9 0.5 collective-permute-start.25
  82.4 0.1 collective-permute-start.29
  82.5 2.0 %shard_map.128 = (bf16[320,128]{1,0:T(8,128)(2,1)}, bf16[1,64,5120]{2,1,0:T(8,128)(2,1)}, bf16[64,128]{1,0:T(8,128)(2,1)S(1)}) custom-call(s32[7]{0:T(128)S(1)} %copy-done.4, bf16[2,64,320]{2,1,0:T(8,128)(2,1)S(1)} %copy-done.5, bf16[5120,128]{1,0:T(8,128)(2,1)S(1)} %get-tuple-element.29.features, bf16[384,128]{1,0:T(8,128)(2,1)S(1)} %get-tuple-element.31.refs_0_, ...), custom_call_target="tpu_custom_call" | custom-call | flops 8000000000 | tf_op jit(solution)/shard_map/pallas_call | solution.py:378
  84.5 2.1 %shard_map.131 = bf16[1,64,13824]{2,1,0:T(8,128)(2,1)} custom-call(s32[7]{0:T(128)S(1)} %copy-done.4, bf16[64,128]{1,0:T(8,128)(2,1)S(1)} %get-tuple-element.36.ranked, bf16[864,128]{1,0:T(8,128)(2,1)S(1)} %collective-permute-done.22.refs_0_, bf16[864,128]{1,0:T(8,128)(2,1)S(1)} %collective-permute-done.23.refs_1_, ...), custom_call_target="tpu_custom_call", output_to_operand_aliasing={{}: (10, {})} | custom-call | flops 20000000000 | tf_op jit(solution)/shard_map/pallas_call | solution.py:392
  (50 shorter events, 0.1 us)
Async XLA Ops:
  0.6 23.9 %copy-start.3 = (bf16[16,2560]{1,0:T(8,128)(2,1)S(1)}, bf16[16,2560]{1,0:T(8,128)(2,1)}, u32[]{:S(2)}) copy-start(bf16[16,2560]{1,0:T(8,128)(2,1)} %refs_0_.1) | copy-start | bytes 245764
  0.6 6.0 %collective-permute-start = (bf16[16,2560]{1,0:T(8,128)(2,1)}, bf16[16,2560]{1,0:T(8,128)(2,1)S(1)}, u32[]{:S(2)}, u32[]{:S(2)}) collective-permute-start(bf16[16,2560]{1,0:T(8,128)(2,1)} %refs_0_.1), channel_id=1, source_target_pairs={{0,4},{2,6},{4,0},{6,2},{8,12},{10,14},{12,8},{14,10},{1,5},{3,7},... | collective-permute-start | bytes 245768 | tf_op jit(solution)/shard_map/ppermute | solution.py:296
  2.3 9.4 %collective-permute-start.3 = (bf16[16,2560]{1,0:T(8,128)(2,1)}, bf16[16,2560]{1,0:T(8,128)(2,1)S(1)}, u32[]{:S(2)}, u32[]{:S(2)}) collective-permute-start(bf16[16,2560]{1,0:T(8,128)(2,1)} %refs_0_.1), channel_id=1, source_target_pairs={{0,8},{2,10},{4,12},{6,14},{8,0},{10,2},{12,4},{14,6},{1,9},{3,11}... | collective-permute-start | bytes 245768 | tf_op jit(solution)/shard_map/ppermute | solution.py:296
  4.9 6.8 %collective-permute-start.5 = (bf16[16,2560]{1,0:T(8,128)(2,1)}, bf16[16,2560]{1,0:T(8,128)(2,1)S(1)}, u32[]{:S(2)}, u32[]{:S(2)}) collective-permute-start(bf16[16,2560]{1,0:T(8,128)(2,1)} %refs_0_.1), channel_id=1, source_target_pairs={{0,12},{2,14},{4,8},{6,10},{8,4},{10,6},{12,0},{14,2},{1,13},{3,15... | collective-permute-start | bytes 245768 | tf_op jit(solution)/shard_map/ppermute | solution.py:296
  5.1 8.1 %collective-permute-start.1 = (bf16[16,2560]{1,0:T(8,128)(2,1)}, bf16[16,2560]{1,0:T(8,128)(2,1)S(1)}, u32[]{:S(2)}, u32[]{:S(2)}) collective-permute-start(bf16[16,2560]{1,0:T(8,128)(2,1)} %refs_0_.1), channel_id=1, source_target_pairs={{0,2},{2,0},{4,6},{6,4},{8,10},{10,8},{12,14},{14,12},{1,3},{3,1},... | collective-permute-start | bytes 245768 | tf_op jit(solution)/shard_map/ppermute | solution.py:296
  6.6 7.1 %collective-permute-start.7 = (bf16[16,2560]{1,0:T(8,128)(2,1)}, bf16[16,2560]{1,0:T(8,128)(2,1)S(1)}, u32[]{:S(2)}, u32[]{:S(2)}) collective-permute-start(bf16[16,2560]{1,0:T(8,128)(2,1)} %refs_0_.1), channel_id=1, source_target_pairs={{0,1},{1,0},{2,3},{3,2},{4,5},{5,4},{6,7},{7,6},{8,9},{9,8},{10,11... | collective-permute-start | bytes 245768 | tf_op jit(solution)/shard_map/ppermute | solution.py:299
  6.6 0.6 copy-start
  10.3 5.5 %collective-permute-start.2 = (bf16[16,2560]{1,0:T(8,128)(2,1)}, bf16[16,2560]{1,0:T(8,128)(2,1)S(1)}, u32[]{:S(2)}, u32[]{:S(2)}) collective-permute-start(bf16[16,2560]{1,0:T(8,128)(2,1)} %get-tuple-element.24), channel_id=1, source_target_pairs={{0,2},{2,0},{4,6},{6,4},{8,10},{10,8},{12,14},{14,12},{1,3},{3,1},... | collective-permute-start | bytes 245768 | tf_op jit(solution)/shard_map/ppermute | solution.py:296
  11.7 4.2 %collective-permute-start.9 = (bf16[16,2560]{1,0:T(8,128)(2,1)}, bf16[16,2560]{1,0:T(8,128)(2,1)S(1)}, u32[]{:S(2)}, u32[]{:S(2)}) collective-permute-start(bf16[16,2560]{1,0:T(8,128)(2,1)} %get-tuple-element.24), channel_id=1, source_target_pairs={{0,1},{1,0},{2,3},{3,2},{4,5},{5,4},{6,7},{7,6},{8,9},{9,8},{10,11... | collective-permute-start | bytes 245768 | tf_op jit(solution)/shard_map/ppermute | solution.py:299
  11.7 5.9 %collective-permute-start.4 = (bf16[16,2560]{1,0:T(8,128)(2,1)S(1)}, bf16[16,2560]{1,0:T(8,128)(2,1)S(1)}, u32[]{:S(2)}, u32[]{:S(2)}) collective-permute-start(bf16[16,2560]{1,0:T(8,128)(2,1)S(1)} %collective-permute-done.3.refs_4_), channel_id=1, source_target_pairs={{0,2},{2,0},{4,6},{6,4},{8,10},{10,8},{12,14},{14,12},{1,3},{3,1},... | collective-permute-start | bytes 245768 | tf_op jit(solution)/shard_map/ppermute | solution.py:296
  13.2 5.7 %collective-permute-start.6 = (bf16[16,2560]{1,0:T(8,128)(2,1)S(1)}, bf16[16,2560]{1,0:T(8,128)(2,1)S(1)}, u32[]{:S(2)}, u32[]{:S(2)}) collective-permute-start(bf16[16,2560]{1,0:T(8,128)(2,1)S(1)} %collective-permute-done.5.refs_6_), channel_id=1, source_target_pairs={{0,2},{2,0},{4,6},{6,4},{8,10},{10,8},{12,14},{14,12},{1,3},{3,1},... | collective-permute-start | bytes 245768 | tf_op jit(solution)/shard_map/ppermute | solution.py:296
  13.7 5.2 %collective-permute-start.11 = (bf16[16,2560]{1,0:T(8,128)(2,1)S(1)}, bf16[16,2560]{1,0:T(8,128)(2,1)S(1)}, u32[]{:S(2)}, u32[]{:S(2)}) collective-permute-start(bf16[16,2560]{1,0:T(8,128)(2,1)S(1)} %collective-permute-done.3.refs_4_), channel_id=1, source_target_pairs={{0,1},{1,0},{2,3},{3,2},{4,5},{5,4},{6,7},{7,6},{8,9},{9,8},{10,11... | collective-permute-start | bytes 245768 | tf_op jit(solution)/shard_map/ppermute | solution.py:299
  15.8 8.6 %collective-permute-start.13 = (bf16[16,2560]{1,0:T(8,128)(2,1)S(1)}, bf16[16,2560]{1,0:T(8,128)(2,1)S(1)}, u32[]{:S(2)}, u32[]{:S(2)}) collective-permute-start(bf16[16,2560]{1,0:T(8,128)(2,1)S(1)} %collective-permute-done.5.refs_6_), channel_id=1, source_target_pairs={{0,1},{1,0},{2,3},{3,2},{4,5},{5,4},{6,7},{7,6},{8,9},{9,8},{10,11... | collective-permute-start | bytes 245768 | tf_op jit(solution)/shard_map/ppermute | solution.py:299
  15.9 8.6 %collective-permute-start.8 = (bf16[16,2560]{1,0:T(8,128)(2,1)S(1)}, bf16[16,2560]{1,0:T(8,128)(2,1)S(1)}, u32[]{:S(2)}, u32[]{:S(2)}) collective-permute-start(bf16[16,2560]{1,0:T(8,128)(2,1)S(1)} %collective-permute-done.1.refs_1_), channel_id=1, source_target_pairs={{0,1},{1,0},{2,3},{3,2},{4,5},{5,4},{6,7},{7,6},{8,9},{9,8},{10,11... | collective-permute-start | bytes 245768 | tf_op jit(solution)/shard_map/ppermute | solution.py:299
  17.6 6.9 %collective-permute-start.10 = (bf16[16,2560]{1,0:T(8,128)(2,1)S(1)}, bf16[16,2560]{1,0:T(8,128)(2,1)S(1)}, u32[]{:S(2)}, u32[]{:S(2)}) collective-permute-start(bf16[16,2560]{1,0:T(8,128)(2,1)S(1)} %collective-permute-done.2.refs_3_), channel_id=1, source_target_pairs={{0,1},{1,0},{2,3},{3,2},{4,5},{5,4},{6,7},{7,6},{8,9},{9,8},{10,11... | collective-permute-start | bytes 245768 | tf_op jit(solution)/shard_map/ppermute | solution.py:299
  19.0 5.5 %collective-permute-start.12 = (bf16[16,2560]{1,0:T(8,128)(2,1)S(1)}, bf16[16,2560]{1,0:T(8,128)(2,1)S(1)}, u32[]{:S(2)}, u32[]{:S(2)}) collective-permute-start(bf16[16,2560]{1,0:T(8,128)(2,1)S(1)} %collective-permute-done.4.refs_5_), channel_id=1, source_target_pairs={{0,1},{1,0},{2,3},{3,2},{4,5},{5,4},{6,7},{7,6},{8,9},{9,8},{10,11... | collective-permute-start | bytes 245768 | tf_op jit(solution)/shard_map/ppermute | solution.py:299
  19.0 5.5 %collective-permute-start.14 = (bf16[16,2560]{1,0:T(8,128)(2,1)S(1)}, bf16[16,2560]{1,0:T(8,128)(2,1)S(1)}, u32[]{:S(2)}, u32[]{:S(2)}) collective-permute-start(bf16[16,2560]{1,0:T(8,128)(2,1)S(1)} %collective-permute-done.6.refs_7_), channel_id=1, source_target_pairs={{0,1},{1,0},{2,3},{3,2},{4,5},{5,4},{6,7},{7,6},{8,9},{9,8},{10,11... | collective-permute-start | bytes 245768 | tf_op jit(solution)/shard_map/ppermute | solution.py:299
  19.5 25.3 %all-to-all-start = ((bf16[8,384,128]{2,1,0:T(8,128)(2,1)}), bf16[8,384,128]{2,1,0:T(8,128)(2,1)S(1)}, u32[]{:S(2)}, u32[]{:S(2)}) async-start(bf16[8,384,128]{2,1,0:T(8,128)(2,1)} %get-tuple-element.23), calls=%async_computation | async-start | bytes 1572864 | tf_op jit(solution)/shard_map/all_to_all | solution.py:325
  24.5 0.9 %copy-start.1 = (bf16[16,2560]{1,0:T(8,128)(2,1)S(1)}, bf16[16,2560]{1,0:T(8,128)(2,1)}, u32[]{:S(2)}) copy-start(bf16[16,2560]{1,0:T(8,128)(2,1)} %copy-done) | copy-start | bytes 245764
  25.4 6.3 %slice-start = ((s8[8847360]{0:T(1024)(128)(4,1)}), s8[4194304]{0:T(1024)(128)(4,1)S(1)}, s32[]{:S(2)}) async-start(s8[8847360]{0:T(1024)(128)(4,1)} %bitcast.12), calls=%async_computation.1 | async-start | bytes 8388608
  25.5 6.2 %slice-start.1 = ((s8[8847360]{0:T(1024)(128)(4,1)}), s8[4194304]{0:T(1024)(128)(4,1)S(1)}, s32[]{:S(2)}) async-start(s8[8847360]{0:T(1024)(128)(4,1)} %bitcast.12), calls=%async_computation.2 | async-start | bytes 8388608
  25.5 6.2 %slice-start.2 = ((s8[8847360]{0:T(1024)(128)(4,1)}), s8[458752]{0:T(1024)(128)(4,1)S(1)}, s32[]{:S(2)}) async-start(s8[8847360]{0:T(1024)(128)(4,1)} %bitcast.12), calls=%async_computation.3 | async-start | bytes 917504
  25.6 8.6 %slice-start.3 = ((s8[8847360]{0:T(1024)(128)(4,1)}), s8[4194304]{0:T(1024)(128)(4,1)S(1)}, s32[]{:S(2)}) async-start(s8[8847360]{0:T(1024)(128)(4,1)} %bitcast.14), calls=%async_computation.4 | async-start | bytes 8388608
  25.6 8.6 %slice-start.4 = ((s8[8847360]{0:T(1024)(128)(4,1)}), s8[4194304]{0:T(1024)(128)(4,1)S(1)}, s32[]{:S(2)}) async-start(s8[8847360]{0:T(1024)(128)(4,1)} %bitcast.14), calls=%async_computation.5 | async-start | bytes 8388608
  31.7 2.5 %slice-start.5 = ((s8[8847360]{0:T(1024)(128)(4,1)}), s8[458752]{0:T(1024)(128)(4,1)S(1)}, s32[]{:S(2)}) async-start(s8[8847360]{0:T(1024)(128)(4,1)} %bitcast.14), calls=%async_computation.6 | async-start | bytes 917504
  34.2 1.6 %copy-start.2 = (bf16[2,64,864]{2,1,0:T(8,128)(2,1)S(1)}, bf16[2,64,864]{2,1,0:T(8,128)(2,1)}, u32[]{:S(2)}) copy-start(bf16[2,64,864]{2,1,0:T(8,128)(2,1)} %get-tuple-element.25.in_blocks) | copy-start | bytes 663556
  34.2 1.6 %copy-start.4 = (s32[7]{0:T(128)S(1)}, s32[7]{0:T(128)}, u32[]{:S(2)}) copy-start(s32[7]{0:T(128)} %get-tuple-element.21.facts) | copy-start | bytes 88
  37.8 2.2 %collective-permute-start.15 = (bf16[2624,128]{1,0:T(8,128)(2,1)S(1)}, bf16[2624,128]{1,0:T(8,128)(2,1)S(1)}, u32[]{:S(2)}, u32[]{:S(2)}) collective-permute-start(bf16[2624,128]{1,0:T(8,128)(2,1)S(1)} %get-tuple-element.27), channel_id=1, source_target_pairs={{0,1},{1,0},{2,3},{3,2},{4,5},{5,4},{6,7},{7,6},{8,9},{9,8},{10,11... | collective-permute-start | bytes 2015240 | tf_op jit(solution)/shard_map/ppermute | solution.py:299
  44.8 23.1 %collective-permute-start.16 = (bf16[8,384,128]{2,1,0:T(8,128)(2,1)S(1)}, bf16[8,384,128]{2,1,0:T(8,128)(2,1)S(1)}, u32[]{:S(2)}, u32[]{:S(2)}) collective-permute-start(bf16[8,384,128]{2,1,0:T(8,128)(2,1)S(1)} %shard_map.125.gathered), channel_id=1, source_target_pairs={{0,1},{1,0},{2,3},{3,2},{4,5},{5,4},{6,7},{7,6},{8,9},{9,8},{10,11... | collective-permute-start | bytes 2359304 | tf_op jit(solution)/shard_map/ppermute | solution.py:299
  44.8 10.0 %collective-permute-start.18 = (bf16[864,128]{1,0:T(8,128)(2,1)S(1)}, bf16[864,128]{1,0:T(8,128)(2,1)S(1)}, u32[]{:S(2)}, u32[]{:S(2)}) collective-permute-start(bf16[864,128]{1,0:T(8,128)(2,1)S(1)} %multiply_convert_fusion.hidden.source), channel_id=1, source_target_pairs={{0,4},{2,6},{4,0},{6,2},{8,12},{10,14},{12,8},{14,10},{1,5},{3,7},... | collective-permute-start | bytes 663560 | tf_op jit(solution)/shard_map/ppermute | solution.py:296
  45.1 22.3 %collective-permute-start.17 = (bf16[1344,128]{1,0:T(8,128)(2,1)S(1)}, bf16[1344,128]{1,0:T(8,128)(2,1)S(1)}, u32[]{:S(2)}, u32[]{:S(2)}) collective-permute-start(bf16[1344,128]{1,0:T(8,128)(2,1)S(1)} %get-tuple-element.30), channel_id=1, source_target_pairs={{0,2},{2,0},{4,6},{6,4},{8,10},{10,8},{12,14},{14,12},{1,3},{3,1},... | collective-permute-start | bytes 1032200 | tf_op jit(solution)/shard_map/ppermute | solution.py:296
  46.3 13.2 %collective-permute-start.22 = (bf16[864,128]{1,0:T(8,128)(2,1)S(1)}, bf16[864,128]{1,0:T(8,128)(2,1)S(1)}, u32[]{:S(2)}, u32[]{:S(2)}) collective-permute-start(bf16[864,128]{1,0:T(8,128)(2,1)S(1)} %multiply_convert_fusion.hidden.source), channel_id=1, source_target_pairs={{0,8},{2,10},{4,12},{6,14},{8,0},{10,2},{12,4},{14,6},{1,9},{3,11}... | collective-permute-start | bytes 663560 | tf_op jit(solution)/shard_map/ppermute | solution.py:296
  54.8 8.8 %collective-permute-start.31 = (bf16[864,128]{1,0:T(8,128)(2,1)S(1)}, bf16[864,128]{1,0:T(8,128)(2,1)S(1)}, u32[]{:S(2)}, u32[]{:S(2)}) collective-permute-start(bf16[864,128]{1,0:T(8,128)(2,1)S(1)} %shard_map.129.refs_0_), channel_id=1, source_target_pairs={{0,2},{2,0},{4,6},{6,4},{8,10},{10,8},{12,14},{14,12},{1,3},{3,1},... | collective-permute-start | bytes 663560 | tf_op jit(solution)/shard_map/ppermute | solution.py:296
  57.3 10.1 %collective-permute-start.34 = (bf16[864,128]{1,0:T(8,128)(2,1)S(1)}, bf16[864,128]{1,0:T(8,128)(2,1)S(1)}, u32[]{:S(2)}, u32[]{:S(2)}) collective-permute-start(bf16[864,128]{1,0:T(8,128)(2,1)S(1)} %collective-permute-done.18.refs_0_.refs_1_.refs_2_._.refs_4_), channel_id=1, source_target_pairs={{0,2},{2,0},{4,6},{6,4},{8,10},{10,8},{12,14},{14,12},{1,3},{3,1},... | collective-permute-start | bytes 663560 | tf_op jit(solution)/shard_map/ppermute | solution.py:296
  59.5 9.8 %collective-permute-start.26 = (bf16[864,128]{1,0:T(8,128)(2,1)S(1)}, bf16[864,128]{1,0:T(8,128)(2,1)S(1)}, u32[]{:S(2)}, u32[]{:S(2)}) collective-permute-start(bf16[864,128]{1,0:T(8,128)(2,1)S(1)} %multiply_convert_fusion.hidden.source), channel_id=1, source_target_pairs={{0,12},{2,14},{4,8},{6,10},{8,4},{10,6},{12,0},{14,2},{1,13},{3,15... | collective-permute-start | bytes 663560 | tf_op jit(solution)/shard_map/ppermute | solution.py:296
  63.6 7.5 %collective-permute-start.30 = (bf16[864,128]{1,0:T(8,128)(2,1)S(1)}, bf16[864,128]{1,0:T(8,128)(2,1)S(1)}, u32[]{:S(2)}, u32[]{:S(2)}) collective-permute-start(bf16[864,128]{1,0:T(8,128)(2,1)S(1)} %shard_map.129.refs_0_), channel_id=1, source_target_pairs={{0,1},{1,0},{2,3},{3,2},{4,5},{5,4},{6,7},{7,6},{8,9},{9,8},{10,11... | collective-permute-start | bytes 663560 | tf_op jit(solution)/shard_map/ppermute | solution.py:299
  67.4 4.0 %collective-permute-start.33 = (bf16[864,128]{1,0:T(8,128)(2,1)S(1)}, bf16[864,128]{1,0:T(8,128)(2,1)S(1)}, u32[]{:S(2)}, u32[]{:S(2)}) collective-permute-start(bf16[864,128]{1,0:T(8,128)(2,1)S(1)} %collective-permute-done.18.refs_0_.refs_1_.refs_2_._.refs_4_), channel_id=1, source_target_pairs={{0,1},{1,0},{2,3},{3,2},{4,5},{5,4},{6,7},{7,6},{8,9},{9,8},{10,11... | collective-permute-start | bytes 663560 | tf_op jit(solution)/shard_map/ppermute | solution.py:299
  67.4 4.1 %collective-permute-start.32 = (bf16[864,128]{1,0:T(8,128)(2,1)S(1)}, bf16[864,128]{1,0:T(8,128)(2,1)S(1)}, u32[]{:S(2)}, u32[]{:S(2)}) collective-permute-start(bf16[864,128]{1,0:T(8,128)(2,1)S(1)} %collective-permute-done.31.refs_2_), channel_id=1, source_target_pairs={{0,1},{1,0},{2,3},{3,2},{4,5},{5,4},{6,7},{7,6},{8,9},{9,8},{10,11... | collective-permute-start | bytes 663560 | tf_op jit(solution)/shard_map/ppermute | solution.py:299
  67.9 6.4 %collective-permute-start.35 = (bf16[864,128]{1,0:T(8,128)(2,1)S(1)}, bf16[864,128]{1,0:T(8,128)(2,1)S(1)}, u32[]{:S(2)}, u32[]{:S(2)}) collective-permute-start(bf16[864,128]{1,0:T(8,128)(2,1)S(1)} %collective-permute-done.34.refs_6_), channel_id=1, source_target_pairs={{0,1},{1,0},{2,3},{3,2},{4,5},{5,4},{6,7},{7,6},{8,9},{9,8},{10,11... | collective-permute-start | bytes 663560 | tf_op jit(solution)/shard_map/ppermute | solution.py:299
  69.3 8.6 %collective-permute-start.24 = (bf16[864,128]{1,0:T(8,128)(2,1)S(1)}, bf16[864,128]{1,0:T(8,128)(2,1)S(1)}, u32[]{:S(2)}, u32[]{:S(2)}) collective-permute-start(bf16[864,128]{1,0:T(8,128)(2,1)S(1)} %collective-permute-done.22.refs_0_), channel_id=1, source_target_pairs={{0,2},{2,0},{4,6},{6,4},{8,10},{10,8},{12,14},{14,12},{1,3},{3,1},... | collective-permute-start | bytes 663560 | tf_op jit(solution)/shard_map/ppermute | solution.py:296
  71.1 10.8 %collective-permute-start.28 = (bf16[864,128]{1,0:T(8,128)(2,1)S(1)}, bf16[864,128]{1,0:T(8,128)(2,1)S(1)}, u32[]{:S(2)}, u32[]{:S(2)}) collective-permute-start(bf16[864,128]{1,0:T(8,128)(2,1)S(1)} %collective-permute-done.26.refs_4_), channel_id=1, source_target_pairs={{0,2},{2,0},{4,6},{6,4},{8,10},{10,8},{12,14},{14,12},{1,3},{3,1},... | collective-permute-start | bytes 663560 | tf_op jit(solution)/shard_map/ppermute | solution.py:296
  71.4 10.5 %collective-permute-start.19 = (bf16[384,128]{1,0:T(8,128)(2,1)S(1)}, bf16[384,128]{1,0:T(8,128)(2,1)S(1)}, u32[]{:S(2)}, u32[]{:S(2)}) collective-permute-start(bf16[384,128]{1,0:T(8,128)(2,1)S(1)} %get-tuple-element.32), channel_id=1, source_target_pairs={{0,4},{2,6},{4,0},{6,2},{8,12},{10,14},{12,8},{14,10},{1,5},{3,7},... | collective-permute-start | bytes 294920 | tf_op jit(solution)/shard_map/ppermute | solution.py:296
  71.5 10.9 %collective-permute-start.20 = (bf16[384,128]{1,0:T(8,128)(2,1)S(1)}, bf16[384,128]{1,0:T(8,128)(2,1)S(1)}, u32[]{:S(2)}, u32[]{:S(2)}) collective-permute-start(bf16[384,128]{1,0:T(8,128)(2,1)S(1)} %get-tuple-element.33), channel_id=1, source_target_pairs={{0,8},{2,10},{4,12},{6,14},{8,0},{10,2},{12,4},{14,6},{1,9},{3,11}... | collective-permute-start | bytes 294920 | tf_op jit(solution)/shard_map/ppermute | solution.py:296
  74.4 8.1 %collective-permute-start.21 = (bf16[384,128]{1,0:T(8,128)(2,1)S(1)}, bf16[384,128]{1,0:T(8,128)(2,1)S(1)}, u32[]{:S(2)}, u32[]{:S(2)}) collective-permute-start(bf16[384,128]{1,0:T(8,128)(2,1)S(1)} %get-tuple-element.34), channel_id=1, source_target_pairs={{0,12},{2,14},{4,8},{6,10},{8,4},{10,6},{12,0},{14,2},{1,13},{3,15... | collective-permute-start | bytes 294920 | tf_op jit(solution)/shard_map/ppermute | solution.py:296
  75.8 6.7 %copy-start.5 = (bf16[2,64,320]{2,1,0:T(8,128)(2,1)S(1)}, bf16[2,64,320]{2,1,0:T(8,128)(2,1)}, u32[]{:S(2)}) copy-start(bf16[2,64,320]{2,1,0:T(8,128)(2,1)} %get-tuple-element.22.out_blocks) | copy-start | bytes 245764
  77.9 6.6 %collective-permute-start.23 = (bf16[864,128]{1,0:T(8,128)(2,1)S(1)}, bf16[864,128]{1,0:T(8,128)(2,1)S(1)}, u32[]{:S(2)}, u32[]{:S(2)}) collective-permute-start(bf16[864,128]{1,0:T(8,128)(2,1)S(1)} %collective-permute-done.22.refs_0_), channel_id=1, source_target_pairs={{0,1},{1,0},{2,3},{3,2},{4,5},{5,4},{6,7},{7,6},{8,9},{9,8},{10,11... | collective-permute-start | bytes 663560 | tf_op jit(solution)/shard_map/ppermute | solution.py:299
  81.9 2.6 %collective-permute-start.27 = (bf16[864,128]{1,0:T(8,128)(2,1)S(1)}, bf16[864,128]{1,0:T(8,128)(2,1)S(1)}, u32[]{:S(2)}, u32[]{:S(2)}) collective-permute-start(bf16[864,128]{1,0:T(8,128)(2,1)S(1)} %collective-permute-done.26.refs_4_), channel_id=1, source_target_pairs={{0,1},{1,0},{2,3},{3,2},{4,5},{5,4},{6,7},{7,6},{8,9},{9,8},{10,11... | collective-permute-start | bytes 663560 | tf_op jit(solution)/shard_map/ppermute | solution.py:299
  81.9 2.6 %collective-permute-start.25 = (bf16[864,128]{1,0:T(8,128)(2,1)S(1)}, bf16[864,128]{1,0:T(8,128)(2,1)S(1)}, u32[]{:S(2)}, u32[]{:S(2)}) collective-permute-start(bf16[864,128]{1,0:T(8,128)(2,1)S(1)} %collective-permute-done.24.refs_2_), channel_id=1, source_target_pairs={{0,1},{1,0},{2,3},{3,2},{4,5},{5,4},{6,7},{7,6},{8,9},{9,8},{10,11... | collective-permute-start | bytes 663560 | tf_op jit(solution)/shard_map/ppermute | solution.py:299
  82.4 2.1 %collective-permute-start.29 = (bf16[864,128]{1,0:T(8,128)(2,1)S(1)}, bf16[864,128]{1,0:T(8,128)(2,1)S(1)}, u32[]{:S(2)}, u32[]{:S(2)}) collective-permute-start(bf16[864,128]{1,0:T(8,128)(2,1)S(1)} %collective-permute-done.28.refs_6_), channel_id=1, source_target_pairs={{0,1},{1,0},{2,3},{3,2},{4,5},{5,4},{6,7},{7,6},{8,9},{9,8},{10,11... | collective-permute-start | bytes 663560 | tf_op jit(solution)/shard_map/ppermute | solution.py:299
